TPU v7x, 256 devices: a whole 4x4x8 slice. The times are simulated.
256 devices in a mesh: seq: 32 (over z, y), head: 8 (over x, core).
Axes of the slice: x: 4, y: 4, z: 8, core: 2. Of those that a mesh axis runs over, the one named last changes fastest.
Arguments:
- queries: bfloat16 [8192, 4096], P(('seq', 'head')), may hold values from -6 to 6
- new_keys: bfloat16 [8192, 4096], P(('seq', 'head')), may hold values from -6 to 6
- new_values: bfloat16 [8192, 4096], P(('seq', 'head')), may hold values from -6 to 6
- attn_out: bfloat16 [8192, 4096], P(('seq', 'head')), may hold values from -6 to 6
- out_grad: bfloat16 [8192, 4096], P(('seq', 'head')), may hold values from -384 to 384
- logsumexp: float32 [32, 8192], P('head', 'seq'), may hold values from 8 to 10
- ctx_keys: bfloat16 [65536, 4096], P('seq', 'head'), may hold values from -6 to 6
- ctx_values: bfloat16 [65536, 4096], P('seq', 'head'), may hold values from -6 to 6
- selected: int32 [32, 2], replicated, may hold values from 0 to 31, all different within a row; in each aligned block of 32 rows (0 to 31, 32 to 63, ...) at most 3 rows name the same one
Outputs:
- query_grad: bfloat16 [8192, 4096], P('seq', 'head')
- new_key_grad: bfloat16 [8192, 4096], P('seq', 'head')
- new_value_grad: bfloat16 [8192, 4096], P('seq', 'head')
- ctx_key_grad: bfloat16 [65536, 4096], P('seq', 'head')
- ctx_value_grad: bfloat16 [65536, 4096], P('seq', 'head')
Inputs may be any that keep to these rules, and one draw needn't show every extreme that they name: Each row lists 2 different context blocks. Every context block is selected by at least one and at most 3 query blocks, and some block by exactly 3.
All inputs are finite; a program needn't handle non-finite values.
Results may differ from a plain program's by a relative error of at most 0.0058.
Values may be sent and summed in bfloat16 or wider, within the bound.
No kernel may reach another device: no remote copies, remote signals or barrier semaphores. Data moves between devices by JAX's collectives and lax.ppermute only.
A program may use at most 128 MiB of HBM per device.

v0:
```python
import jax
import jax.numpy as jnp
from jax import lax
from jax.sharding import PartitionSpec as P


def split_heads(tensor, head_count):
    row_count, features = tensor.shape
    return tensor.reshape(row_count, head_count, features // head_count).transpose(1, 0, 2)


def merge_heads(tensor):
    head_count, row_count, head_size = tensor.shape
    return tensor.transpose(1, 0, 2).reshape(row_count, head_count * head_size)


def head_grads(query, key_block, value_block, grad_out, log_norm, out_dot, allowed):
    scaling = query.shape[-1] ** (-0.5)
    scores = jnp.dot(query, key_block.T, preferred_element_type=jnp.float32) * scaling
    weights = jnp.exp(scores - log_norm[:, None])
    if allowed is not None:
        weights = jnp.where(allowed, weights, 0.0)
    rounded = weights.astype(jnp.bfloat16)
    value_part = jnp.dot(rounded.T, grad_out, preferred_element_type=jnp.float32)
    dweights = jnp.dot(grad_out, value_block.T, preferred_element_type=jnp.float32)
    dscores = (weights * (dweights - out_dot[:, None])).astype(jnp.bfloat16)
    query_part = jnp.dot(dscores, key_block, preferred_element_type=jnp.float32) * scaling
    key_part = jnp.dot(dscores.T, query, preferred_element_type=jnp.float32) * scaling
    return (query_part, key_part, value_part)


def per_device(
    queries, new_keys, new_values, attn_out, out_grad, logsumexp, ctx_keys, ctx_values, selected
):
    head_count = logsumexp.shape[0]
    query_rows = logsumexp.shape[1]
    owners = lax.axis_size("seq")
    key_rows = ctx_keys.shape[0]
    features = ctx_keys.shape[1]
    piece_rows = key_rows // owners
    chosen = selected.shape[1]
    local = (
        lax.all_to_all(queries, "head", split_axis=1, concat_axis=0, tiled=True),
        lax.all_to_all(new_keys, "head", split_axis=1, concat_axis=0, tiled=True),
        lax.all_to_all(new_values, "head", split_axis=1, concat_axis=0, tiled=True),
        lax.all_to_all(attn_out, "head", split_axis=1, concat_axis=0, tiled=True),
        lax.all_to_all(out_grad, "head", split_axis=1, concat_axis=0, tiled=True),
    )
    query_heads, keys_heads, values_heads, output_heads, grad_heads = [
        split_heads(tensor, head_count) for tensor in local
    ]
    out_dot = jnp.sum(grad_heads.astype(jnp.float32) * output_heads.astype(jnp.float32), axis=-1)
    causal = jnp.arange(query_rows)[:, None] >= jnp.arange(query_rows)[None, :]

    def own_head(operands):
        query, key_block, value_block, grad_out, log_norm, dots = operands
        return head_grads(query, key_block, value_block, grad_out, log_norm, dots, causal)

    own_dq, own_dk, own_dv = lax.map(
        own_head, (query_heads, keys_heads, values_heads, grad_heads, logsumexp, out_dot)
    )
    stacked = jnp.stack([ctx_keys, ctx_values]).reshape(2, owners, piece_rows, features)
    relay = lax.all_to_all(stacked, "seq", split_axis=1, concat_axis=1, tiled=True)
    outgoing = jnp.take(relay, selected.T, axis=1)

    def per_block(block_pair):
        keys_b = split_heads(block_pair[0], head_count)
        values_b = split_heads(block_pair[1], head_count)

        def one_head(operands):
            query, key_block, value_block, grad_out, log_norm, dots = operands
            return head_grads(query, key_block, value_block, grad_out, log_norm, dots, None)

        part_q, part_k, part_v = lax.map(
            one_head, (query_heads, keys_b, values_b, grad_heads, logsumexp, out_dot)
        )
        partials = jnp.stack([merge_heads(part_k), merge_heads(part_v)]).astype(jnp.bfloat16)
        return (merge_heads(part_q), partials)

    blocks = lax.all_to_all(outgoing, "seq", split_axis=2, concat_axis=2, tiled=True)
    items = blocks.shape[1]
    block_pairs = jnp.moveaxis(blocks.reshape(2, items, key_rows, features), 1, 0)
    query_parts, partials = lax.map(per_block, block_pairs)
    partials, query_parts = (partials, query_parts)
    query_grad = (merge_heads(own_dq) + jnp.sum(query_parts, axis=0)).astype(jnp.bfloat16)
    backward = partials.reshape(chosen, 2, owners, piece_rows, features)
    returned = lax.all_to_all(backward, "seq", split_axis=2, concat_axis=2, tiled=True)
    owner_of = selected.T
    onehot = (owner_of[None, :, :] == jnp.arange(owners)[:, None, None]).astype(jnp.bfloat16)
    summed = jnp.einsum(
        "osr,sgrpw->gopw", onehot, returned, preferred_element_type=jnp.float32
    ).astype(jnp.bfloat16)
    arrived = lax.all_to_all(summed, "seq", split_axis=1, concat_axis=1, tiled=True)
    context_grads = arrived.reshape(2, key_rows, features)
    new_key_grad = merge_heads(own_dk).astype(jnp.bfloat16)
    new_value_grad = merge_heads(own_dv).astype(jnp.bfloat16)
    return (query_grad, new_key_grad, new_value_grad, context_grads[0], context_grads[1])


def solution(mesh):
    in_specs = (
        P(("seq", "head"), None),
        P(("seq", "head"), None),
        P(("seq", "head"), None),
        P(("seq", "head"), None),
        P(("seq", "head"), None),
        P("head", "seq"),
        P("seq", "head"),
        P("seq", "head"),
        P(),
    )
    out_specs = (
        P("seq", "head"),
        P("seq", "head"),
        P("seq", "head"),
        P("seq", "head"),
        P("seq", "head"),
    )
    return jax.shard_map(
        per_device, mesh=mesh, in_specs=in_specs, out_specs=out_specs, check_vma=False
    )
```

profile of v0, /device:TPU:32, one launch (start us, length us, event | category | flops | bytes accessed | tf_op | source)
XLA Modules:
  0.0 813.6 jit_solution(1611955550363419624)
XLA Ops:
  6.6 4.6 pad_maximum_fusion
  14.1 11.4 %all-to-all-start.5 = ((bf16[2,32,64,512]{3,2,0,1:T(8,128)(2,1)}), bf16[2,32,64,512]{3,2,0,1:T(8,128)(2,1)}, u32[]{:S(2)}, u32[]{:S(2)}) async-start(bf16[2,32,64,512]{3,2,0,1:T(8,128)(2,1)} %pad_maximum_fusion), calls=%async_computation.5 | async-start | bytes 8388608 | tf_op jit(solution)/shard_map/all_to_all | solution.py:63
  26.4 93.5 %all-to-all-done.5 = bf16[2,32,64,512]{3,2,0,1:T(8,128)(2,1)} async-done(((bf16[2,32,64,512]{3,2,0,1:T(8,128)(2,1)}), bf16[2,32,64,512]{3,2,0,1:T(8,128)(2,1)}, u32[]{:S(2)}, u32[]{:S(2)}) %all-to-all-start.5) | async-done | bytes 4194336 | tf_op jit(solution)/shard_map/all_to_all | solution.py:63
  124.1 7.8 gather_fusion
  131.8 4.7 all-to-all-start.4
  136.6 7.5 select_bitcast_fusion
  144.1 7.8 copy.82
  151.8 6.6 all-to-all-start.6
  160.1 188.9 %all-to-all-done.6 = bf16[2,2,32,64,512]{4,3,0,1,2:T(8,128)(2,1)} async-done(((bf16[2,2,32,64,512]{4,3,0,1,2:T(8,128)(2,1)}), bf16[2,2,32,64,512]{4,3,0,1,2:T(8,128)(2,1)}, u32[]{:S(2)}, u32[]{:S(2)}) %all-to-all-start.6) | async-done | bytes 8388640 | tf_op jit(solution)/shard_map/all_to_all | solution.py:80
  353.2 7.8 copy.83
  361.0 104.2 %while.42 = (s32[]{:T(128)}, f32[2,256,512]{2,1,0:T(8,128)}, bf16[2,2,2048,512]{3,2,1,0:T(8,128)(2,1)}, bf16[2,2,2048,512]{3,2,0,1:T(8,128)(2,1)}, bf16[4,256,12...) while((s32[]{:T(128)}, f32[2,256,512]{2,1,0:T(8,128)}, ...), condition=%wide.region_6.7_spmd, body=%wide.region_3.6_spmd.sunk | while | flops 682917888 | bytes 100544032 | solution.py:83
  361.0 4.5 constant_dynamic-slice_fusion.9
  372.4 22.6 %while.44 = (s32[]{:T(128)}, f32[4,256,128]{2,1,0:T(8,128)S(1)}, bf16[4,2048,128]{2,1,0:T(8,128)(2,1)}, bf16[4,2048,128]{2,1,0:T(8,128)(2,1)}, bf16[4,256,128]{2...) while((s32[]{:T(128)}, f32[4,256,128]{2,1,0:T(8,128)S(1)}, ...), condition=%wide.region_5.5_spmd, body=%wide.region_4.4_spmd.sunk | while | flops 674529280 | bytes 47066344 | solution.py:74
  413.1 4.5 constant_dynamic-slice_fusion.9
  424.6 22.6 %while.44 = (s32[]{:T(128)}, f32[4,256,128]{2,1,0:T(8,128)S(1)}, bf16[4,2048,128]{2,1,0:T(8,128)(2,1)}, bf16[4,2048,128]{2,1,0:T(8,128)(2,1)}, bf16[4,256,128]{2...) while((s32[]{:T(128)}, f32[4,256,128]{2,1,0:T(8,128)S(1)}, ...), condition=%wide.region_5.5_spmd, body=%wide.region_4.4_spmd.sunk | while | flops 674529280 | bytes 47066344 | solution.py:74
  465.2 16.4 %copy.90 = bf16[2,2,32,64,512]{4,0,3,1,2:T(2,128)(2,1)} copy(bf16[2,2,32,64,512]{4,3,2,1,0:T(8,128)(2,1)} %bitcast.247) | data formatting | bytes 16777216 | tf_op jit(solution)/shard_map/reshape | solution.py:86
  481.7 13.0 %all-to-all-start.7 = ((bf16[2,2,32,64,512]{4,0,3,1,2:T(2,128)(2,1)}), bf16[2,2,32,64,512]{4,0,3,1,2:T(2,128)(2,1)}, u32[]{:S(2)}, u32[]{:S(2)}) async-start(bf16[2,2,32,64,512]{4,0,3,1,2:T(2,128)(2,1)} %copy.90), calls=%async_computation.7 | async-start | bytes 16777216 | tf_op jit(solution)/shard_map/all_to_all | solution.py:87
  495.4 187.7 %all-to-all-done.7 = bf16[2,2,32,64,512]{4,0,3,1,2:T(2,128)(2,1)} async-done(((bf16[2,2,32,64,512]{4,0,3,1,2:T(2,128)(2,1)}), bf16[2,2,32,64,512]{4,0,3,1,2:T(2,128)(2,1)}, u32[]{:S(2)}, u32[]{:S(2)}) %all-to-all-start.7) | async-done | bytes 8388640 | tf_op jit(solution)/shard_map/all_to_all | solution.py:87
  683.1 4.9 all-to-all-start.3
  688.0 9.1 %fusion.63 = bf16[2,32,64,512]{3,1,2,0:T(8,128)(2,1)S(1)} fusion(bf16[2,2,32,64,512]{4,0,3,1,2:T(2,128)(2,1)} %all-to-all-done.7, s32[2,32]{1,0:T(2,128)S(1)} %bitcast.268), kind=kOutput, calls=%fused_computation.86 | convolution fusion | flops 270534656 | bytes 12583168 | tf_op jit(solution)/shard_map/osr,sgrpw->gopw/dot_general | solution.py:90
  701.5 13.5 %all-to-all-start.8 = ((bf16[2,32,64,512]{3,2,0,1:T(8,128)(2,1)}), bf16[2,32,64,512]{3,2,0,1:T(8,128)(2,1)}, u32[]{:S(2)}, u32[]{:S(2)}) async-start(bf16[2,32,64,512]{3,2,0,1:T(8,128)(2,1)} %copy.92), calls=%async_computation.8 | async-start | bytes 8388608 | tf_op jit(solution)/shard_map/all_to_all | solution.py:93
  716.2 4.5 while.43
  722.4 86.4 %all-to-all-done.8 = bf16[2,32,64,512]{3,2,0,1:T(8,128)(2,1)} async-done(((bf16[2,32,64,512]{3,2,0,1:T(8,128)(2,1)}), bf16[2,32,64,512]{3,2,0,1:T(8,128)(2,1)}, u32[]{:S(2)}, u32[]{:S(2)}) %all-to-all-start.8) | async-done | bytes 4194336 | tf_op jit(solution)/shard_map/all_to_all | solution.py:93
  808.8 4.7 fusion.71
  (224 shorter events, 126.6 us)
Async XLA Ops:
  2.3 11.8 %all-to-all-start = ((bf16[32,8,512]{2,0,1:T(8,128)(2,1)}), bf16[32,8,512]{2,0,1:T(8,128)(2,1)S(1)}, u32[]{:S(2)}, u32[]{:S(2)}) async-start(bf16[32,8,512]{2,0,1:T(8,128)(2,1)} %bitcast.173), calls=%async_computation | async-start | bytes 524288 | tf_op jit(solution)/shard_map/all_to_all | solution.py:43
  11.2 14.4 %copy-start.12 = (s32[32,2]{0,1:T(2,128)S(1)}, s32[32,2]{0,1:T(2,128)}, u32[]{:S(2)}) copy-start(s32[32,2]{0,1:T(2,128)} %param.23) | copy-start | bytes 772
  11.2 14.5 %copy-start.7 = (bf16[32,4096]{1,0:T(8,128)(2,1)S(1)}, bf16[32,4096]{1,0:T(8,128)(2,1)}, u32[]{:S(2)}) copy-start(bf16[32,4096]{1,0:T(8,128)(2,1)} %param.19) | copy-start | bytes 786436
  11.2 112.1 %copy-start.8 = (bf16[32,4096]{1,0:T(8,128)(2,1)S(1)}, bf16[32,4096]{1,0:T(8,128)(2,1)}, u32[]{:S(2)}) copy-start(bf16[32,4096]{1,0:T(8,128)(2,1)} %param.18) | copy-start | bytes 786436
  14.1 105.7 %all-to-all-start.5 = ((bf16[2,32,64,512]{3,2,0,1:T(8,128)(2,1)}), bf16[2,32,64,512]{3,2,0,1:T(8,128)(2,1)}, u32[]{:S(2)}, u32[]{:S(2)}) async-start(bf16[2,32,64,512]{3,2,0,1:T(8,128)(2,1)} %pad_maximum_fusion), calls=%async_computation.5 | async-start | bytes 8388608 | tf_op jit(solution)/shard_map/all_to_all | solution.py:63
  119.9 12.0 %all-to-all-start.2 = ((bf16[32,8,512]{2,0,1:T(8,128)(2,1)}), bf16[32,8,512]{2,0,1:T(8,128)(2,1)S(1)}, u32[]{:S(2)}, u32[]{:S(2)}) async-start(bf16[32,8,512]{2,0,1:T(8,128)(2,1)} %bitcast.171), calls=%async_computation.2 | async-start | bytes 524288 | tf_op jit(solution)/shard_map/all_to_all | solution.py:47
  131.8 20.0 %all-to-all-start.4 = ((bf16[32,8,512]{2,0,1:T(8,128)(2,1)}), bf16[32,8,512]{2,0,1:T(8,128)(2,1)S(1)}, u32[]{:S(2)}, u32[]{:S(2)}) async-start(bf16[32,8,512]{2,0,1:T(8,128)(2,1)} %bitcast.169), calls=%async_computation.4 | async-start | bytes 524288 | tf_op jit(solution)/shard_map/all_to_all | solution.py:46
  151.8 6.6 copy-start.9
  151.8 197.1 %all-to-all-start.6 = ((bf16[2,2,32,64,512]{4,3,0,1,2:T(8,128)(2,1)}), bf16[2,2,32,64,512]{4,3,0,1,2:T(8,128)(2,1)}, u32[]{:S(2)}, u32[]{:S(2)}) async-start(bf16[2,2,32,64,512]{4,3,0,1,2:T(8,128)(2,1)} %copy.82), calls=%async_computation.6 | async-start | bytes 16777216 | tf_op jit(solution)/shard_map/all_to_all | solution.py:80
  349.0 132.7 %all-to-all-start.1 = ((bf16[32,8,512]{2,0,1:T(8,128)(2,1)}), bf16[32,8,512]{2,0,1:T(8,128)(2,1)}, u32[]{:S(2)}, u32[]{:S(2)}) async-start(bf16[32,8,512]{2,0,1:T(8,128)(2,1)} %bitcast.172), calls=%async_computation.1 | async-start | bytes 524288 | tf_op jit(solution)/shard_map/all_to_all | solution.py:44
  353.2 7.8 copy-start.11
  372.9 2.1 copy-start
  378.6 2.1 copy-start
  384.2 2.1 copy-start
  389.9 2.1 copy-start
  425.0 2.1 copy-start
  430.7 2.1 copy-start
  442.0 2.1 copy-start
  481.6 13.0 %copy-start.10 = (bf16[32,4096]{1,0:T(8,128)(2,1)S(1)}, bf16[32,4096]{1,0:T(8,128)(2,1)}, u32[]{:S(2)}) copy-start(bf16[32,4096]{1,0:T(8,128)(2,1)} %param.17) | copy-start | bytes 786436
  481.6 206.3 %copy-start.13 = (s32[32,2]{0,1:T(2,128)S(1)}, s32[32,2]{0,1:T(2,128)}, u32[]{:S(2)}) copy-start(s32[32,2]{0,1:T(2,128)} %param.23) | copy-start | bytes 772
  481.7 201.4 %all-to-all-start.7 = ((bf16[2,2,32,64,512]{4,0,3,1,2:T(2,128)(2,1)}), bf16[2,2,32,64,512]{4,0,3,1,2:T(2,128)(2,1)}, u32[]{:S(2)}, u32[]{:S(2)}) async-start(bf16[2,2,32,64,512]{4,0,3,1,2:T(2,128)(2,1)} %copy.90), calls=%async_computation.7 | async-start | bytes 16777216 | tf_op jit(solution)/shard_map/all_to_all | solution.py:87
  683.1 18.4 %all-to-all-start.3 = ((bf16[32,8,512]{2,0,1:T(8,128)(2,1)}), bf16[32,8,512]{2,0,1:T(8,128)(2,1)S(1)}, u32[]{:S(2)}, u32[]{:S(2)}) async-start(bf16[32,8,512]{2,0,1:T(8,128)(2,1)} %bitcast.170), calls=%async_computation.3 | async-start | bytes 524288 | tf_op jit(solution)/shard_map/all_to_all | solution.py:45
  701.5 107.4 %all-to-all-start.8 = ((bf16[2,32,64,512]{3,2,0,1:T(8,128)(2,1)}), bf16[2,32,64,512]{3,2,0,1:T(8,128)(2,1)}, u32[]{:S(2)}, u32[]{:S(2)}) async-start(bf16[2,32,64,512]{3,2,0,1:T(8,128)(2,1)} %copy.92), calls=%async_computation.8 | async-start | bytes 8388608 | tf_op jit(solution)/shard_map/all_to_all | solution.py:93
  716.2 5.4 copy-start.6
  (29 other events, 40.7 us)
where the time goes:
time: 820 us; the launch traced here: 814 us
  waiting for transfers between devices  559 us (68%)
  local copies, waits for them, and re-layouts  121 us (15%)
  starting transfers between devices  66.1 us (8%)
  matrix products  43.2 us (5%)
  other arithmetic  22.3 us (3%)
    all_to_all x1, waiting for transfers between devices, per_device(): lax.all_to_all(outgoing, 'seq', split_axis=2, concat_axis=2, tiled=True)  189 us
    all_to_all x1, waiting for transfers between devices, per_device(): lax.all_to_all(backward, 'seq', split_axis=2, concat_axis=2, tiled=True)  188 us
    all_to_all x1, waiting for transfers between devices, per_device(): lax.all_to_all(stacked, 'seq', split_axis=1, concat_axis=1, tiled=True)  93.5 us
    all_to_all x1, waiting for transfers between devices, per_device(): lax.all_to_all(summed, 'seq', split_axis=1, concat_axis=1, tiled=True)  86.4 us
    while x76, local copies, waits for them, and re-layouts  32.1 us
    reshape x1, local copies, waits for them, and re-layouts, per_device(): backward = partials.reshape(chosen, 2, owners, piece_rows, features)  16.4 us
  transfers between devices with their start and end apart: 9, of which 5 were waited for; matrix products, arithmetic and copies ran while one was open for 20% of the time, Pallas kernels for 0%

commit v1 on v0

v1 whole, which is shorter than its diff:
```python
import functools
import math

import jax
import jax.numpy as jnp
from jax import lax
from jax.experimental import pallas as pl
from jax.experimental.pallas import tpu as pltpu
from jax.sharding import PartitionSpec as P

BF16 = jnp.bfloat16
F32 = jnp.float32
LANES = 128
VMEM_LIMIT = 48 * 1024 * 1024
SLOTS = 3
NT = (((1,), (1,)), ((), ()))
TN = (((0,), (0,)), ((), ()))
FILL = 1e5


def dot(lhs, rhs, dims=(((1,), (0,)), ((), ()))):
    return lax.dot_general(lhs, rhs, dims, preferred_element_type=F32)


def vmem():
    return pl.BlockSpec(memory_space=pltpu.VMEM)


def params():
    return pltpu.CompilerParams(vmem_limit_bytes=VMEM_LIMIT)


def spread_terms(rows):
    high = rows.astype(BF16)
    rest = rows - high.astype(F32)
    middle = rest.astype(BF16)
    low = (rest - middle.astype(F32)).astype(BF16)
    shape = (rows.shape[1], LANES)
    at = lax.broadcasted_iota(jnp.int32, shape, 0)
    lane = lax.broadcasted_iota(jnp.int32, shape, 1)
    out = jnp.zeros((rows.shape[0], LANES), F32)
    for term, values in enumerate((high, middle, low)):
        pick = jnp.where(lane == at * 4 + term, 1.0, 0.0).astype(BF16)
        out = out + dot(values, pick)
    return out


def prepare_kernel(q_ref, do_ref, o_ref, lse_ref, out_ref, lse_out_ref):
    rows, features = q_ref.shape
    heads = features // LANES
    groups = out_ref.shape[0]
    per_group = heads // groups
    product = do_ref[...].astype(F32) * o_ref[...].astype(F32)
    high = product.astype(BF16)
    low = (product - high.astype(F32)).astype(BF16)
    head_at = lax.broadcasted_iota(jnp.int32, (heads, features), 0)
    lane = lax.broadcasted_iota(jnp.int32, (heads, features), 1)
    pick = jnp.where((lane >= head_at * LANES) & (lane < head_at * LANES + LANES), 1.0, 0.0).astype(BF16)
    dots = dot(pick, high, NT) + dot(pick, low, NT)
    dot_terms = spread_terms(dots)
    for h in range(groups):
        for g in range(per_group):
            c = (h * per_group + g) * LANES
            out_ref[h, g * rows : (g + 1) * rows, :] = q_ref[:, c : c + LANES]
            base = (per_group + g) * rows
            out_ref[h, base : base + rows, :] = do_ref[:, c : c + LANES]
        block = dot_terms[h * per_group : (h + 1) * per_group]
        block = jnp.concatenate([block, jnp.zeros((8 - per_group, LANES), F32)], axis=0)
        out_ref[h, 2 * per_group * rows :, :] = block.astype(BF16)
    lse_out_ref[...] = spread_terms(lse_ref[...] * math.sqrt(LANES)).astype(BF16)


def relay_kernel(h_ref, lse_ref, out_ref):
    groups = h_ref.shape[0]
    per_group = lse_ref.shape[0] // groups
    rows = 32
    lse = lse_ref[...].astype(F32)
    quarters = groups // 2
    for g in range(per_group):
        for u in range(quarters):
            for a in range(2):
                r = (a * per_group + g) * quarters + u
                base = (a * per_group + g) * rows
                stats = []
                for part in range(2):
                    src = 2 * u + part
                    out_ref[r, part * rows : (part + 1) * rows, :] = h_ref[src, base : base + rows, :]
                    if a == 0:
                        stats.append(lse[g * groups + src : g * groups + src + 1])
                    else:
                        tile = h_ref[src, 2 * per_group * rows :, :].astype(F32)
                        stats.append(tile[g : g + 1])
                stats.append(jnp.zeros((6, LANES), F32))
                out_ref[r, 2 * rows :, :] = jnp.concatenate(stats, axis=0).astype(BF16)


def gather_kernel(src_ref, fill_ref, in_ref, out_ref):
    owners = out_ref.shape[0]
    fill = fill_ref[0].astype(F32)

    def body(j, carry):
        stats = []
        for slot in range(SLOTS):
            src = src_ref[j * SLOTS + slot]
            at = jnp.maximum(src, 0)
            out_ref[j, slot * 64 : (slot + 1) * 64, :] = in_ref[at, 0:64, :]
            tile = in_ref[at, 64:72, :].astype(F32)
            stats.append(jnp.where(src >= 0, tile[0:2], fill))
        stats.append(jnp.zeros((8 - 2 * SLOTS, LANES), F32))
        out_ref[j, SLOTS * 64 :, :] = jnp.concatenate(stats, axis=0).astype(BF16)
        return carry

    lax.fori_loop(0, owners, body, 0)


def term_mask():
    row = lax.broadcasted_iota(jnp.int32, (32, LANES), 0)
    lane = lax.broadcasted_iota(jnp.int32, (32, LANES), 1)
    return (lane >= row * 4) & (lane < row * 4 + 4)


def assemble(x_ref, head, qx, dx):
    mask = term_mask()
    for a, out in ((0, qx), (1, dx)):
        for u in range(4):
            r = a * 16 + head * 4 + u
            stats = x_ref[r, SLOTS * 64 :, :].astype(F32)
            for slot in range(SLOTS):
                base = slot * 256 + u * 64
                out[base : base + 64, 0:LANES] = x_ref[r, slot * 64 : (slot + 1) * 64, :]
                for part in range(2):
                    row = slot * 2 + part
                    ext = jnp.where(mask, stats[row : row + 1], 0.0).astype(BF16)
                    out[base + part * 32 : base + part * 32 + 32, LANES:] = ext


def extend(block):
    return jnp.concatenate([block, jnp.full((block.shape[0], LANES), -1.0, BF16)], axis=1)


SCALE = LANES**-0.5
EXP_SCALE = SCALE * math.log2(math.e)


def query_kernel(x_ref, k_ref, v_ref, out_ref, qx, dx, acc, *, chunk):
    head = pl.program_id(0)
    assemble(x_ref, head, qx, dx)
    acc[...] = jnp.zeros_like(acc)

    def body(i, carry):
        at = pl.ds(pl.multiple_of(i * chunk, chunk), chunk)
        keys = k_ref[at, :]
        weights = jnp.exp2(dot(qx[...], extend(keys), NT) * EXP_SCALE)
        dscores = (weights * dot(dx[...], extend(v_ref[at, :]), NT)).astype(BF16)
        acc[...] += dot(dscores, keys)
        return carry

    lax.fori_loop(0, k_ref.shape[0] // chunk, body, 0)
    for e in range(8):
        for slot in range(SLOTS):
            base = slot * 256 + e * 32
            out_ref[e, slot * 32 : (slot + 1) * 32, :] = (acc[base : base + 32, :] * SCALE).astype(BF16)


def context_kernel(x_ref, k_ref, v_ref, dk_ref, dv_ref, qx, dx, *, chunk):
    head = pl.program_id(0)
    assemble(x_ref, head, qx, dx)

    def body(i, carry):
        at = pl.ds(pl.multiple_of(i * chunk, chunk), chunk)
        weights = jnp.exp2(dot(extend(k_ref[at, :]), qx[...], NT) * EXP_SCALE)
        dscores = (weights * dot(extend(v_ref[at, :]), dx[...], NT)).astype(BF16)
        dv_ref[at, :] = dot(weights.astype(BF16), dx[:, 0:LANES]).astype(BF16)
        dk_ref[at, :] = (dot(dscores, qx[:, 0:LANES]) * SCALE).astype(BF16)
        return carry

    lax.fori_loop(0, k_ref.shape[0] // chunk, body, 0)


def own_kernel(h_ref, kv_ref, lse_ref, dq_ref, dk_ref, dv_ref, qx, dx, kx, vx):
    head = pl.program_id(0)
    groups = h_ref.shape[0]
    mask = term_mask()
    lse = lse_ref[0].astype(F32)
    kx[:, LANES:] = jnp.full((kx.shape[0], LANES), -1.0, BF16)
    vx[:, LANES:] = jnp.full((kx.shape[0], LANES), -1.0, BF16)
    for src in range(groups):
        at = slice(src * 32, src * 32 + 32)
        first = pl.ds(pl.multiple_of(head * 32, 32), 32)
        second = pl.ds(pl.multiple_of(head * 32 + 128, 32), 32)
        qx[at, 0:LANES] = h_ref[src, first, :]
        dx[at, 0:LANES] = h_ref[src, second, :]
        kx[at, 0:LANES] = kv_ref[src, first, :]
        vx[at, 0:LANES] = kv_ref[src, second, :]
        qx[at, LANES:] = jnp.where(mask, lse[src : src + 1], 0.0).astype(BF16)
        tile = h_ref[src, 256:, :].astype(F32)
        at_head = lax.broadcasted_iota(jnp.int32, tile.shape, 0) == head
        row = jnp.sum(jnp.where(at_head, tile, 0.0), axis=0, keepdims=True)
        dx[at, LANES:] = jnp.where(mask, row, 0.0).astype(BF16)
    shape = (qx.shape[0], kx.shape[0])
    allowed = lax.broadcasted_iota(jnp.int32, shape, 0) >= lax.broadcasted_iota(jnp.int32, shape, 1)
    weights = jnp.where(allowed, jnp.exp2(dot(qx[...], kx[...], NT) * EXP_SCALE), 0.0)
    dscores = (weights * dot(dx[...], vx[...], NT)).astype(BF16)
    dq_ref[...] = dot(dscores, kx[:, 0:LANES]) * SCALE
    dk_ref[...] = (dot(dscores, qx[:, 0:LANES], TN) * SCALE).astype(BF16)
    dv_ref[...] = dot(weights.astype(BF16), dx[:, 0:LANES], TN).astype(BF16)


def pair_kernel(at_ref, in_ref, out_ref):
    def body(b, carry):
        total = None
        for s in range(2):
            part = at_ref[b * 2 + s]
            owner = part // SLOTS
            row = pl.multiple_of((part - owner * SLOTS) * 32, 32)
            value = in_ref[owner, pl.ds(row, 32), :].astype(F32)
            total = value if total is None else total + value
        out_ref[b] = total.astype(BF16)
        return carry

    lax.fori_loop(0, out_ref.shape[0], body, 0)


def finish_kernel(in_ref, own_ref, out_ref):
    out_ref[...] = (in_ref[...].astype(F32).reshape(own_ref.shape) + own_ref[...]).astype(BF16)


def per_device(queries, new_keys, new_values, attn_out, out_grad, logsumexp, ctx_keys, ctx_values, selected):
    owners = lax.axis_size("seq")
    groups = lax.axis_size("head")
    per_group, block_rows = logsumexp.shape
    rows = queries.shape[0]
    key_rows, features = ctx_keys.shape
    relay = lax.axis_index("seq")

    flat = selected.reshape(-1)
    order = jnp.arange(flat.shape[0])
    same = flat[:, None] == flat[None, :]
    slot_of = jnp.sum(same & (order[None, :] < order[:, None]), axis=1).astype(jnp.int32)
    place = flat * SLOTS + slot_of
    hit = place[None, :] == jnp.arange(owners * SLOTS)[:, None]
    source = jnp.max(jnp.where(hit, (order // selected.shape[1])[None, :], -1), axis=1).astype(jnp.int32)
    fill = jnp.where(relay < owners // 2, FILL, 0.0).astype(F32).reshape(1)

    lse_rows = logsumexp.reshape(per_group * groups, rows)
    head_out, lse_terms = pl.pallas_call(
        prepare_kernel,
        out_shape=(
            jax.ShapeDtypeStruct((groups, 2 * per_group * rows + 8, LANES), BF16),
            jax.ShapeDtypeStruct((per_group * groups, LANES), BF16),
        ),
        in_specs=[vmem()] * 4,
        out_specs=(vmem(), vmem()),
        compiler_params=params(),
        name="prepare",
    )(queries, out_grad, attn_out, lse_rows)
    window = lax.all_to_all(head_out, "head", split_axis=0, concat_axis=0, tiled=True)

    pieces = pl.pallas_call(
        relay_kernel,
        out_shape=jax.ShapeDtypeStruct((owners, 72, LANES), BF16),
        in_specs=[vmem()] * 2,
        out_specs=vmem(),
        compiler_params=params(),
        name="relay",
    )(window, lse_terms)
    held = lax.all_to_all(pieces, "seq", split_axis=0, concat_axis=0, tiled=True)

    smem = pl.BlockSpec(memory_space=pltpu.SMEM)
    outgoing = pl.pallas_call(
        gather_kernel,
        out_shape=jax.ShapeDtypeStruct((owners, SLOTS * 64 + 8, LANES), BF16),
        in_specs=[smem, smem, vmem()],
        out_specs=vmem(),
        compiler_params=params(),
        name="gather",
    )(source, fill, held)
    items = lax.all_to_all(outgoing, "seq", split_axis=0, concat_axis=0, tiled=True)

    def heads_of(tensor):
        return tensor.reshape(rows, groups, per_group, LANES).transpose(1, 2, 0, 3).reshape(groups, per_group * rows, LANES)

    own_kv = jnp.concatenate([heads_of(new_keys), heads_of(new_values)], axis=1)
    items, own_kv = lax.optimization_barrier((items, own_kv))
    own_kv = lax.all_to_all(own_kv, "head", split_axis=0, concat_axis=0, tiled=True)

    chunk = 256
    slot_rows = SLOTS * block_rows
    context_spec = pl.BlockSpec((key_rows, LANES), lambda g: (0, g))
    items_spec = pl.BlockSpec((owners, SLOTS * 64 + 8, LANES), lambda g: (0, 0, 0))
    work = 2 * slot_rows * key_rows * LANES * per_group
    parts = pl.pallas_call(
        functools.partial(query_kernel, chunk=chunk),
        grid=(per_group,),
        out_shape=jax.ShapeDtypeStruct((owners, SLOTS * 32, LANES), BF16),
        in_specs=[items_spec, context_spec, context_spec],
        out_specs=pl.BlockSpec((owners // per_group, SLOTS * 32, LANES), lambda g: (g, 0, 0)),
        scratch_shapes=[
            pltpu.VMEM((slot_rows, 2 * LANES), BF16),
            pltpu.VMEM((slot_rows, 2 * LANES), BF16),
            pltpu.VMEM((slot_rows, LANES), F32),
        ],
        compiler_params=params(),
        cost_estimate=pl.CostEstimate(flops=5 * work, bytes_accessed=6 << 20, transcendentals=slot_rows * key_rows * per_group),
        name="query_parts",
    )(items, ctx_keys, ctx_values)

    returned = lax.all_to_all(parts, "seq", split_axis=0, concat_axis=0, tiled=True)

    items_later, own_kv, _ = lax.optimization_barrier((items, own_kv, parts))
    ctx_key_grad, ctx_value_grad = pl.pallas_call(
        functools.partial(context_kernel, chunk=chunk),
        grid=(per_group,),
        out_shape=(jax.ShapeDtypeStruct((key_rows, features), BF16),) * 2,
        in_specs=[items_spec, context_spec, context_spec],
        out_specs=(context_spec, context_spec),
        scratch_shapes=[
            pltpu.VMEM((slot_rows, 2 * LANES), BF16),
            pltpu.VMEM((slot_rows, 2 * LANES), BF16),
        ],
        compiler_params=params(),
        cost_estimate=pl.CostEstimate(flops=6 * work, bytes_accessed=10 << 20, transcendentals=slot_rows * key_rows * per_group),
        name="context_grads",
    )(items_later, ctx_keys, ctx_values)

    head_spec = pl.BlockSpec((block_rows, LANES), lambda g: (0, g))
    whole = lambda shape: pl.BlockSpec(shape, lambda g: (0,) * len(shape))
    own_dq, new_key_grad, new_value_grad = pl.pallas_call(
        own_kernel,
        grid=(per_group,),
        out_shape=(
            jax.ShapeDtypeStruct((block_rows, features), F32),
            jax.ShapeDtypeStruct((block_rows, features), BF16),
            jax.ShapeDtypeStruct((block_rows, features), BF16),
        ),
        in_specs=[whole(window.shape), whole(own_kv.shape), pl.BlockSpec((1, groups, LANES), lambda g: (g, 0, 0))],
        out_specs=(head_spec, head_spec, head_spec),
        scratch_shapes=[pltpu.VMEM((block_rows, 2 * LANES), BF16)] * 4,
        compiler_params=params(),
        cost_estimate=pl.CostEstimate(flops=10 * block_rows * block_rows * features, bytes_accessed=2 << 20, transcendentals=0),
        name="own_set",
    )(window, own_kv, lse_terms.reshape(per_group, groups, LANES))

    summed = pl.pallas_call(
        pair_kernel,
        out_shape=jax.ShapeDtypeStruct((owners, 32, LANES), BF16),
        in_specs=[smem, vmem()],
        out_specs=vmem(),
        compiler_params=params(),
        name="pair_sum",
    )(place, returned)
    home = lax.all_to_all(summed, "seq", split_axis=0, concat_axis=0, tiled=True)
    query_grad = pl.pallas_call(
        finish_kernel,
        grid=(per_group,),
        out_shape=jax.ShapeDtypeStruct((block_rows, features), BF16),
        in_specs=[pl.BlockSpec((owners // per_group, 32, LANES), lambda g: (g, 0, 0)), head_spec],
        out_specs=head_spec,
        compiler_params=params(),
        name="finish",
    )(home, own_dq)
    return (query_grad, new_key_grad, new_value_grad, ctx_key_grad, ctx_value_grad)


def solution(mesh):
    in_specs = (
        P(("seq", "head"), None),
        P(("seq", "head"), None),
        P(("seq", "head"), None),
        P(("seq", "head"), None),
        P(("seq", "head"), None),
        P("head", "seq"),
        P("seq", "head"),
        P("seq", "head"),
        P(),
    )
    out_specs = (P("seq", "head"),) * 5
    return jax.shard_map(per_device, mesh=mesh, in_specs=in_specs, out_specs=out_specs, check_vma=False)
```

time: 820 us -> 191 us (0.23)
  waiting for transfers between devices: 559 us -> 74.1 us
  local copies, waits for them, and re-layouts: 121 us -> 11.8 us
  Pallas kernels: 0 us -> 54.1 us
  matrix products: 43.2 us -> 0 us
  starting transfers between devices: 66.1 us -> 32.8 us
  other arithmetic: 22.3 us -> 1.12 us
  blocking collectives: 0 us -> 14.7 us
    all_to_all x9 -> x5, waiting for transfers between devices: 559 us -> 74.1 us  [the longest x1 37.5 us: per_device(): lax.all_to_all(outgoing, 'seq', split_axis=0, concat_axis=0, tiled=True)]
    pallas_call x0 -> x8, Pallas kernels: none -> 54.1 us  [the longest x1 22.1 us: per_device(): pl.pallas_call(functools.partial(query_kernel, chunk=chunk), grid=(per_gr...]
    dot_general x61 -> x0, matrix products: 43.2 us -> none  [the longest x12 13.8 us: head_grads(): jnp.dot(grad_out, value_block.T, preferred_element_type=jnp.float32)]
    all_to_all x9 -> x5, starting transfers between devices: 66.1 us -> 32.8 us  [the longest x1 11.4 us: per_device(): lax.all_to_all(pieces, 'seq', split_axis=0, concat_axis=0, tiled=True)]
    while x76 -> x0, local copies, waits for them, and re-layouts: 32.1 us -> none
    reshape x5 -> x6, local copies, waits for them, and re-layouts: 17.6 us -> 1.42 us  [the longest x1 0.76 us: per_device(): lse_rows = logsumexp.reshape(per_group * groups, rows)]
    all_to_all x0 -> x1, blocking collectives: none -> 14.7 us  [per_device(): lax.all_to_all(head_out, 'head', split_axis=0, concat_axis=0, tiled=True)]
    transpose x6 -> x0, local copies, waits for them, and re-layouts: 14.4 us -> none  [merge_heads(): return tensor.transpose(1, 0, 2).reshape(row_count, head_count * head_size)]
  transfers between devices with their start and end apart: 9 -> 5, of which waited for: 5 -> 3; matrix products, arithmetic and copies ran while one was open for 20% -> 1% of each run, Pallas kernels for 0% -> 25%
where the time goes in v1:
time: 191 us; the launch traced here: 189 us
  waiting for transfers between devices  74.1 us (39%)
  Pallas kernels  54.1 us (28%)
  starting transfers between devices  32.8 us (17%)
  blocking collectives  14.7 us (8%)
  local copies, waits for them, and re-layouts  11.8 us (6%)
    all_to_all x1, waiting for transfers between devices, per_device(): lax.all_to_all(outgoing, 'seq', split_axis=0, concat_axis=0, tiled=True)  37.5 us
    pallas_call x1, Pallas kernels, per_device(): pl.pallas_call(functools.partial(query_kernel, chunk=chunk), grid=(per_gr...  22.1 us
    pallas_call x1, Pallas kernels, per_device(): pl.pallas_call(functools.partial(context_kernel, chunk=chunk), grid=(per_...  22 us
    all_to_all x1, waiting for transfers between devices, per_device(): lax.all_to_all(parts, 'seq', split_axis=0, concat_axis=0, tiled=True)  18.4 us
    all_to_all x1, waiting for transfers between devices, per_device(): lax.all_to_all(pieces, 'seq', split_axis=0, concat_axis=0, tiled=True)  18.2 us
    all_to_all x1, blocking collectives, per_device(): lax.all_to_all(head_out, 'head', split_axis=0, concat_axis=0, tiled=True)  14.7 us
    all_to_all x1, starting transfers between devices, per_device(): lax.all_to_all(pieces, 'seq', split_axis=0, concat_axis=0, tiled=True)  11.4 us
    unnamed x25, local copies, waits for them, and re-layouts  10.4 us
  transfers between devices with their start and end apart: 5, of which 3 were waited for; matrix products, arithmetic and copies ran while one was open for 1% of the time, Pallas kernels for 25%

profile of v1, /device:TPU:32, one launch (start us, length us, event | category | flops | bytes accessed | tf_op | source)
XLA Modules:
  0.0 189.5 jit_solution(10269493054795121501)
XLA Ops:
  1.4 0.9 copy-done.3
  2.3 0.9 copy-done.4
  3.3 0.9 copy-done.5
  4.7 14.7 %all_to_all.30.h_ref = bf16[8,264,128]{2,1,0:T(8,128)(2,1)S(1)} all-to-all(bf16[8,264,128]{2,1,0:T(8,128)(2,1)S(1)} %get-tuple-element.16), channel_id=1, replica_groups=mesh['seq'=32,'head'=8] {'head'}, dimensions={0} | all-to-all | bytes 1081344 | tf_op jit(solution)/shard_map/all_to_all | solution.py:257
  19.4 0.9 relay.1
  20.3 11.4 %all-to-all-start.1 = ((bf16[32,72,128]{2,1,0:T(8,128)(2,1)}), bf16[32,72,128]{2,1,0:T(8,128)(2,1)S(1)}, u32[]{:S(2)}, u32[]{:S(2)}) async-start(bf16[32,72,128]{2,1,0:T(8,128)(2,1)} %relay.1), calls=%async_computation.1 | async-start | bytes 1179648 | tf_op jit(solution)/shard_map/all_to_all | solution.py:267
  32.1 18.2 %all-to-all-done.1.in_ref = bf16[32,72,128]{2,1,0:T(8,128)(2,1)S(1)} async-done(((bf16[32,72,128]{2,1,0:T(8,128)(2,1)}), bf16[32,72,128]{2,1,0:T(8,128)(2,1)S(1)}, u32[]{:S(2)}, u32[]{:S(2)}) %all-to-all-start.1) | async-done | bytes 589856 | tf_op jit(solution)/shard_map/all_to_all | solution.py:267
  50.3 2.3 %gather.1 = bf16[32,200,128]{2,1,0:T(8,128)(2,1)} custom-call(s32[96]{0:T(128)S(1)} %select_reduce_fusion.src_ref, f32[1]{0:T(128)} %bitcast.fill_ref, bf16[32,72,128]{2,1,0:T(8,128)(2,1)S(1)} %all-to-all-done.1.in_ref), custom_call_target="tpu_custom_call" | custom-call | tf_op jit(solution)/shard_map/gather/pallas_call | solution.py:270
  52.6 5.4 %all-to-all-start.2 = ((bf16[32,200,128]{2,1,0:T(8,128)(2,1)}), bf16[32,200,128]{2,1,0:T(8,128)(2,1)S(1)}, u32[]{:S(2)}, u32[]{:S(2)}) async-start(bf16[32,200,128]{2,1,0:T(8,128)(2,1)} %gather.1), calls=%async_computation.2 | async-start | bytes 3276800 | tf_op jit(solution)/shard_map/all_to_all | solution.py:278
  59.4 37.5 %all-to-all-done.2.x_ref = bf16[32,200,128]{2,1,0:T(8,128)(2,1)S(1)} async-done(((bf16[32,200,128]{2,1,0:T(8,128)(2,1)}), bf16[32,200,128]{2,1,0:T(8,128)(2,1)S(1)}, u32[]{:S(2)}, u32[]{:S(2)}) %all-to-all-start.2) | async-done | bytes 1638432 | tf_op jit(solution)/shard_map/all_to_all | solution.py:278
  96.9 3.5 %all-to-all-start.5 = ((bf16[8,256,128]{2,1,0:T(8,128)(2,1)}), bf16[8,256,128]{2,1,0:T(8,128)(2,1)S(1)}, u32[]{:S(2)}, u32[]{:S(2)}) async-start(bf16[8,256,128]{2,1,0:T(8,128)(2,1)} %pad_maximum_fusion), calls=%async_computation.5 | async-start | bytes 1048576 | tf_op jit(solution)/shard_map/all_to_all | solution.py:285
  100.5 1.6 copy-done.6
  102.0 22.1 %query_parts.1 = bf16[32,96,128]{2,1,0:T(8,128)(2,1)S(1)} custom-call(bf16[32,200,128]{2,1,0:T(8,128)(2,1)S(1)} %all-to-all-done.2.x_ref, bf16[2048,512]{1,0:T(8,128)(2,1)S(1)} %copy-done.6, bf16[2048,512]{1,0:T(8,128)(2,1)} %v_ref.3), custom_call_target="tpu_custom_call" | custom-call | flops 8053063680 | bytes 6291456 | tf_op jit(solution)/shard_map/query_parts/pallas_call | solution.py:292
  124.1 0.9 copy-done
  125.8 6.5 %all-to-all-start.3 = ((bf16[32,96,128]{2,1,0:T(8,128)(2,1)}), bf16[32,96,128]{2,1,0:T(8,128)(2,1)S(1)}, u32[]{:S(2)}, u32[]{:S(2)}) async-start(bf16[32,96,128]{2,1,0:T(8,128)(2,1)} %copy-done), calls=%async_computation.3 | async-start | bytes 1572864 | tf_op jit(solution)/shard_map/all_to_all | solution.py:308
  132.3 1.0 copy-done.2
  133.3 3.0 %own_set.1 = (f32[256,512]{1,0:T(8,128)S(1)}, bf16[256,512]{1,0:T(8,128)(2,1)}, bf16[256,512]{1,0:T(8,128)(2,1)}) custom-call(bf16[8,264,128]{2,1,0:T(8,128)(2,1)S(1)} %all_to_all.30.h_ref, bf16[8,256,128]{2,1,0:T(8,128)(2,1)S(1)} %copy-done.2, bf16[4,8,128]{2,1,0:T(8,128)(2,1)S(1)} %bitcast.8), custom_call_target="tpu_custom_call" | custom-call | flops 335544320 | bytes 2097152 | tf_op jit(solution)/shard_map/own_set/pallas_call | solution.py:328
  136.3 18.4 %all-to-all-done.3.in_ref = bf16[32,96,128]{2,1,0:T(8,128)(2,1)S(1)} async-done(((bf16[32,96,128]{2,1,0:T(8,128)(2,1)}), bf16[32,96,128]{2,1,0:T(8,128)(2,1)S(1)}, u32[]{:S(2)}, u32[]{:S(2)}) %all-to-all-start.3) | async-done | bytes 786464 | tf_op jit(solution)/shard_map/all_to_all | solution.py:308
  154.8 2.1 %pair_sum.1 = bf16[32,32,128]{2,1,0:T(8,128)(2,1)} custom-call(s32[64]{0:T(128)S(1)} %get-tuple-element.28.at_ref, bf16[32,96,128]{2,1,0:T(8,128)(2,1)S(1)} %all-to-all-done.3.in_ref), custom_call_target="tpu_custom_call" | custom-call | tf_op jit(solution)/shard_map/pair_sum/pallas_call | solution.py:344
  156.8 6.1 %all-to-all-start.4 = ((bf16[32,32,128]{2,1,0:T(8,128)(2,1)}), bf16[32,32,128]{2,1,0:T(8,128)(2,1)S(1)}, u32[]{:S(2)}, u32[]{:S(2)}) async-start(bf16[32,32,128]{2,1,0:T(8,128)(2,1)} %pair_sum.1), calls=%async_computation.4 | async-start | bytes 524288 | tf_op jit(solution)/shard_map/all_to_all | solution.py:352
  162.9 1.6 copy-done.7
  164.5 1.6 copy-done.8
  166.1 22.0 %context_grads.1 = (bf16[2048,512]{1,0:T(8,128)(2,1)}, bf16[2048,512]{1,0:T(8,128)(2,1)}) custom-call(bf16[32,200,128]{2,1,0:T(8,128)(2,1)S(1)} %all-to-all-done.2.x_ref, bf16[2048,512]{1,0:T(8,128)(2,1)S(1)} %copy-done.7, bf16[2048,512]{1,0:T(8,128)(2,1)S(1)} %copy-done.8), custom_call_target="tpu_custom_call" | custom-call | flops 9663676416 | bytes 10485760 | tf_op jit(solution)/shard_map/context_grads/pallas_call | solution.py:311
  188.1 1.4 finish.1
  (30 shorter events, 3.9 us)
Async XLA Ops:
  1.4 1.0 copy-start.3
  2.3 0.9 copy-start.4
  3.3 0.9 copy-start.5
  4.2 27.4 %copy-start.11 = (s32[32,2]{0,1:T(2,128)S(1)}, s32[32,2]{0,1:T(2,128)}, u32[]{:S(2)}) copy-start(s32[32,2]{0,1:T(2,128)} %param.17) | copy-start | bytes 772
  20.3 30.1 %all-to-all-start.1 = ((bf16[32,72,128]{2,1,0:T(8,128)(2,1)}), bf16[32,72,128]{2,1,0:T(8,128)(2,1)S(1)}, u32[]{:S(2)}, u32[]{:S(2)}) async-start(bf16[32,72,128]{2,1,0:T(8,128)(2,1)} %relay.1), calls=%async_computation.1 | async-start | bytes 1179648 | tf_op jit(solution)/shard_map/all_to_all | solution.py:267
  52.6 5.5 %copy-start.9 = (bf16[32,4096]{1,0:T(8,128)(2,1)S(1)}, bf16[32,4096]{1,0:T(8,128)(2,1)}, u32[]{:S(2)}) copy-start(bf16[32,4096]{1,0:T(8,128)(2,1)} %param.10) | copy-start | bytes 786436
  52.6 5.7 %copy-start.10 = (bf16[32,4096]{1,0:T(8,128)(2,1)S(1)}, bf16[32,4096]{1,0:T(8,128)(2,1)}, u32[]{:S(2)}) copy-start(bf16[32,4096]{1,0:T(8,128)(2,1)} %param.11) | copy-start | bytes 786436
  52.6 44.4 %all-to-all-start.2 = ((bf16[32,200,128]{2,1,0:T(8,128)(2,1)}), bf16[32,200,128]{2,1,0:T(8,128)(2,1)S(1)}, u32[]{:S(2)}, u32[]{:S(2)}) async-start(bf16[32,200,128]{2,1,0:T(8,128)(2,1)} %gather.1), calls=%async_computation.2 | async-start | bytes 3276800 | tf_op jit(solution)/shard_map/all_to_all | solution.py:278
  96.9 28.1 %all-to-all-start.5 = ((bf16[8,256,128]{2,1,0:T(8,128)(2,1)}), bf16[8,256,128]{2,1,0:T(8,128)(2,1)S(1)}, u32[]{:S(2)}, u32[]{:S(2)}) async-start(bf16[8,256,128]{2,1,0:T(8,128)(2,1)} %pad_maximum_fusion), calls=%async_computation.5 | async-start | bytes 1048576 | tf_op jit(solution)/shard_map/all_to_all | solution.py:285
  100.4 1.6 copy-start.6
  124.1 0.9 copy-start
  125.0 0.8 copy-start.1
  125.8 29.0 %all-to-all-start.3 = ((bf16[32,96,128]{2,1,0:T(8,128)(2,1)}), bf16[32,96,128]{2,1,0:T(8,128)(2,1)S(1)}, u32[]{:S(2)}, u32[]{:S(2)}) async-start(bf16[32,96,128]{2,1,0:T(8,128)(2,1)} %copy-done), calls=%async_computation.3 | async-start | bytes 1572864 | tf_op jit(solution)/shard_map/all_to_all | solution.py:308
  132.3 1.0 copy-start.2
  156.8 31.2 %all-to-all-start.4 = ((bf16[32,32,128]{2,1,0:T(8,128)(2,1)}), bf16[32,32,128]{2,1,0:T(8,128)(2,1)S(1)}, u32[]{:S(2)}, u32[]{:S(2)}) async-start(bf16[32,32,128]{2,1,0:T(8,128)(2,1)} %pair_sum.1), calls=%async_computation.4 | async-start | bytes 524288 | tf_op jit(solution)/shard_map/all_to_all | solution.py:352
  162.9 1.6 copy-start.7
  164.5 1.6 copy-start.8

commit v2 on v1

--- a/solution.py
+++ b/solution.py
@@ -11,7 +11,7 @@
 BF16 = jnp.bfloat16
 F32 = jnp.float32
 LANES = 128
-VMEM_LIMIT = 48 * 1024 * 1024
+MIB = 1024 * 1024
 SLOTS = 3
 NT = (((1,), (1,)), ((), ()))
 TN = (((0,), (0,)), ((), ()))
@@ -26,8 +26,12 @@
     return pl.BlockSpec(memory_space=pltpu.VMEM)
 
 
-def params():
-    return pltpu.CompilerParams(vmem_limit_bytes=VMEM_LIMIT)
+def in_hbm(array):
+    return pltpu.with_memory_space_constraint(array, pltpu.HBM)
+
+
+def params(mib=8):
+    return pltpu.CompilerParams(vmem_limit_bytes=mib * MIB)
 
 
 def spread_terms(rows):
@@ -45,11 +49,23 @@
     return out
 
 
-def prepare_kernel(q_ref, do_ref, o_ref, lse_ref, out_ref, lse_out_ref):
+def lse_kernel(lse_ref, out_ref):
+    out_ref[...] = spread_terms(lse_ref[...] * math.sqrt(LANES)).astype(BF16)
+
+
+def prepare_kernel(q_hbm, do_hbm, o_hbm, out_ref, q_ref, do_ref, o_ref, sems):
+    copies = [
+        pltpu.make_async_copy(src, dst, sems.at[n])
+        for n, (src, dst) in enumerate(((do_hbm, do_ref), (o_hbm, o_ref), (q_hbm, q_ref)))
+    ]
+    for copy in copies:
+        copy.start()
     rows, features = q_ref.shape
     heads = features // LANES
     groups = out_ref.shape[0]
     per_group = heads // groups
+    copies[0].wait()
+    copies[1].wait()
     product = do_ref[...].astype(F32) * o_ref[...].astype(F32)
     high = product.astype(BF16)
     low = (product - high.astype(F32)).astype(BF16)
@@ -58,6 +74,7 @@
     pick = jnp.where((lane >= head_at * LANES) & (lane < head_at * LANES + LANES), 1.0, 0.0).astype(BF16)
     dots = dot(pick, high, NT) + dot(pick, low, NT)
     dot_terms = spread_terms(dots)
+    copies[2].wait()
     for h in range(groups):
         for g in range(per_group):
             c = (h * per_group + g) * LANES
@@ -67,7 +84,6 @@
         block = dot_terms[h * per_group : (h + 1) * per_group]
         block = jnp.concatenate([block, jnp.zeros((8 - per_group, LANES), F32)], axis=0)
         out_ref[h, 2 * per_group * rows :, :] = block.astype(BF16)
-    lse_out_ref[...] = spread_terms(lse_ref[...] * math.sqrt(LANES)).astype(BF16)
 
 
 def relay_kernel(h_ref, lse_ref, out_ref):
@@ -94,23 +110,33 @@
                 out_ref[r, 2 * rows :, :] = jnp.concatenate(stats, axis=0).astype(BF16)
 
 
-def gather_kernel(src_ref, fill_ref, in_ref, out_ref):
+def gather_kernel(src_ref, fill_ref, in_ref, out_hbm, out_ref, sems):
     owners = out_ref.shape[0]
     fill = fill_ref[0].astype(F32)
-
-    def body(j, carry):
-        stats = []
-        for slot in range(SLOTS):
-            src = src_ref[j * SLOTS + slot]
-            at = jnp.maximum(src, 0)
-            out_ref[j, slot * 64 : (slot + 1) * 64, :] = in_ref[at, 0:64, :]
-            tile = in_ref[at, 64:72, :].astype(F32)
-            stats.append(jnp.where(src >= 0, tile[0:2], fill))
-        stats.append(jnp.zeros((8 - 2 * SLOTS, LANES), F32))
-        out_ref[j, SLOTS * 64 :, :] = jnp.concatenate(stats, axis=0).astype(BF16)
+    count = 4
+
+    def leave(part):
+        at = pl.ds(part * count, count)
+        return pltpu.make_async_copy(out_ref.at[at], out_hbm.at[at], sems.at[part])
+
+    def body(part, carry):
+        for k in range(count):
+            j = part * count + k
+            stats = []
+            for slot in range(SLOTS):
+                src = src_ref[j * SLOTS + slot]
+                at = jnp.maximum(src, 0)
+                out_ref[j, slot * 64 : (slot + 1) * 64, :] = in_ref[at, 0:64, :]
+                tile = in_ref[at, 64:72, :].astype(F32)
+                stats.append(jnp.where(src >= 0, tile[0:2], fill))
+            stats.append(jnp.zeros((8 - 2 * SLOTS, LANES), F32))
+            out_ref[j, SLOTS * 64 :, :] = jnp.concatenate(stats, axis=0).astype(BF16)
+        leave(part).start()
         return carry
 
-    lax.fori_loop(0, owners, body, 0)
+    lax.fori_loop(0, owners // count, body, 0)
+    for part in range(owners // count):
+        leave(part).wait()
 
 
 def term_mask():
@@ -142,24 +168,42 @@
 EXP_SCALE = SCALE * math.log2(math.e)
 
 
-def query_kernel(x_ref, k_ref, v_ref, out_ref, qx, dx, acc, *, chunk):
-    head = pl.program_id(0)
-    assemble(x_ref, head, qx, dx)
-    acc[...] = jnp.zeros_like(acc)
-
-    def body(i, carry):
-        at = pl.ds(pl.multiple_of(i * chunk, chunk), chunk)
-        keys = k_ref[at, :]
-        weights = jnp.exp2(dot(qx[...], extend(keys), NT) * EXP_SCALE)
-        dscores = (weights * dot(dx[...], extend(v_ref[at, :]), NT)).astype(BF16)
-        acc[...] += dot(dscores, keys)
+def query_kernel(x_ref, k_hbm, v_hbm, out_hbm, k_ref, v_ref, out_ref, qx, dx, sems, out_sems):
+    per_group = k_ref.shape[0]
+
+    def fetch(head, which):
+        src, dst = ((k_hbm, k_ref), (v_hbm, v_ref))[which]
+        at = pl.ds(pl.multiple_of(head * LANES, LANES), LANES)
+        return pltpu.make_async_copy(src.at[:, at], dst.at[head], sems.at[head, which])
+
+    def leave(head):
+        at = pl.ds(head * 8, 8)
+        return pltpu.make_async_copy(out_ref.at[at], out_hbm.at[at], out_sems.at[head])
+
+    for head in range(per_group):
+        fetch(head, 0).start()
+        fetch(head, 1).start()
+
+    def body(head, carry):
+        assemble(x_ref, head, qx, dx)
+        fetch(head, 0).wait()
+        fetch(head, 1).wait()
+        keys = k_ref[head]
+        keys_ext = extend(keys)
+        values_ext = extend(v_ref[head])
+        for slot in range(SLOTS):
+            at = slice(slot * 256, slot * 256 + 256)
+            weights = jnp.exp2(dot(qx[at], keys_ext, NT) * EXP_SCALE)
+            dscores = (weights * dot(dx[at], values_ext, NT)).astype(BF16)
+            part = (dot(dscores, keys) * SCALE).astype(BF16)
+            for e in range(8):
+                out_ref[head * 8 + e, slot * 32 : (slot + 1) * 32, :] = part[e * 32 : (e + 1) * 32]
+        leave(head).start()
         return carry
 
-    lax.fori_loop(0, k_ref.shape[0] // chunk, body, 0)
-    for e in range(8):
-        for slot in range(SLOTS):
-            base = slot * 256 + e * 32
-            out_ref[e, slot * 32 : (slot + 1) * 32, :] = (acc[base : base + 32, :] * SCALE).astype(BF16)
+    lax.fori_loop(0, per_group, body, 0)
+    for head in range(per_group):
+        leave(head).wait()
 
 
 def context_kernel(x_ref, k_ref, v_ref, dk_ref, dv_ref, qx, dx, *, chunk):
@@ -174,7 +218,7 @@
         dk_ref[at, :] = (dot(dscores, qx[:, 0:LANES]) * SCALE).astype(BF16)
         return carry
 
-    lax.fori_loop(0, k_ref.shape[0] // chunk, body, 0)
+    lax.fori_loop(0, k_ref.shape[0] // chunk, body, 0, unroll=True)
 
 
 def own_kernel(h_ref, kv_ref, lse_ref, dq_ref, dk_ref, dv_ref, qx, dx, kx, vx):
@@ -206,23 +250,25 @@
     dv_ref[...] = dot(weights.astype(BF16), dx[:, 0:LANES], TN).astype(BF16)
 
 
-def pair_kernel(at_ref, in_ref, out_ref):
+def pair_kernel(owner_ref, row_ref, in_ref, out_ref):
     def body(b, carry):
         total = None
         for s in range(2):
-            part = at_ref[b * 2 + s]
-            owner = part // SLOTS
-            row = pl.multiple_of((part - owner * SLOTS) * 32, 32)
-            value = in_ref[owner, pl.ds(row, 32), :].astype(F32)
+            row = pl.multiple_of(row_ref[b * 2 + s], 32)
+            value = in_ref[owner_ref[b * 2 + s], pl.ds(row, 32), :].astype(F32)
             total = value if total is None else total + value
         out_ref[b] = total.astype(BF16)
         return carry
 
-    lax.fori_loop(0, out_ref.shape[0], body, 0)
+    lax.fori_loop(0, out_ref.shape[0], body, 0, unroll=4)
 
 
 def finish_kernel(in_ref, own_ref, out_ref):
-    out_ref[...] = (in_ref[...].astype(F32).reshape(own_ref.shape) + own_ref[...]).astype(BF16)
+    count = in_ref.shape[0] // 4
+    for g in range(4):
+        part = in_ref[g * count : (g + 1) * count].astype(F32).reshape(own_ref.shape[0], LANES)
+        at = slice(g * LANES, (g + 1) * LANES)
+        out_ref[:, at] = (part + own_ref[:, at]).astype(BF16)
 
 
 def per_device(queries, new_keys, new_values, attn_out, out_grad, logsumexp, ctx_keys, ctx_values, selected):
@@ -242,18 +288,24 @@
     source = jnp.max(jnp.where(hit, (order // selected.shape[1])[None, :], -1), axis=1).astype(jnp.int32)
     fill = jnp.where(relay < owners // 2, FILL, 0.0).astype(F32).reshape(1)
 
-    lse_rows = logsumexp.reshape(per_group * groups, rows)
-    head_out, lse_terms = pl.pallas_call(
+    hbm = pl.BlockSpec(memory_space=pltpu.HBM)
+    head_out = pl.pallas_call(
         prepare_kernel,
-        out_shape=(
-            jax.ShapeDtypeStruct((groups, 2 * per_group * rows + 8, LANES), BF16),
-            jax.ShapeDtypeStruct((per_group * groups, LANES), BF16),
-        ),
-        in_specs=[vmem()] * 4,
-        out_specs=(vmem(), vmem()),
+        out_shape=jax.ShapeDtypeStruct((groups, 2 * per_group * rows + 8, LANES), BF16),
+        in_specs=[hbm] * 3,
+        out_specs=vmem(),
+        scratch_shapes=[pltpu.VMEM(queries.shape, BF16)] * 3 + [pltpu.SemaphoreType.DMA((3,))],
         compiler_params=params(),
         name="prepare",
-    )(queries, out_grad, attn_out, lse_rows)
+    )(in_hbm(queries), in_hbm(out_grad), in_hbm(attn_out))
+    lse_terms = pl.pallas_call(
+        lse_kernel,
+        out_shape=jax.ShapeDtypeStruct((per_group * groups, LANES), BF16),
+        in_specs=[vmem()],
+        out_specs=vmem(),
+        compiler_params=params(),
+        name="lse_terms",
+    )(logsumexp.reshape(per_group * groups, rows))
     window = lax.all_to_all(head_out, "head", split_axis=0, concat_axis=0, tiled=True)
 
     pieces = pl.pallas_call(
@@ -271,60 +323,67 @@
         gather_kernel,
         out_shape=jax.ShapeDtypeStruct((owners, SLOTS * 64 + 8, LANES), BF16),
         in_specs=[smem, smem, vmem()],
-        out_specs=vmem(),
+        out_specs=hbm,
+        scratch_shapes=[pltpu.VMEM((owners, SLOTS * 64 + 8, LANES), BF16), pltpu.SemaphoreType.DMA((8,))],
         compiler_params=params(),
         name="gather",
     )(source, fill, held)
     items = lax.all_to_all(outgoing, "seq", split_axis=0, concat_axis=0, tiled=True)
 
-    def heads_of(tensor):
-        return tensor.reshape(rows, groups, per_group, LANES).transpose(1, 2, 0, 3).reshape(groups, per_group * rows, LANES)
-
-    own_kv = jnp.concatenate([heads_of(new_keys), heads_of(new_values)], axis=1)
-    items, own_kv = lax.optimization_barrier((items, own_kv))
-    own_kv = lax.all_to_all(own_kv, "head", split_axis=0, concat_axis=0, tiled=True)
-
-    chunk = 256
+    pair = [
+        tensor.reshape(rows, groups, per_group, LANES).transpose(1, 2, 0, 3).reshape(groups, per_group * rows, LANES)
+        for tensor in (new_keys, new_values)
+    ]
+    items, pair = lax.optimization_barrier((items, jnp.concatenate(pair, axis=1)))
+    own_kv = lax.all_to_all(pair, "head", split_axis=0, concat_axis=0, tiled=True)
+
     slot_rows = SLOTS * block_rows
+    work = 2 * slot_rows * key_rows * LANES * per_group
+    ctx_keys, ctx_values = in_hbm(ctx_keys), in_hbm(ctx_values)
+    wide = pltpu.VMEM((slot_rows, 2 * LANES), BF16)
+    parts = pl.pallas_call(
+        query_kernel,
+        out_shape=jax.ShapeDtypeStruct((owners, SLOTS * 32, LANES), BF16),
+        in_specs=[vmem(), hbm, hbm],
+        out_specs=hbm,
+        scratch_shapes=[pltpu.VMEM((per_group, key_rows, LANES), BF16)] * 2
+        + [pltpu.VMEM((owners, SLOTS * 32, LANES), BF16), wide, wide]
+        + [pltpu.SemaphoreType.DMA((per_group, 2)), pltpu.SemaphoreType.DMA((per_group,))],
+        compiler_params=params(32),
+        cost_estimate=pl.CostEstimate(flops=8 * work, bytes_accessed=6 << 20, transcendentals=0),
+        name="query_parts",
+    )(items, ctx_keys, ctx_values)
+
+    parts, own_kv = lax.optimization_barrier((parts, own_kv))
+    returned = lax.all_to_all(parts, "seq", split_axis=0, concat_axis=0, tiled=True)
+
+    items_later, _ = lax.optimization_barrier((items, parts))
     context_spec = pl.BlockSpec((key_rows, LANES), lambda g: (0, g))
     items_spec = pl.BlockSpec((owners, SLOTS * 64 + 8, LANES), lambda g: (0, 0, 0))
-    work = 2 * slot_rows * key_rows * LANES * per_group
-    parts = pl.pallas_call(
-        functools.partial(query_kernel, chunk=chunk),
-        grid=(per_group,),
-        out_shape=jax.ShapeDtypeStruct((owners, SLOTS * 32, LANES), BF16),
-        in_specs=[items_spec, context_spec, context_spec],
-        out_specs=pl.BlockSpec((owners // per_group, SLOTS * 32, LANES), lambda g: (g, 0, 0)),
-        scratch_shapes=[
-            pltpu.VMEM((slot_rows, 2 * LANES), BF16),
-            pltpu.VMEM((slot_rows, 2 * LANES), BF16),
-            pltpu.VMEM((slot_rows, LANES), F32),
-        ],
-        compiler_params=params(),
-        cost_estimate=pl.CostEstimate(flops=5 * work, bytes_accessed=6 << 20, transcendentals=slot_rows * key_rows * per_group),
-        name="query_parts",
-    )(items, ctx_keys, ctx_values)
-
-    returned = lax.all_to_all(parts, "seq", split_axis=0, concat_axis=0, tiled=True)
-
-    items_later, own_kv, _ = lax.optimization_barrier((items, own_kv, parts))
     ctx_key_grad, ctx_value_grad = pl.pallas_call(
-        functools.partial(context_kernel, chunk=chunk),
+        functools.partial(context_kernel, chunk=256),
         grid=(per_group,),
         out_shape=(jax.ShapeDtypeStruct((key_rows, features), BF16),) * 2,
         in_specs=[items_spec, context_spec, context_spec],
         out_specs=(context_spec, context_spec),
-        scratch_shapes=[
-            pltpu.VMEM((slot_rows, 2 * LANES), BF16),
-            pltpu.VMEM((slot_rows, 2 * LANES), BF16),
-        ],
-        compiler_params=params(),
-        cost_estimate=pl.CostEstimate(flops=6 * work, bytes_accessed=10 << 20, transcendentals=slot_rows * key_rows * per_group),
+        scratch_shapes=[wide, wide],
+        compiler_params=params(24),
+        cost_estimate=pl.CostEstimate(flops=10 * work, bytes_accessed=10 << 20, transcendentals=0),
         name="context_grads",
     )(items_later, ctx_keys, ctx_values)
 
+    returned, ctx_key_grad, ctx_value_grad = lax.optimization_barrier((returned, ctx_key_grad, ctx_value_grad))
+    summed = pl.pallas_call(
+        pair_kernel,
+        out_shape=jax.ShapeDtypeStruct((owners, 32, LANES), BF16),
+        in_specs=[smem, smem, vmem()],
+        out_specs=vmem(),
+        compiler_params=params(),
+        name="pair_sum",
+    )(flat, slot_of * 32, returned)
+    home = lax.all_to_all(summed, "seq", split_axis=0, concat_axis=0, tiled=True)
+    own_kv, _ = lax.optimization_barrier((own_kv, summed))
     head_spec = pl.BlockSpec((block_rows, LANES), lambda g: (0, g))
-    whole = lambda shape: pl.BlockSpec(shape, lambda g: (0,) * len(shape))
     own_dq, new_key_grad, new_value_grad = pl.pallas_call(
         own_kernel,
         grid=(per_group,),
@@ -333,7 +392,11 @@
             jax.ShapeDtypeStruct((block_rows, features), BF16),
             jax.ShapeDtypeStruct((block_rows, features), BF16),
         ),
-        in_specs=[whole(window.shape), whole(own_kv.shape), pl.BlockSpec((1, groups, LANES), lambda g: (g, 0, 0))],
+        in_specs=[
+            pl.BlockSpec(window.shape, lambda g: (0, 0, 0)),
+            pl.BlockSpec(own_kv.shape, lambda g: (0, 0, 0)),
+            pl.BlockSpec((1, groups, LANES), lambda g: (g, 0, 0)),
+        ],
         out_specs=(head_spec, head_spec, head_spec),
         scratch_shapes=[pltpu.VMEM((block_rows, 2 * LANES), BF16)] * 4,
         compiler_params=params(),
@@ -341,21 +404,11 @@
         name="own_set",
     )(window, own_kv, lse_terms.reshape(per_group, groups, LANES))
 
-    summed = pl.pallas_call(
-        pair_kernel,
-        out_shape=jax.ShapeDtypeStruct((owners, 32, LANES), BF16),
-        in_specs=[smem, vmem()],
-        out_specs=vmem(),
-        compiler_params=params(),
-        name="pair_sum",
-    )(place, returned)
-    home = lax.all_to_all(summed, "seq", split_axis=0, concat_axis=0, tiled=True)
     query_grad = pl.pallas_call(
         finish_kernel,
-        grid=(per_group,),
         out_shape=jax.ShapeDtypeStruct((block_rows, features), BF16),
-        in_specs=[pl.BlockSpec((owners // per_group, 32, LANES), lambda g: (g, 0, 0)), head_spec],
-        out_specs=head_spec,
+        in_specs=[vmem()] * 2,
+        out_specs=vmem(),
         compiler_params=params(),
         name="finish",
     )(home, own_dq)

time: 191 us -> 163 us (0.85)
  blocking collectives: 14.7 us -> 0 us
  Pallas kernels: 54.1 us -> 40.4 us
  local copies, waits for them, and re-layouts: 11.8 us -> 1.75 us
  waiting for transfers between devices: 74.1 us -> 79.9 us
  starting transfers between devices: 32.8 us -> 37.2 us
    all_to_all x1 -> x0, blocking collectives: 14.7 us -> none  [per_device(): lax.all_to_all(head_out, 'head', split_axis=0, concat_axis=0, tiled=True)]
    pallas_call x4 -> x5, Pallas kernels: 45.9 us -> 33.3 us  [the longest x1 16.4 us: per_device(): pl.pallas_call(functools.partial(context_kernel, chunk=256), grid=(per_gr...]
    all_to_all x1, waiting for transfers between devices: 18.4 us -> 6.1 us  [per_device(): lax.all_to_all(parts, 'seq', split_axis=0, concat_axis=0, tiled=True)]
    all_to_all x1 -> x2, waiting for transfers between devices: 0.01 us -> 10.3 us  [the longest x1 10.3 us: per_device(): lax.all_to_all(head_out, 'head', split_axis=0, concat_axis=0, tiled=True)]
    unnamed x25 -> x11, local copies, waits for them, and re-layouts: 10.4 us -> 1.01 us
    all_to_all x1, waiting for transfers between devices: 0.01 us -> 8.27 us  [per_device(): lax.all_to_all(summed, 'seq', split_axis=0, concat_axis=0, tiled=True)]
    all_to_all x1 -> x2, starting transfers between devices: 3.49 us -> 7.81 us  [the longest x1 4.31 us: per_device(): lax.all_to_all(head_out, 'head', split_axis=0, concat_axis=0, tiled=True)]
  transfers between devices with their start and end apart: 5 -> 6, of which waited for: 3 -> 5; matrix products, arithmetic and copies ran while one was open for 1% -> 1% of each run, Pallas kernels for 25% -> 21%
where the time goes in v2:
time: 163 us; the launch traced here: 161 us
  waiting for transfers between devices  79.9 us (49%)
  Pallas kernels  40.4 us (25%)
  starting transfers between devices  37.2 us (23%)
  local copies, waits for them, and re-layouts  1.75 us (1%)
    all_to_all x1, waiting for transfers between devices, per_device(): lax.all_to_all(outgoing, 'seq', split_axis=0, concat_axis=0, tiled=True)  37.4 us
    all_to_all x1, waiting for transfers between devices, per_device(): lax.all_to_all(pieces, 'seq', split_axis=0, concat_axis=0, tiled=True)  17.8 us
    pallas_call x1, Pallas kernels, per_device(): pl.pallas_call(functools.partial(context_kernel, chunk=256), grid=(per_gr...  16.4 us
    pallas_call x1, Pallas kernels, per_device(): pl.pallas_call(query_kernel, out_shape=jax.ShapeDtypeStruct((owners, SLOT...  13.6 us
    all_to_all x1, starting transfers between devices, per_device(): lax.all_to_all(pieces, 'seq', split_axis=0, concat_axis=0, tiled=True)  11.4 us
    all_to_all x1, waiting for transfers between devices, per_device(): lax.all_to_all(head_out, 'head', split_axis=0, concat_axis=0, tiled=True)  10.3 us
    all_to_all x1, waiting for transfers between devices, per_device(): lax.all_to_all(summed, 'seq', split_axis=0, concat_axis=0, tiled=True)  8.27 us
    all_to_all x1, starting transfers between devices, per_device(): lax.all_to_all(parts, 'seq', split_axis=0, concat_axis=0, tiled=True)  6.46 us
  transfers between devices with their start and end apart: 6, of which 5 were waited for; matrix products, arithmetic and copies ran while one was open for 1% of the time, Pallas kernels for 21%

profile of v2, /device:TPU:32, one launch (start us, length us, event | category | flops | bytes accessed | tf_op | source)
XLA Modules:
  0.0 161.1 jit_solution(14057207010070154703)
XLA Ops:
  0.7 2.4 %prepare.1 = bf16[8,264,128]{2,1,0:T(8,128)(2,1)} custom-call(bf16[32,4096]{1,0:T(8,128)(2,1)} %q_hbm.1, bf16[32,4096]{1,0:T(8,128)(2,1)} %do_hbm.1, bf16[32,4096]{1,0:T(8,128)(2,1)} %o_hbm.1), custom_call_target="tpu_custom_call" | custom-call | tf_op jit(solution)/shard_map/prepare/pallas_call | solution.py:292
  3.1 4.3 %all-to-all-start = ((bf16[8,264,128]{2,1,0:T(8,128)(2,1)}), bf16[8,264,128]{2,1,0:T(8,128)(2,1)S(1)}, u32[]{:S(2)}, u32[]{:S(2)}) async-start(bf16[8,264,128]{2,1,0:T(8,128)(2,1)} %prepare.1), calls=%async_computation | async-start | bytes 1081344 | tf_op jit(solution)/shard_map/all_to_all | solution.py:309
  7.6 10.3 %all-to-all-done.h_ref = bf16[8,264,128]{2,1,0:T(8,128)(2,1)S(1)} async-done(((bf16[8,264,128]{2,1,0:T(8,128)(2,1)}), bf16[8,264,128]{2,1,0:T(8,128)(2,1)S(1)}, u32[]{:S(2)}, u32[]{:S(2)}) %all-to-all-start) | async-done | bytes 540704 | tf_op jit(solution)/shard_map/all_to_all | solution.py:309
  17.9 0.9 relay.1
  18.8 11.4 %all-to-all-start.1 = ((bf16[32,72,128]{2,1,0:T(8,128)(2,1)}), bf16[32,72,128]{2,1,0:T(8,128)(2,1)S(1)}, u32[]{:S(2)}, u32[]{:S(2)}) async-start(bf16[32,72,128]{2,1,0:T(8,128)(2,1)} %relay.1), calls=%async_computation.1 | async-start | bytes 1179648 | tf_op jit(solution)/shard_map/all_to_all | solution.py:319
  30.4 0.2 convert_reduce_fusion
  30.7 17.8 %all-to-all-done.1.in_ref = bf16[32,72,128]{2,1,0:T(8,128)(2,1)S(1)} async-done(((bf16[32,72,128]{2,1,0:T(8,128)(2,1)}), bf16[32,72,128]{2,1,0:T(8,128)(2,1)S(1)}, u32[]{:S(2)}, u32[]{:S(2)}) %all-to-all-start.1) | async-done | bytes 589856 | tf_op jit(solution)/shard_map/all_to_all | solution.py:319
  48.4 1.8 %gather.1 = bf16[32,200,128]{2,1,0:T(8,128)(2,1)} custom-call(s32[96]{0:T(128)S(1)} %select_reduce_fusion.src_ref, f32[1]{0:T(128)} %bitcast.fill_ref, bf16[32,72,128]{2,1,0:T(8,128)(2,1)S(1)} %all-to-all-done.1.in_ref), custom_call_target="tpu_custom_call" | custom-call | tf_op jit(solution)/shard_map/gather/pallas_call | solution.py:322
  50.3 5.5 %all-to-all-start.2 = ((bf16[32,200,128]{2,1,0:T(8,128)(2,1)}), bf16[32,200,128]{2,1,0:T(8,128)(2,1)S(1)}, u32[]{:S(2)}, u32[]{:S(2)}) async-start(bf16[32,200,128]{2,1,0:T(8,128)(2,1)} %gather.1), calls=%async_computation.2 | async-start | bytes 3276800 | tf_op jit(solution)/shard_map/all_to_all | solution.py:331
  55.7 0.2 reshape.60
  56.0 0.2 reshape.62
  56.3 0.8 pad_maximum_fusion
  57.2 37.4 %all-to-all-done.2.x_ref = bf16[32,200,128]{2,1,0:T(8,128)(2,1)S(1)} async-done(((bf16[32,200,128]{2,1,0:T(8,128)(2,1)}), bf16[32,200,128]{2,1,0:T(8,128)(2,1)S(1)}, u32[]{:S(2)}, u32[]{:S(2)}) %all-to-all-start.2) | async-done | bytes 1638432 | tf_op jit(solution)/shard_map/all_to_all | solution.py:331
  94.6 3.5 %all-to-all-start.3 = ((bf16[8,256,128]{2,1,0:T(8,128)(2,1)}), bf16[8,256,128]{2,1,0:T(8,128)(2,1)S(1)}, u32[]{:S(2)}, u32[]{:S(2)}) async-start(bf16[8,256,128]{2,1,0:T(8,128)(2,1)} %pad_maximum_fusion), calls=%async_computation.3 | async-start | bytes 1048576 | tf_op jit(solution)/shard_map/all_to_all | solution.py:338
  98.1 13.6 %query_parts.1 = bf16[32,96,128]{2,1,0:T(8,128)(2,1)S(1)} custom-call(bf16[32,200,128]{2,1,0:T(8,128)(2,1)S(1)} %all-to-all-done.2.x_ref, bf16[2048,512]{1,0:T(8,128)(2,1)} %k_ref.1, bf16[2048,512]{1,0:T(8,128)(2,1)} %v_ref.1), custom_call_target="tpu_custom_call" | custom-call | flops 12884901888 | bytes 6291456 | tf_op jit(solution)/shard_map/query_parts/pallas_call | solution.py:344
  111.6 0.9 copy-done
  112.5 6.5 %all-to-all-start.4 = ((bf16[32,96,128]{2,1,0:T(8,128)(2,1)}), bf16[32,96,128]{2,1,0:T(8,128)(2,1)S(1)}, u32[]{:S(2)}, u32[]{:S(2)}) async-start(bf16[32,96,128]{2,1,0:T(8,128)(2,1)} %copy-done), calls=%async_computation.4 | async-start | bytes 1572864 | tf_op jit(solution)/shard_map/all_to_all | solution.py:358
  119.0 16.4 %context_grads.1 = (bf16[2048,512]{1,0:T(8,128)(2,1)}, bf16[2048,512]{1,0:T(8,128)(2,1)}) custom-call(bf16[32,200,128]{2,1,0:T(8,128)(2,1)S(1)} %all-to-all-done.2.x_ref, bf16[2048,512]{1,0:T(8,128)(2,1)} %k_ref.1, bf16[2048,512]{1,0:T(8,128)(2,1)} %v_ref.1), custom_call_target="tpu_custom_call" | custom-call | flops 16106127360 | bytes 10485760 | tf_op jit(solution)/shard_map/context_grads/pallas_call | solution.py:363
  135.4 6.1 %all-to-all-done.4.in_ref = bf16[32,96,128]{2,1,0:T(8,128)(2,1)S(1)} async-done(((bf16[32,96,128]{2,1,0:T(8,128)(2,1)}), bf16[32,96,128]{2,1,0:T(8,128)(2,1)S(1)}, u32[]{:S(2)}, u32[]{:S(2)}) %all-to-all-start.4) | async-done | bytes 786464 | tf_op jit(solution)/shard_map/all_to_all | solution.py:358
  141.5 1.4 pair_sum.1
  143.0 6.1 %all-to-all-start.5 = ((bf16[32,32,128]{2,1,0:T(8,128)(2,1)}), bf16[32,32,128]{2,1,0:T(8,128)(2,1)S(1)}, u32[]{:S(2)}, u32[]{:S(2)}) async-start(bf16[32,32,128]{2,1,0:T(8,128)(2,1)} %pair_sum.1), calls=%async_computation.5 | async-start | bytes 524288 | tf_op jit(solution)/shard_map/all_to_all | solution.py:384
  149.1 3.0 %own_set.1 = (f32[256,512]{1,0:T(8,128)S(1)}, bf16[256,512]{1,0:T(8,128)(2,1)}, bf16[256,512]{1,0:T(8,128)(2,1)}) custom-call(bf16[8,264,128]{2,1,0:T(8,128)(2,1)S(1)} %all-to-all-done.h_ref, bf16[8,256,128]{2,1,0:T(8,128)(2,1)S(1)} %all-to-all-done.3.kv_ref, bf16[4,8,128]{2,1,0:T(8,128)(2,1)S(1)} %bitcast.8), custom_call_target="tpu_custom_call" | custom-call | flops 335544320 | bytes 2097152 | tf_op jit(solution)/shard_map/own_set/pallas_call | solution.py:387
  152.1 8.3 %all-to-all-done.5.in_ref = bf16[32,32,128]{2,1,0:T(8,128)(2,1)S(1)} async-done(((bf16[32,32,128]{2,1,0:T(8,128)(2,1)}), bf16[32,32,128]{2,1,0:T(8,128)(2,1)S(1)}, u32[]{:S(2)}, u32[]{:S(2)}) %all-to-all-start.5) | async-done | bytes 262176 | tf_op jit(solution)/shard_map/all_to_all | solution.py:384
  160.4 0.8 finish.1
  (19 shorter events, 0.7 us)
Async XLA Ops:
  0.6 6.8 %copy-start.3 = (f32[4,256]{1,0:T(4,128)S(1)}, f32[4,256]{1,0:T(4,128)}, u32[]{:S(2)}) copy-start(f32[4,256]{1,0:T(4,128)} %param.14) | copy-start | bytes 12292
  0.6 29.5 %copy-start.4 = (s32[32,2]{0,1:T(2,128)S(1)}, s32[32,2]{0,1:T(2,128)}, u32[]{:S(2)}) copy-start(s32[32,2]{0,1:T(2,128)} %param.17) | copy-start | bytes 772
  3.1 14.8 %all-to-all-start = ((bf16[8,264,128]{2,1,0:T(8,128)(2,1)}), bf16[8,264,128]{2,1,0:T(8,128)(2,1)S(1)}, u32[]{:S(2)}, u32[]{:S(2)}) async-start(bf16[8,264,128]{2,1,0:T(8,128)(2,1)} %prepare.1), calls=%async_computation | async-start | bytes 1081344 | tf_op jit(solution)/shard_map/all_to_all | solution.py:309
  18.8 29.7 %all-to-all-start.1 = ((bf16[32,72,128]{2,1,0:T(8,128)(2,1)}), bf16[32,72,128]{2,1,0:T(8,128)(2,1)S(1)}, u32[]{:S(2)}, u32[]{:S(2)}) async-start(bf16[32,72,128]{2,1,0:T(8,128)(2,1)} %relay.1), calls=%async_computation.1 | async-start | bytes 1179648 | tf_op jit(solution)/shard_map/all_to_all | solution.py:319
  50.2 5.5 %copy-start.1 = (bf16[32,4096]{1,0:T(8,128)(2,1)S(1)}, bf16[32,4096]{1,0:T(8,128)(2,1)}, u32[]{:S(2)}) copy-start(bf16[32,4096]{1,0:T(8,128)(2,1)} %param.10) | copy-start | bytes 786436
  50.3 5.8 %copy-start.2 = (bf16[32,4096]{1,0:T(8,128)(2,1)S(1)}, bf16[32,4096]{1,0:T(8,128)(2,1)}, u32[]{:S(2)}) copy-start(bf16[32,4096]{1,0:T(8,128)(2,1)} %param.11) | copy-start | bytes 786436
  50.3 44.3 %all-to-all-start.2 = ((bf16[32,200,128]{2,1,0:T(8,128)(2,1)}), bf16[32,200,128]{2,1,0:T(8,128)(2,1)S(1)}, u32[]{:S(2)}, u32[]{:S(2)}) async-start(bf16[32,200,128]{2,1,0:T(8,128)(2,1)} %gather.1), calls=%async_computation.2 | async-start | bytes 3276800 | tf_op jit(solution)/shard_map/all_to_all | solution.py:331
  94.6 18.0 %all-to-all-start.3 = ((bf16[8,256,128]{2,1,0:T(8,128)(2,1)}), bf16[8,256,128]{2,1,0:T(8,128)(2,1)S(1)}, u32[]{:S(2)}, u32[]{:S(2)}) async-start(bf16[8,256,128]{2,1,0:T(8,128)(2,1)} %pad_maximum_fusion), calls=%async_computation.3 | async-start | bytes 1048576 | tf_op jit(solution)/shard_map/all_to_all | solution.py:338
  111.6 0.9 copy-start
  112.5 29.0 %all-to-all-start.4 = ((bf16[32,96,128]{2,1,0:T(8,128)(2,1)}), bf16[32,96,128]{2,1,0:T(8,128)(2,1)S(1)}, u32[]{:S(2)}, u32[]{:S(2)}) async-start(bf16[32,96,128]{2,1,0:T(8,128)(2,1)} %copy-done), calls=%async_computation.4 | async-start | bytes 1572864 | tf_op jit(solution)/shard_map/all_to_all | solution.py:358
  143.0 17.4 %all-to-all-start.5 = ((bf16[32,32,128]{2,1,0:T(8,128)(2,1)}), bf16[32,32,128]{2,1,0:T(8,128)(2,1)S(1)}, u32[]{:S(2)}, u32[]{:S(2)}) async-start(bf16[32,32,128]{2,1,0:T(8,128)(2,1)} %pair_sum.1), calls=%async_computation.5 | async-start | bytes 524288 | tf_op jit(solution)/shard_map/all_to_all | solution.py:384

commit v3 on v2

v3 whole, which is shorter than its diff:
```python
import functools
import math

import jax
import jax.numpy as jnp
from jax import lax
from jax.experimental import pallas as pl
from jax.experimental.pallas import tpu as pltpu
from jax.sharding import PartitionSpec as P

BF16 = jnp.bfloat16
F32 = jnp.float32
LANES = 128
MIB = 1024 * 1024
SLOTS = 3
NT = (((1,), (1,)), ((), ()))
TN = (((0,), (0,)), ((), ()))
FILL = 1e5


def dot(lhs, rhs, dims=(((1,), (0,)), ((), ()))):
    return lax.dot_general(lhs, rhs, dims, preferred_element_type=F32)


def vmem():
    return pl.BlockSpec(memory_space=pltpu.VMEM)


def in_hbm(array):
    return pltpu.with_memory_space_constraint(array, pltpu.HBM)


def params(mib=8):
    return pltpu.CompilerParams(vmem_limit_bytes=mib * MIB)


def spread(values, term):
    high = values.astype(BF16)
    low = (values - high.astype(F32)).astype(BF16)
    shape = (values.shape[1], LANES)
    at = lax.broadcasted_iota(jnp.int32, shape, 0) * 4 + term
    lane = lax.broadcasted_iota(jnp.int32, shape, 1)
    out = dot(high, jnp.where(lane == at, 1.0, 0.0).astype(BF16))
    return out + dot(low, jnp.where(lane == at + 1, 1.0, 0.0).astype(BF16))


def statistics_kernel(lse_ref, dots_ref, out_ref):
    out_ref[...] = (spread(lse_ref[...] * math.sqrt(LANES), 0) + spread(dots_ref[...], 2)).astype(BF16)


def prepare_kernel(q_hbm, do_hbm, o_hbm, out_hbm, dots_ref, q_ref, do_ref, o_ref, out_ref, sems, out_sems):
    copies = [
        pltpu.make_async_copy(src, dst, sems.at[n])
        for n, (src, dst) in enumerate(((q_hbm, q_ref), (do_hbm, do_ref), (o_hbm, o_ref)))
    ]
    for copy in copies:
        copy.start()
    rows, features = q_ref.shape
    heads = features // LANES
    groups, _, _ = dots_ref.shape
    per_group = heads // groups
    octets = rows // 8
    leaving = []
    for a, ref in enumerate((q_ref, do_ref)):
        copies[a].wait()
        for g in range(per_group):
            for o in range(octets):
                for h in range(groups):
                    c = (h * per_group + g) * LANES
                    out_ref[((a * per_group + g) * octets + o) * groups + h] = ref[o * 8 : o * 8 + 8, c : c + LANES]
        half = pl.ds(a * per_group * octets * groups, per_group * octets * groups)
        leaving.append(pltpu.make_async_copy(out_ref.at[half], out_hbm.at[half], out_sems.at[a]))
        leaving[a].start()
    copies[2].wait()
    product = do_ref[...].astype(F32) * o_ref[...].astype(F32)
    high = product.astype(BF16)
    low = (product - high.astype(F32)).astype(BF16)
    head_at = lax.broadcasted_iota(jnp.int32, (heads, features), 0)
    lane = lax.broadcasted_iota(jnp.int32, (heads, features), 1)
    pick = jnp.where((lane >= head_at * LANES) & (lane < head_at * LANES + LANES), 1.0, 0.0).astype(BF16)
    dots = dot(pick, high, NT) + dot(pick, low, NT)
    for h in range(groups):
        dots_ref[h] = dots[h * per_group : (h + 1) * per_group]
    for copy in leaving:
        copy.wait()


def gather_kernel(src_ref, in_ref, stats_ref, out_hbm, out_ref, sems):
    owners = out_ref.shape[0]
    count = 4

    def leave(part):
        at = pl.ds(part * count, count)
        return pltpu.make_async_copy(out_ref.at[at], out_hbm.at[at], sems.at[part])

    def body(part, carry):
        stats = stats_ref[...]
        for k in range(count):
            j = part * count + k
            for slot in range(SLOTS):
                at = jnp.maximum(src_ref[j * SLOTS + slot], 0)
                out_ref[j, slot * 64 : (slot + 1) * 64, :] = in_ref[at]
            out_ref[j, SLOTS * 64 :, :] = stats
        leave(part).start()
        return carry

    lax.fori_loop(0, owners // count, body, 0)
    for part in range(owners // count):
        leave(part).wait()


def load_statistics(src_ref, x_ref, stats_ref):
    lane = lax.broadcasted_iota(jnp.int32, (32, LANES), 1)
    is_lse = lane % 4 < 2
    for slot in range(SLOTS):
        src = src_ref[slot]
        tile = x_ref[jnp.maximum(src, 0), SLOTS * 64 :, :].astype(F32)
        stats_ref[slot] = jnp.where(is_lse & (src < 0), FILL, tile)


def assemble(x_ref, stats_ref, head, qx, dx):
    row = lax.broadcasted_iota(jnp.int32, (32, LANES), 0)
    lane = lax.broadcasted_iota(jnp.int32, (32, LANES), 1)
    for slot in range(SLOTS):
        stats = stats_ref[slot, pl.ds(pl.multiple_of(head * 8, 8), 8), :]
        for a, out in ((0, qx), (1, dx)):
            first = row * 4 + 2 * a
            mask = (lane == first) | (lane == first + 1)
            for u in range(4):
                base = slot * 256 + u * 64
                out[base : base + 64, 0:LANES] = x_ref[a * 16 + head * 4 + u, slot * 64 : (slot + 1) * 64, :]
            for e in range(8):
                base = slot * 256 + e * 32
                out[base : base + 32, LANES:] = jnp.where(mask, stats[e : e + 1], 0.0).astype(BF16)


def extend(block):
    return jnp.concatenate([block, jnp.full((block.shape[0], LANES), -1.0, BF16)], axis=1)


SCALE = LANES**-0.5
EXP_SCALE = SCALE * math.log2(math.e)


def query_kernel(src_ref, x_ref, k_hbm, v_hbm, out_hbm, k_ref, v_ref, out_ref, qx, dx, stats, sems, out_sems):
    per_group = k_ref.shape[0]

    def fetch(head, which):
        src, dst = ((k_hbm, k_ref), (v_hbm, v_ref))[which]
        at = pl.ds(pl.multiple_of(head * LANES, LANES), LANES)
        return pltpu.make_async_copy(src.at[:, at], dst.at[head], sems.at[head, which])

    def leave(head):
        at = pl.ds(head * 8, 8)
        return pltpu.make_async_copy(out_ref.at[at], out_hbm.at[at], out_sems.at[head])

    for head in range(per_group):
        fetch(head, 0).start()
        fetch(head, 1).start()
    load_statistics(src_ref, x_ref, stats)

    def body(head, carry):
        assemble(x_ref, stats, head, qx, dx)
        fetch(head, 0).wait()
        fetch(head, 1).wait()
        keys = k_ref[head]
        keys_ext = extend(keys)
        values_ext = extend(v_ref[head])
        for slot in range(SLOTS):
            at = slice(slot * 256, slot * 256 + 256)
            weights = jnp.exp2(dot(qx[at], keys_ext, NT) * EXP_SCALE)
            dscores = (weights * dot(dx[at], values_ext, NT)).astype(BF16)
            part = (dot(dscores, keys) * SCALE).astype(BF16)
            for e in range(8):
                out_ref[head * 8 + e, slot * 32 : (slot + 1) * 32, :] = part[e * 32 : (e + 1) * 32]
        leave(head).start()
        return carry

    lax.fori_loop(0, per_group, body, 0)
    for head in range(per_group):
        leave(head).wait()


def context_kernel(src_ref, x_ref, k_ref, v_ref, dk_ref, dv_ref, qx, dx, stats, *, chunk):
    load_statistics(src_ref, x_ref, stats)
    assemble(x_ref, stats, pl.program_id(0), qx, dx)

    def body(i, carry):
        at = pl.ds(pl.multiple_of(i * chunk, chunk), chunk)
        weights = jnp.exp2(dot(extend(k_ref[at, :]), qx[...], NT) * EXP_SCALE)
        dscores = (weights * dot(extend(v_ref[at, :]), dx[...], NT)).astype(BF16)
        dv_ref[at, :] = dot(weights.astype(BF16), dx[:, 0:LANES]).astype(BF16)
        dk_ref[at, :] = (dot(dscores, qx[:, 0:LANES]) * SCALE).astype(BF16)
        return carry

    lax.fori_loop(0, k_ref.shape[0] // chunk, body, 0, unroll=True)


def own_kernel(me_ref, w_ref, stats_ref, dq_ref, dk_ref, dv_ref, qx, dx, kx, vx):
    head = pl.program_id(0)
    groups = w_ref.shape[0]
    row = lax.broadcasted_iota(jnp.int32, (8, LANES), 0)
    lane = lax.broadcasted_iota(jnp.int32, (8, LANES), 1)
    stats = stats_ref[0].astype(F32)
    kx[:, LANES:] = jnp.full((kx.shape[0], LANES), -1.0, BF16)
    vx[:, LANES:] = jnp.full((kx.shape[0], LANES), -1.0, BF16)
    for src in range(groups):
        at = slice(src * 32, src * 32 + 32)
        for n, ref in enumerate((qx, dx, kx, vx)):
            piece = pl.ds(pl.multiple_of(n * 128 + head * 32, 32), 32)
            ref[at, 0:LANES] = w_ref[me_ref[0] ^ src, piece, :]
        for a, ref in ((0, qx), (1, dx)):
            first = ((src % 4) * 8 + row) * 4 + 2 * a
            mask = (lane == first) | (lane == first + 1)
            e = src // 4
            terms = [jnp.where(mask, stats[o * 2 + e : o * 2 + e + 1], 0.0) for o in range(4)]
            ref[at, LANES:] = jnp.concatenate(terms, axis=0).astype(BF16)
    shape = (qx.shape[0], kx.shape[0])
    allowed = lax.broadcasted_iota(jnp.int32, shape, 0) >= lax.broadcasted_iota(jnp.int32, shape, 1)
    weights = jnp.where(allowed, jnp.exp2(dot(qx[...], kx[...], NT) * EXP_SCALE), 0.0)
    dscores = (weights * dot(dx[...], vx[...], NT)).astype(BF16)
    dq_ref[...] = dot(dscores, kx[:, 0:LANES]) * SCALE
    dk_ref[...] = (dot(dscores, qx[:, 0:LANES], TN) * SCALE).astype(BF16)
    dv_ref[...] = dot(weights.astype(BF16), dx[:, 0:LANES], TN).astype(BF16)


def pair_kernel(owner_ref, row_ref, in_ref, out_ref):
    def body(b, carry):
        total = None
        for s in range(2):
            row = pl.multiple_of(row_ref[b * 2 + s], 32)
            value = in_ref[owner_ref[b * 2 + s], pl.ds(row, 32), :].astype(F32)
            total = value if total is None else total + value
        out_ref[b] = total.astype(BF16)
        return carry

    lax.fori_loop(0, out_ref.shape[0], body, 0, unroll=4)


def finish_kernel(in_ref, own_ref, out_ref):
    for g in range(4):
        at = slice(g * LANES, (g + 1) * LANES)
        parts = [in_ref[g * 8 + e].astype(F32) for e in range(8)]
        for h in range(8):
            octet = slice((h % 4) * 8, (h % 4) * 8 + 8)
            block = jnp.concatenate([parts[o * 2 + h // 4][octet] for o in range(4)], axis=0)
            rows = slice(h * 32, h * 32 + 32)
            out_ref[rows, at] = (block + own_ref[rows, at]).astype(BF16)


def per_device(queries, new_keys, new_values, attn_out, out_grad, logsumexp, ctx_keys, ctx_values, selected):
    owners = lax.axis_size("seq")
    groups = lax.axis_size("head")
    per_group, block_rows = logsumexp.shape
    rows = queries.shape[0]
    key_rows, features = ctx_keys.shape
    relay = lax.axis_index("seq")

    flat = selected.reshape(-1)
    order = jnp.arange(flat.shape[0])
    same = flat[:, None] == flat[None, :]
    slot_of = jnp.sum(same & (order[None, :] < order[:, None]), axis=1).astype(jnp.int32)
    place = flat * SLOTS + slot_of
    hit = place[None, :] == jnp.arange(owners * SLOTS)[:, None]
    source = jnp.max(jnp.where(hit, (order // selected.shape[1])[None, :], -1), axis=1).astype(jnp.int32)
    mine = lax.dynamic_slice(source, (relay * SLOTS,), (SLOTS,))
    me = lax.axis_index("head").astype(jnp.int32)

    def swap(tensor):
        parts = [lax.dynamic_index_in_dim(tensor, me, 0, keepdims=False)]
        for k in range(1, groups):
            part = lax.dynamic_index_in_dim(tensor, me ^ k, 0, keepdims=False)
            parts.append(lax.ppermute(part, "head", [(i, i ^ k) for i in range(groups)]))
        return parts

    hbm = pl.BlockSpec(memory_space=pltpu.HBM)
    smem = pl.BlockSpec(memory_space=pltpu.SMEM)
    tiles = owners * groups
    pieces, dots = pl.pallas_call(
        prepare_kernel,
        out_shape=(
            jax.ShapeDtypeStruct((tiles, 8, LANES), BF16),
            jax.ShapeDtypeStruct((groups, per_group, rows), F32),
        ),
        in_specs=[hbm] * 3,
        out_specs=(hbm, vmem()),
        scratch_shapes=[pltpu.VMEM(queries.shape, BF16)] * 3
        + [pltpu.VMEM((tiles, 8, LANES), BF16), pltpu.SemaphoreType.DMA((3,)), pltpu.SemaphoreType.DMA((2,))],
        compiler_params=params(),
        name="prepare",
    )(in_hbm(queries), in_hbm(out_grad), in_hbm(attn_out))
    held = lax.all_to_all(pieces, ("seq", "head"), split_axis=0, concat_axis=0, tiled=True)
    held = held.reshape(owners, 64, LANES)

    dots = jnp.take(jnp.stack(swap(dots)), me ^ jnp.arange(groups), axis=0)
    dots = dots.reshape(2, 4, per_group, 4, 8).transpose(2, 3, 0, 1, 4).reshape(32, 32)
    lse = logsumexp.reshape(per_group, 2, 4, 4, 8).transpose(0, 3, 1, 2, 4).reshape(32, 32)
    stats = pl.pallas_call(
        statistics_kernel,
        out_shape=jax.ShapeDtypeStruct((32, LANES), BF16),
        in_specs=[vmem()] * 2,
        out_specs=vmem(),
        compiler_params=params(),
        name="statistics",
    )(lse, dots)

    item_rows = SLOTS * 64 + 32
    outgoing = pl.pallas_call(
        gather_kernel,
        out_shape=jax.ShapeDtypeStruct((owners, item_rows, LANES), BF16),
        in_specs=[smem, vmem(), vmem()],
        out_specs=hbm,
        scratch_shapes=[pltpu.VMEM((owners, item_rows, LANES), BF16), pltpu.SemaphoreType.DMA((8,))],
        compiler_params=params(),
        name="gather",
    )(source, held, stats)

    window = [
        tensor.reshape(rows, groups, per_group, LANES).transpose(1, 2, 0, 3).reshape(groups, per_group * rows, LANES)
        for tensor in (queries, out_grad, new_keys, new_values)
    ]
    outgoing, window = lax.optimization_barrier((outgoing, jnp.concatenate(window, axis=1)))
    items = lax.all_to_all(outgoing, "seq", split_axis=0, concat_axis=0, tiled=True)
    window = swap(window)

    slot_rows = SLOTS * block_rows
    work = 2 * slot_rows * key_rows * LANES * per_group
    ctx_keys, ctx_values = in_hbm(ctx_keys), in_hbm(ctx_values)
    wide = pltpu.VMEM((slot_rows, 2 * LANES), BF16)
    slot_stats = pltpu.VMEM((SLOTS, 32, LANES), F32)
    parts = pl.pallas_call(
        query_kernel,
        out_shape=jax.ShapeDtypeStruct((owners, SLOTS * 32, LANES), BF16),
        in_specs=[smem, vmem(), hbm, hbm],
        out_specs=hbm,
        scratch_shapes=[pltpu.VMEM((per_group, key_rows, LANES), BF16)] * 2
        + [pltpu.VMEM((owners, SLOTS * 32, LANES), BF16), wide, wide, slot_stats]
        + [pltpu.SemaphoreType.DMA((per_group, 2)), pltpu.SemaphoreType.DMA((per_group,))],
        compiler_params=params(32),
        cost_estimate=pl.CostEstimate(flops=8 * work, bytes_accessed=6 << 20, transcendentals=0),
        name="query_parts",
    )(mine, items, ctx_keys, ctx_values)

    returned = lax.all_to_all(parts, "seq", split_axis=0, concat_axis=0, tiled=True)

    items_later, _ = lax.optimization_barrier((items, parts))
    context_spec = pl.BlockSpec((key_rows, LANES), lambda g: (0, g))
    items_spec = pl.BlockSpec((owners, item_rows, LANES), lambda g: (0, 0, 0))
    ctx_key_grad, ctx_value_grad = pl.pallas_call(
        functools.partial(context_kernel, chunk=256),
        grid=(per_group,),
        out_shape=(jax.ShapeDtypeStruct((key_rows, features), BF16),) * 2,
        in_specs=[smem, items_spec, context_spec, context_spec],
        out_specs=(context_spec, context_spec),
        scratch_shapes=[wide, wide, slot_stats],
        compiler_params=params(24),
        cost_estimate=pl.CostEstimate(flops=10 * work, bytes_accessed=10 << 20, transcendentals=0),
        name="context_grads",
    )(mine, items_later, ctx_keys, ctx_values)

    returned, ctx_key_grad, ctx_value_grad = lax.optimization_barrier((returned, ctx_key_grad, ctx_value_grad))
    summed = pl.pallas_call(
        pair_kernel,
        out_shape=jax.ShapeDtypeStruct((owners, 32, LANES), BF16),
        in_specs=[smem, smem, vmem()],
        out_specs=vmem(),
        compiler_params=params(),
        name="pair_sum",
    )(flat, slot_of * 32, returned)
    home = lax.all_to_all(summed, "seq", split_axis=0, concat_axis=0, tiled=True)
    window, _ = lax.optimization_barrier((jnp.stack(window), summed))
    head_spec = pl.BlockSpec((block_rows, LANES), lambda g: (0, g))
    own_dq, new_key_grad, new_value_grad = pl.pallas_call(
        own_kernel,
        grid=(per_group,),
        out_shape=(
            jax.ShapeDtypeStruct((block_rows, features), F32),
            jax.ShapeDtypeStruct((block_rows, features), BF16),
            jax.ShapeDtypeStruct((block_rows, features), BF16),
        ),
        in_specs=[
            smem,
            pl.BlockSpec(window.shape, lambda g: (0, 0, 0)),
            pl.BlockSpec((1, groups, LANES), lambda g: (g, 0, 0)),
        ],
        out_specs=(head_spec, head_spec, head_spec),
        scratch_shapes=[pltpu.VMEM((block_rows, 2 * LANES), BF16)] * 4,
        compiler_params=params(),
        cost_estimate=pl.CostEstimate(flops=10 * block_rows * block_rows * features, bytes_accessed=2 << 20, transcendentals=0),
        name="own_set",
    )(me.reshape(1), window, stats.reshape(per_group, groups, LANES))

    query_grad = pl.pallas_call(
        finish_kernel,
        out_shape=jax.ShapeDtypeStruct((block_rows, features), BF16),
        in_specs=[vmem()] * 2,
        out_specs=vmem(),
        compiler_params=params(),
        name="finish",
    )(home, own_dq)
    return (query_grad, new_key_grad, new_value_grad, ctx_key_grad, ctx_value_grad)


def solution(mesh):
    in_specs = (
        P(("seq", "head"), None),
        P(("seq", "head"), None),
        P(("seq", "head"), None),
        P(("seq", "head"), None),
        P(("seq", "head"), None),
        P("head", "seq"),
        P("seq", "head"),
        P("seq", "head"),
        P(),
    )
    out_specs = (P("seq", "head"),) * 5
    return jax.shard_map(per_device, mesh=mesh, in_specs=in_specs, out_specs=out_specs, check_vma=False)
```

time: 163 us -> 154 us (0.945)
  waiting for transfers between devices: 79.9 us -> 47.2 us
  starting transfers between devices: 37.2 us -> 49.7 us
  local copies, waits for them, and re-layouts: 1.75 us -> 13 us
    all_to_all x3 -> x1, waiting for transfers between devices: 28.1 us -> 2.49 us  [per_device(): lax.all_to_all(pieces, ('seq', 'head'), split_axis=0, concat_axis=0, tile...]
    ppermute x0 -> x14, waiting for transfers between devices: none -> 20.5 us  [swap(): lax.ppermute(part, 'head', [(i, i ^ k) for i in range(groups)])]
    all_to_all x1, waiting for transfers between devices: 37.4 us -> 19.3 us  [per_device(): lax.all_to_all(outgoing, 'seq', split_axis=0, concat_axis=0, tiled=True)]
    ppermute x0 -> x14, starting transfers between devices: none -> 13.8 us  [swap(): lax.ppermute(part, 'head', [(i, i ^ k) for i in range(groups)])]
    all_to_all x1, waiting for transfers between devices: 8.27 us -> 1.84 us  [per_device(): lax.all_to_all(summed, 'seq', split_axis=0, concat_axis=0, tiled=True)]
    unnamed x11 -> x29, local copies, waits for them, and re-layouts: 1.01 us -> 7.04 us
    all_to_all x3 -> x1, starting transfers between devices: 19.2 us -> 14.4 us  [per_device(): lax.all_to_all(pieces, ('seq', 'head'), split_axis=0, concat_axis=0, tile...]
    all_to_all x1, waiting for transfers between devices: 6.1 us -> 3.02 us  [per_device(): lax.all_to_all(parts, 'seq', split_axis=0, concat_axis=0, tiled=True)]
  transfers between devices with their start and end apart: 6 -> 18, of which waited for: 5 -> 8; matrix products, arithmetic and copies ran while one was open for 1% -> 9% of each run, Pallas kernels for 21% -> 23%
where the time goes in v3:
time: 154 us; the launch traced here: 152 us
  starting transfers between devices  49.7 us (32%)
  waiting for transfers between devices  47.2 us (31%)
  Pallas kernels  39.7 us (26%)
  local copies, waits for them, and re-layouts  13 us (8%)
    ppermute x14, waiting for transfers between devices, swap(): lax.ppermute(part, 'head', [(i, i ^ k) for i in range(groups)])  20.5 us
    all_to_all x1, waiting for transfers between devices, per_device(): lax.all_to_all(outgoing, 'seq', split_axis=0, concat_axis=0, tiled=True)  19.3 us
    pallas_call x1, Pallas kernels, per_device(): pl.pallas_call(functools.partial(context_kernel, chunk=256), grid=(per_gr...  16.5 us
    all_to_all x1, starting transfers between devices, per_device(): lax.all_to_all(pieces, ('seq', 'head'), split_axis=0, concat_axis=0, tile...  14.4 us
    pallas_call x1, Pallas kernels, per_device(): pl.pallas_call(query_kernel, out_shape=jax.ShapeDtypeStruct((owners, SLOT...  14.1 us
    ppermute x14, starting transfers between devices, swap(): lax.ppermute(part, 'head', [(i, i ^ k) for i in range(groups)])  13.8 us
    all_to_all x1, starting transfers between devices, per_device(): lax.all_to_all(outgoing, 'seq', split_axis=0, concat_axis=0, tiled=True)  8.23 us
    unnamed x29, local copies, waits for them, and re-layouts  7.04 us
  transfers between devices with their start and end apart: 18, of which 8 were waited for; matrix products, arithmetic and copies ran while one was open for 9% of the time, Pallas kernels for 23%

profile of v3, /device:TPU:32, one launch (start us, length us, event | category | flops | bytes accessed | tf_op | source)
XLA Modules:
  0.0 152.1 jit_solution(6512512576163874224)
XLA Ops:
  0.7 1.9 %prepare.1 = (bf16[256,8,128]{2,1,0:T(8,128)(2,1)}, f32[8,4,32]{2,1,0:T(4,128)S(1)}) custom-call(bf16[32,4096]{1,0:T(8,128)(2,1)} %q_hbm.1, bf16[32,4096]{1,0:T(8,128)(2,1)} %do_hbm.1, bf16[32,4096]{1,0:T(8,128)(2,1)} %o_hbm.1), custom_call_target="tpu_custom_call" | custom-call | tf_op jit(solution)/shard_map/prepare/pallas_call | solution.py:279
  2.6 14.4 %all-to-all-start = ((bf16[256,8,128]{2,1,0:T(8,128)(2,1)}), bf16[256,8,128]{2,1,0:T(8,128)(2,1)S(1)}, u32[]{:S(2)}, u32[]{:S(2)}) async-start(bf16[256,8,128]{2,1,0:T(8,128)(2,1)} %get-tuple-element.19), calls=%async_computation | async-start | bytes 1048576 | tf_op jit(solution)/shard_map/all_to_all | solution.py:292
  17.1 2.6 %collective-permute-start.6 = (f32[4,32]{1,0:T(4,128)S(1)}, f32[4,32]{1,0:T(4,128)S(1)}, u32[]{:S(2)}, u32[]{:S(2)}) collective-permute-start(f32[4,32]{1,0:T(4,128)S(1)} %get-tuple-element.41), channel_id=1, source_target_pairs={{0,7},{1,6},{2,5},{3,4},{4,3},{5,2},{6,1},{7,0},{8,15},{9,14},{10,... | collective-permute-start | bytes 1544 | tf_op jit(solution)/shard_map/ppermute | solution.py:273
  21.6 1.7 %collective-permute-start.3 = (f32[4,32]{1,0:T(4,128)S(1)}, f32[4,32]{1,0:T(4,128)S(1)}, u32[]{:S(2)}, u32[]{:S(2)}) collective-permute-start(f32[4,32]{1,0:T(4,128)S(1)} %get-tuple-element.44), channel_id=1, source_target_pairs={{0,4},{1,5},{2,6},{3,7},{4,0},{5,1},{6,2},{7,3},{8,12},{9,13},{10,... | collective-permute-start | bytes 1544 | tf_op jit(solution)/shard_map/ppermute | solution.py:273
  27.0 3.2 %collective-permute-done.1 = f32[4,32]{1,0:T(4,128)S(1)} collective-permute-done((f32[4,32]{1,0:T(4,128)S(1)}, f32[4,32]{1,0:T(4,128)S(1)}, u32[]{:S(2)}, u32[]{:S(2)}) %collective-permute-start.1) | collective-permute-done | bytes 544 | tf_op jit(solution)/shard_map/ppermute | solution.py:273
  30.3 3.0 %collective-permute-done.2 = f32[4,32]{1,0:T(4,128)S(1)} collective-permute-done((f32[4,32]{1,0:T(4,128)S(1)}, f32[4,32]{1,0:T(4,128)S(1)}, u32[]{:S(2)}, u32[]{:S(2)}) %collective-permute-start.2) | collective-permute-done | bytes 544 | tf_op jit(solution)/shard_map/ppermute | solution.py:273
  34.3 2.5 %all-to-all-done = bf16[256,8,128]{2,1,0:T(8,128)(2,1)S(1)} async-done(((bf16[256,8,128]{2,1,0:T(8,128)(2,1)}), bf16[256,8,128]{2,1,0:T(8,128)(2,1)S(1)}, u32[]{:S(2)}, u32[]{:S(2)}) %all-to-all-start) | async-done | bytes 524320 | tf_op jit(solution)/shard_map/all_to_all | solution.py:292
  36.8 1.8 %gather.11 = bf16[32,224,128]{2,1,0:T(8,128)(2,1)} custom-call(s32[96]{0:T(128)S(1)} %select_reduce_fusion.src_ref, bf16[32,64,128]{2,1,0:T(8,128)(2,1)S(1)} %bitcast.78, bf16[32,128]{1,0:T(8,128)(2,1)S(1)} %statistics.1.stats_ref), custom_call_target="tpu_custom_call" | custom-call | tf_op jit(solution)/shard_map/gather/pallas_call | solution.py:308
  38.7 8.2 %all-to-all-start.1 = ((bf16[32,224,128]{2,1,0:T(8,128)(2,1)}), bf16[32,224,128]{2,1,0:T(8,128)(2,1)S(1)}, u32[]{:S(2)}, u32[]{:S(2)}) async-start(bf16[32,224,128]{2,1,0:T(8,128)(2,1)} %gather.11), calls=%async_computation.1 | async-start | bytes 3670016 | tf_op jit(solution)/shard_map/all_to_all | solution.py:323
  46.9 2.1 %dynamic-slice_bitcast_fusion = (bf16[512,128]{1,0:T(8,128)(2,1)S(1)}, bf16[512,128]{1,0:T(8,128)(2,1)S(1)}, bf16[512,128]{1,0:T(8,128)(2,1)}, bf16[512,128]{1,0...) fusion(bf16[8,512,128]{2,1,0:T(8,128)(2,1)} %pad_maximum_fusion, ...), kind=kLoop, calls=%fused_computation.9 | loop fusion | bytes 2097184 | tf_op jit(solution)/shard_map/jit(dynamic_index_in_dim)/squeeze | solution.py:272
  49.1 2.8 %collective-permute-start.13 = (bf16[512,128]{1,0:T(8,128)(2,1)S(1)}, bf16[512,128]{1,0:T(8,128)(2,1)}, u32[]{:S(2)}, u32[]{:S(2)}) collective-permute-start(bf16[512,128]{1,0:T(8,128)(2,1)S(1)} %get-tuple-element.33), channel_id=1, source_target_pairs={{0,7},{1,6},{2,5},{3,4},{4,3},{5,2},{6,1},{7,0},{8,15},{9,14},{10,... | collective-permute-start | bytes 393224 | tf_op jit(solution)/shard_map/ppermute | solution.py:273
  52.8 2.5 %collective-permute-start.10 = (bf16[512,128]{1,0:T(8,128)(2,1)S(1)}, bf16[512,128]{1,0:T(8,128)(2,1)}, u32[]{:S(2)}, u32[]{:S(2)}) collective-permute-start(bf16[512,128]{1,0:T(8,128)(2,1)S(1)} %get-tuple-element.36), channel_id=1, source_target_pairs={{0,4},{1,5},{2,6},{3,7},{4,0},{5,1},{6,2},{7,3},{8,12},{9,13},{10,... | collective-permute-start | bytes 393224 | tf_op jit(solution)/shard_map/ppermute | solution.py:273
  57.0 8.5 %collective-permute-done.8 = bf16[512,128]{1,0:T(8,128)(2,1)S(1)} collective-permute-done((bf16[512,128]{1,0:T(8,128)(2,1)}, bf16[512,128]{1,0:T(8,128)(2,1)S(1)}, u32[]{:S(2)}, u32[]{:S(2)}) %collective-permute-start.8) | collective-permute-done | bytes 131104 | tf_op jit(solution)/shard_map/ppermute | solution.py:273
  65.6 5.7 %collective-permute-done.9 = bf16[512,128]{1,0:T(8,128)(2,1)S(1)} collective-permute-done((bf16[512,128]{1,0:T(8,128)(2,1)}, bf16[512,128]{1,0:T(8,128)(2,1)S(1)}, u32[]{:S(2)}, u32[]{:S(2)}) %collective-permute-start.9) | collective-permute-done | bytes 131104 | tf_op jit(solution)/shard_map/ppermute | solution.py:273
  71.3 19.3 %all-to-all-done.1.x_ref = bf16[32,224,128]{2,1,0:T(8,128)(2,1)S(1)} async-done(((bf16[32,224,128]{2,1,0:T(8,128)(2,1)}), bf16[32,224,128]{2,1,0:T(8,128)(2,1)S(1)}, u32[]{:S(2)}, u32[]{:S(2)}) %all-to-all-start.1) | async-done | bytes 1835040 | tf_op jit(solution)/shard_map/all_to_all | solution.py:323
  90.6 14.1 %query_parts.1 = bf16[32,96,128]{2,1,0:T(8,128)(2,1)} custom-call(s32[3]{0:T(128)S(1)} %dynamic_slice.53.src_ref, bf16[32,224,128]{2,1,0:T(8,128)(2,1)S(1)} %all-to-all-done.1.x_ref, bf16[2048,512]{1,0:T(8,128)(2,1)} %k_ref.1, bf16[2048,512]{1,0:T(8,128)(2,1)} %v_ref.1), custom_call_target="tpu_custom_call" | custom-call | flops 12884901888 | bytes 6291456 | tf_op jit(solution)/shard_map/query_parts/pallas_call | solution.py:331
  104.8 6.5 %all-to-all-start.2 = ((bf16[32,96,128]{2,1,0:T(8,128)(2,1)}), bf16[32,96,128]{2,1,0:T(8,128)(2,1)S(1)}, u32[]{:S(2)}, u32[]{:S(2)}) async-start(bf16[32,96,128]{2,1,0:T(8,128)(2,1)} %query_parts.1), calls=%async_computation.2 | async-start | bytes 1572864 | tf_op jit(solution)/shard_map/all_to_all | solution.py:344
  112.8 16.5 %context_grads.1 = (bf16[2048,512]{1,0:T(8,128)(2,1)}, bf16[2048,512]{1,0:T(8,128)(2,1)}) custom-call(s32[3]{0:T(128)S(1)} %dynamic_slice.53.src_ref, bf16[32,224,128]{2,1,0:T(8,128)(2,1)S(1)} %all-to-all-done.1.x_ref, bf16[2048,512]{1,0:T(8,128)(2,1)} %k_ref.1, bf16[2048,512]{1,0:T(8,128)(2,1)} %v_ref.1), custom_call_target="tpu_custom_call" | custom-call | flops 16106127360 | bytes 10485760 | tf_op jit(solution)/shard_map/context_grads/pallas_call | solution.py:349
  129.3 3.0 %all-to-all-done.2.in_ref = bf16[32,96,128]{2,1,0:T(8,128)(2,1)S(1)} async-done(((bf16[32,96,128]{2,1,0:T(8,128)(2,1)}), bf16[32,96,128]{2,1,0:T(8,128)(2,1)S(1)}, u32[]{:S(2)}, u32[]{:S(2)}) %all-to-all-start.2) | async-done | bytes 786464 | tf_op jit(solution)/shard_map/all_to_all | solution.py:344
  133.8 6.8 %all-to-all-start.3 = ((bf16[32,32,128]{2,1,0:T(8,128)(2,1)}), bf16[32,32,128]{2,1,0:T(8,128)(2,1)S(1)}, u32[]{:S(2)}, u32[]{:S(2)}) async-start(bf16[32,32,128]{2,1,0:T(8,128)(2,1)} %pair_sum.1), calls=%async_computation.3 | async-start | bytes 524288 | tf_op jit(solution)/shard_map/all_to_all | solution.py:370
  140.5 1.6 %bitcast_dynamic-update-slice_fusion.2 = bf16[8,512,128]{2,1,0:T(8,128)(2,1)} fusion(bf16[8,512,128]{2,1,0:T(8,128)(2,1)} %bitcast_dynamic-update-slice_fusion.3, bf16[512,128]{1,0:T(8,128)(2,1)} %collective-permute-done.11), kind=kLoop, calls=%fused_computation.4 | loop fusion | bytes 262144
  143.7 1.6 %bitcast_dynamic-update-slice_fusion.w_ref = bf16[8,512,128]{2,1,0:T(8,128)(2,1)} fusion(bf16[8,512,128]{2,1,0:T(8,128)(2,1)} %bitcast_dynamic-update-slice_fusion.1, bf16[512,128]{1,0:T(8,128)(2,1)} %collective-permute-done.13), kind=kLoop, calls=%fused_computation.2 | loop fusion | bytes 262144 | tf_op jit(solution)/shard_map/stack | solution.py:371
  146.5 3.0 %own_set.1 = (f32[256,512]{1,0:T(8,128)S(1)}, bf16[256,512]{1,0:T(8,128)(2,1)}, bf16[256,512]{1,0:T(8,128)(2,1)}) custom-call(s32[1]{0:T(128)} %bitcast.26.me_ref, bf16[8,512,128]{2,1,0:T(8,128)(2,1)S(1)} %copy-done.1, bf16[4,8,128]{2,1,0:T(8,128)(2,1)S(1)} %bitcast.79), custom_call_target="tpu_custom_call" | custom-call | flops 335544320 | bytes 2097152 | tf_op jit(solution)/shard_map/own_set/pallas_call | solution.py:373
  149.5 1.8 %all-to-all-done.3.in_ref = bf16[32,32,128]{2,1,0:T(8,128)(2,1)S(1)} async-done(((bf16[32,32,128]{2,1,0:T(8,128)(2,1)}), bf16[32,32,128]{2,1,0:T(8,128)(2,1)S(1)}, u32[]{:S(2)}, u32[]{:S(2)}) %all-to-all-start.3) | async-done | bytes 262176 | tf_op jit(solution)/shard_map/all_to_all | solution.py:370
  (78 shorter events, 15.8 us)
Async XLA Ops:
  0.6 23.1 %copy-start.3 = (bf16[32,4096]{1,0:T(8,128)(2,1)S(1)}, bf16[32,4096]{1,0:T(8,128)(2,1)}, u32[]{:S(2)}) copy-start(bf16[32,4096]{1,0:T(8,128)(2,1)} %do_hbm.1) | copy-start | bytes 786436
  0.6 22.9 %copy-start.2 = (bf16[32,4096]{1,0:T(8,128)(2,1)S(1)}, bf16[32,4096]{1,0:T(8,128)(2,1)}, u32[]{:S(2)}) copy-start(bf16[32,4096]{1,0:T(8,128)(2,1)} %q_hbm.1) | copy-start | bytes 786436
  0.7 23.3 %copy-start.7 = (s32[32,2]{0,1:T(2,128)S(1)}, s32[32,2]{0,1:T(2,128)}, u32[]{:S(2)}) copy-start(s32[32,2]{0,1:T(2,128)} %param.17) | copy-start | bytes 772
  0.7 23.7 %copy-start.4 = (bf16[32,4096]{1,0:T(8,128)(2,1)S(1)}, bf16[32,4096]{1,0:T(8,128)(2,1)}, u32[]{:S(2)}) copy-start(bf16[32,4096]{1,0:T(8,128)(2,1)} %param.10) | copy-start | bytes 786436
  0.7 23.9 %copy-start.5 = (bf16[32,4096]{1,0:T(8,128)(2,1)S(1)}, bf16[32,4096]{1,0:T(8,128)(2,1)}, u32[]{:S(2)}) copy-start(bf16[32,4096]{1,0:T(8,128)(2,1)} %param.11) | copy-start | bytes 786436
  2.6 34.2 %all-to-all-start = ((bf16[256,8,128]{2,1,0:T(8,128)(2,1)}), bf16[256,8,128]{2,1,0:T(8,128)(2,1)S(1)}, u32[]{:S(2)}, u32[]{:S(2)}) async-start(bf16[256,8,128]{2,1,0:T(8,128)(2,1)} %get-tuple-element.19), calls=%async_computation | async-start | bytes 1048576 | tf_op jit(solution)/shard_map/all_to_all | solution.py:292
  17.1 16.3 %collective-permute-start.6 = (f32[4,32]{1,0:T(4,128)S(1)}, f32[4,32]{1,0:T(4,128)S(1)}, u32[]{:S(2)}, u32[]{:S(2)}) collective-permute-start(f32[4,32]{1,0:T(4,128)S(1)} %get-tuple-element.41), channel_id=1, source_target_pairs={{0,7},{1,6},{2,5},{3,4},{4,3},{5,2},{6,1},{7,0},{8,15},{9,14},{10,... | collective-permute-start | bytes 1544 | tf_op jit(solution)/shard_map/ppermute | solution.py:273
  19.6 13.7 %collective-permute-start.5 = (f32[4,32]{1,0:T(4,128)S(1)}, f32[4,32]{1,0:T(4,128)S(1)}, u32[]{:S(2)}, u32[]{:S(2)}) collective-permute-start(f32[4,32]{1,0:T(4,128)S(1)} %get-tuple-element.42), channel_id=1, source_target_pairs={{0,6},{1,7},{2,4},{3,5},{4,2},{5,3},{6,0},{7,1},{8,14},{9,15},{10,... | collective-permute-start | bytes 1544 | tf_op jit(solution)/shard_map/ppermute | solution.py:273
  20.2 13.1 %collective-permute-start.4 = (f32[4,32]{1,0:T(4,128)S(1)}, f32[4,32]{1,0:T(4,128)S(1)}, u32[]{:S(2)}, u32[]{:S(2)}) collective-permute-start(f32[4,32]{1,0:T(4,128)S(1)} %get-tuple-element.43), channel_id=1, source_target_pairs={{0,5},{1,4},{2,7},{3,6},{4,1},{5,0},{6,3},{7,2},{8,13},{9,12},{10,... | collective-permute-start | bytes 1544 | tf_op jit(solution)/shard_map/ppermute | solution.py:273
  21.6 11.7 %collective-permute-start.3 = (f32[4,32]{1,0:T(4,128)S(1)}, f32[4,32]{1,0:T(4,128)S(1)}, u32[]{:S(2)}, u32[]{:S(2)}) collective-permute-start(f32[4,32]{1,0:T(4,128)S(1)} %get-tuple-element.44), channel_id=1, source_target_pairs={{0,4},{1,5},{2,6},{3,7},{4,0},{5,1},{6,2},{7,3},{8,12},{9,13},{10,... | collective-permute-start | bytes 1544 | tf_op jit(solution)/shard_map/ppermute | solution.py:273
  23.4 3.2 %collective-permute-start = (f32[4,32]{1,0:T(4,128)S(1)}, f32[4,32]{1,0:T(4,128)S(1)}, u32[]{:S(2)}, u32[]{:S(2)}) collective-permute-start(f32[4,32]{1,0:T(4,128)S(1)} %get-tuple-element.47), channel_id=1, source_target_pairs={{0,1},{1,0},{2,3},{3,2},{4,5},{5,4},{6,7},{7,6},{8,9},{9,8},{10,11... | collective-permute-start | bytes 1544 | tf_op jit(solution)/shard_map/ppermute | solution.py:273
  26.6 3.7 %collective-permute-start.1 = (f32[4,32]{1,0:T(4,128)S(1)}, f32[4,32]{1,0:T(4,128)S(1)}, u32[]{:S(2)}, u32[]{:S(2)}) collective-permute-start(f32[4,32]{1,0:T(4,128)S(1)} %get-tuple-element.46), channel_id=1, source_target_pairs={{0,2},{1,3},{2,0},{3,1},{4,6},{5,7},{6,4},{7,5},{8,10},{9,11},{10,... | collective-permute-start | bytes 1544 | tf_op jit(solution)/shard_map/ppermute | solution.py:273
  30.2 3.0 %collective-permute-start.2 = (f32[4,32]{1,0:T(4,128)S(1)}, f32[4,32]{1,0:T(4,128)S(1)}, u32[]{:S(2)}, u32[]{:S(2)}) collective-permute-start(f32[4,32]{1,0:T(4,128)S(1)} %get-tuple-element.45), channel_id=1, source_target_pairs={{0,3},{1,2},{2,1},{3,0},{4,7},{5,6},{6,5},{7,4},{8,11},{9,10},{10,... | collective-permute-start | bytes 1544 | tf_op jit(solution)/shard_map/ppermute | solution.py:273
  38.7 51.9 %all-to-all-start.1 = ((bf16[32,224,128]{2,1,0:T(8,128)(2,1)}), bf16[32,224,128]{2,1,0:T(8,128)(2,1)S(1)}, u32[]{:S(2)}, u32[]{:S(2)}) async-start(bf16[32,224,128]{2,1,0:T(8,128)(2,1)} %gather.11), calls=%async_computation.1 | async-start | bytes 3670016 | tf_op jit(solution)/shard_map/all_to_all | solution.py:323
  49.0 6.3 %collective-permute-start.7 = (bf16[512,128]{1,0:T(8,128)(2,1)}, bf16[512,128]{1,0:T(8,128)(2,1)}, u32[]{:S(2)}, u32[]{:S(2)}) collective-permute-start(bf16[512,128]{1,0:T(8,128)(2,1)} %get-tuple-element.39), channel_id=1, source_target_pairs={{0,1},{1,0},{2,3},{3,2},{4,5},{5,4},{6,7},{7,6},{8,9},{9,8},{10,11... | collective-permute-start | bytes 393224 | tf_op jit(solution)/shard_map/ppermute | solution.py:273
  49.1 94.6 %collective-permute-start.13 = (bf16[512,128]{1,0:T(8,128)(2,1)S(1)}, bf16[512,128]{1,0:T(8,128)(2,1)}, u32[]{:S(2)}, u32[]{:S(2)}) collective-permute-start(bf16[512,128]{1,0:T(8,128)(2,1)S(1)} %get-tuple-element.33), channel_id=1, source_target_pairs={{0,7},{1,6},{2,5},{3,4},{4,3},{5,2},{6,1},{7,0},{8,15},{9,14},{10,... | collective-permute-start | bytes 393224 | tf_op jit(solution)/shard_map/ppermute | solution.py:273
  52.0 90.2 %collective-permute-start.12 = (bf16[512,128]{1,0:T(8,128)(2,1)S(1)}, bf16[512,128]{1,0:T(8,128)(2,1)}, u32[]{:S(2)}, u32[]{:S(2)}) collective-permute-start(bf16[512,128]{1,0:T(8,128)(2,1)S(1)} %get-tuple-element.34), channel_id=1, source_target_pairs={{0,6},{1,7},{2,4},{3,5},{4,2},{5,3},{6,0},{7,1},{8,14},{9,15},{10,... | collective-permute-start | bytes 393224 | tf_op jit(solution)/shard_map/ppermute | solution.py:273
  52.5 88.1 %collective-permute-start.11 = (bf16[512,128]{1,0:T(8,128)(2,1)}, bf16[512,128]{1,0:T(8,128)(2,1)}, u32[]{:S(2)}, u32[]{:S(2)}) collective-permute-start(bf16[512,128]{1,0:T(8,128)(2,1)} %get-tuple-element.35), channel_id=1, source_target_pairs={{0,5},{1,4},{2,7},{3,6},{4,1},{5,0},{6,3},{7,2},{8,13},{9,12},{10,... | collective-permute-start | bytes 393224 | tf_op jit(solution)/shard_map/ppermute | solution.py:273
  52.8 58.4 %collective-permute-start.10 = (bf16[512,128]{1,0:T(8,128)(2,1)S(1)}, bf16[512,128]{1,0:T(8,128)(2,1)}, u32[]{:S(2)}, u32[]{:S(2)}) collective-permute-start(bf16[512,128]{1,0:T(8,128)(2,1)S(1)} %get-tuple-element.36), channel_id=1, source_target_pairs={{0,4},{1,5},{2,6},{3,7},{4,0},{5,1},{6,2},{7,3},{8,12},{9,13},{10,... | collective-permute-start | bytes 393224 | tf_op jit(solution)/shard_map/ppermute | solution.py:273
  55.4 10.2 %collective-permute-start.8 = (bf16[512,128]{1,0:T(8,128)(2,1)}, bf16[512,128]{1,0:T(8,128)(2,1)S(1)}, u32[]{:S(2)}, u32[]{:S(2)}) collective-permute-start(bf16[512,128]{1,0:T(8,128)(2,1)} %get-tuple-element.38), channel_id=1, source_target_pairs={{0,2},{1,3},{2,0},{3,1},{4,6},{5,7},{6,4},{7,5},{8,10},{9,11},{10,... | collective-permute-start | bytes 393224 | tf_op jit(solution)/shard_map/ppermute | solution.py:273
  65.5 5.7 %collective-permute-start.9 = (bf16[512,128]{1,0:T(8,128)(2,1)}, bf16[512,128]{1,0:T(8,128)(2,1)S(1)}, u32[]{:S(2)}, u32[]{:S(2)}) collective-permute-start(bf16[512,128]{1,0:T(8,128)(2,1)} %get-tuple-element.37), channel_id=1, source_target_pairs={{0,3},{1,2},{2,1},{3,0},{4,7},{5,6},{6,5},{7,4},{8,11},{9,10},{10,... | collective-permute-start | bytes 393224 | tf_op jit(solution)/shard_map/ppermute | solution.py:273
  71.3 33.5 %copy-start = (bf16[8,512,128]{2,1,0:T(8,128)(2,1)}, bf16[8,512,128]{2,1,0:T(8,128)(2,1)S(1)}, u32[]{:S(2)}) copy-start(bf16[8,512,128]{2,1,0:T(8,128)(2,1)S(1)} %bitcast_dynamic-update-slice_fusion.4) | copy-start | bytes 3145732
  104.8 27.5 %all-to-all-start.2 = ((bf16[32,96,128]{2,1,0:T(8,128)(2,1)}), bf16[32,96,128]{2,1,0:T(8,128)(2,1)S(1)}, u32[]{:S(2)}, u32[]{:S(2)}) async-start(bf16[32,96,128]{2,1,0:T(8,128)(2,1)} %query_parts.1), calls=%async_computation.2 | async-start | bytes 1572864 | tf_op jit(solution)/shard_map/all_to_all | solution.py:344
  133.8 17.6 %all-to-all-start.3 = ((bf16[32,32,128]{2,1,0:T(8,128)(2,1)}), bf16[32,32,128]{2,1,0:T(8,128)(2,1)S(1)}, u32[]{:S(2)}, u32[]{:S(2)}) async-start(bf16[32,32,128]{2,1,0:T(8,128)(2,1)} %pair_sum.1), calls=%async_computation.3 | async-start | bytes 524288 | tf_op jit(solution)/shard_map/all_to_all | solution.py:370
  (2 other events, 2.9 us)

commit v4 on v3

--- a/solution.py
+++ b/solution.py
@@ -48,18 +48,16 @@
     out_ref[...] = (spread(lse_ref[...] * math.sqrt(LANES), 0) + spread(dots_ref[...], 2)).astype(BF16)
 
 
-def prepare_kernel(q_hbm, do_hbm, o_hbm, out_hbm, dots_ref, q_ref, do_ref, o_ref, out_ref, sems, out_sems):
+def prepare_kernel(q_hbm, do_hbm, out_hbm, q_ref, do_ref, out_ref, sems, out_sems, *, per_group):
     copies = [
-        pltpu.make_async_copy(src, dst, sems.at[n])
-        for n, (src, dst) in enumerate(((q_hbm, q_ref), (do_hbm, do_ref), (o_hbm, o_ref)))
+        pltpu.make_async_copy(src, dst, sems.at[n]) for n, (src, dst) in enumerate(((q_hbm, q_ref), (do_hbm, do_ref)))
     ]
     for copy in copies:
         copy.start()
     rows, features = q_ref.shape
+    octets = rows // 8
     heads = features // LANES
-    groups, _, _ = dots_ref.shape
-    per_group = heads // groups
-    octets = rows // 8
+    groups = heads // per_group
     leaving = []
     for a, ref in enumerate((q_ref, do_ref)):
         copies[a].wait()
@@ -71,7 +69,14 @@
         half = pl.ds(a * per_group * octets * groups, per_group * octets * groups)
         leaving.append(pltpu.make_async_copy(out_ref.at[half], out_hbm.at[half], out_sems.at[a]))
         leaving[a].start()
-    copies[2].wait()
+    for copy in leaving:
+        copy.wait()
+
+
+def dots_kernel(do_ref, o_ref, dots_ref):
+    features = do_ref.shape[1]
+    heads = features // LANES
+    groups, per_group, _ = dots_ref.shape
     product = do_ref[...].astype(F32) * o_ref[...].astype(F32)
     high = product.astype(BF16)
     low = (product - high.astype(F32)).astype(BF16)
@@ -81,8 +86,6 @@
     dots = dot(pick, high, NT) + dot(pick, low, NT)
     for h in range(groups):
         dots_ref[h] = dots[h * per_group : (h + 1) * per_group]
-    for copy in leaving:
-        copy.wait()
 
 
 def gather_kernel(src_ref, in_ref, stats_ref, out_hbm, out_ref, sems):
@@ -154,15 +157,20 @@
         at = pl.ds(head * 8, 8)
         return pltpu.make_async_copy(out_ref.at[at], out_hbm.at[at], out_sems.at[head])
 
-    for head in range(per_group):
-        fetch(head, 0).start()
-        fetch(head, 1).start()
+    fetch(0, 0).start()
+    fetch(0, 1).start()
     load_statistics(src_ref, x_ref, stats)
 
     def body(head, carry):
         assemble(x_ref, stats, head, qx, dx)
         fetch(head, 0).wait()
         fetch(head, 1).wait()
+
+        @pl.when(head + 1 < per_group)
+        def _():
+            fetch(head + 1, 0).start()
+            fetch(head + 1, 1).start()
+
         keys = k_ref[head]
         keys_ext = extend(keys)
         values_ext = extend(v_ref[head])
@@ -181,9 +189,10 @@
         leave(head).wait()
 
 
-def context_kernel(src_ref, x_ref, k_ref, v_ref, dk_ref, dv_ref, qx, dx, stats, *, chunk):
+def context_kernel(src_ref, x_ref, k_ref, v_ref, *refs, chunk, first):
+    dk_ref, dv_ref, qx, dx, stats = refs[-5:]
     load_statistics(src_ref, x_ref, stats)
-    assemble(x_ref, stats, pl.program_id(0), qx, dx)
+    assemble(x_ref, stats, pl.program_id(0) + first, qx, dx)
 
     def body(i, carry):
         at = pl.ds(pl.multiple_of(i * chunk, chunk), chunk)
@@ -196,19 +205,20 @@
     lax.fori_loop(0, k_ref.shape[0] // chunk, body, 0, unroll=True)
 
 
-def own_kernel(me_ref, w_ref, stats_ref, dq_ref, dk_ref, dv_ref, qx, dx, kx, vx):
+def own_kernel(me_ref, stats_ref, *refs):
     head = pl.program_id(0)
-    groups = w_ref.shape[0]
+    window, (dq_ref, dk_ref, dv_ref, qx, dx, kx, vx) = refs[:-7], refs[-7:]
     row = lax.broadcasted_iota(jnp.int32, (8, LANES), 0)
     lane = lax.broadcasted_iota(jnp.int32, (8, LANES), 1)
     stats = stats_ref[0].astype(F32)
     kx[:, LANES:] = jnp.full((kx.shape[0], LANES), -1.0, BF16)
     vx[:, LANES:] = jnp.full((kx.shape[0], LANES), -1.0, BF16)
-    for src in range(groups):
-        at = slice(src * 32, src * 32 + 32)
+    for src, w_ref in enumerate(window):
+        at = pl.ds(pl.multiple_of((me_ref[0] ^ src) * 32, 32), 32)
         for n, ref in enumerate((qx, dx, kx, vx)):
             piece = pl.ds(pl.multiple_of(n * 128 + head * 32, 32), 32)
-            ref[at, 0:LANES] = w_ref[me_ref[0] ^ src, piece, :]
+            ref[at, 0:LANES] = w_ref[piece, :]
+        at = slice(src * 32, src * 32 + 32)
         for a, ref in ((0, qx), (1, dx)):
             first = ((src % 4) * 8 + row) * 4 + 2 * a
             mask = (lane == first) | (lane == first + 1)
@@ -224,17 +234,29 @@
     dv_ref[...] = dot(weights.astype(BF16), dx[:, 0:LANES], TN).astype(BF16)
 
 
-def pair_kernel(owner_ref, row_ref, in_ref, out_ref):
-    def body(b, carry):
-        total = None
-        for s in range(2):
-            row = pl.multiple_of(row_ref[b * 2 + s], 32)
-            value = in_ref[owner_ref[b * 2 + s], pl.ds(row, 32), :].astype(F32)
-            total = value if total is None else total + value
-        out_ref[b] = total.astype(BF16)
+def pair_kernel(owner_ref, row_ref, in_ref, out_hbm, out_ref, sems):
+    count = 8
+
+    def leave(part):
+        at = pl.ds(part * count, count)
+        return pltpu.make_async_copy(out_ref.at[at], out_hbm.at[at], sems.at[part])
+
+    def body(part, carry):
+        for k in range(count):
+            b = part * count + k
+            total = None
+            for s in range(2):
+                row = pl.multiple_of(row_ref[b * 2 + s], 32)
+                value = in_ref[owner_ref[b * 2 + s], pl.ds(row, 32), :].astype(F32)
+                total = value if total is None else total + value
+            out_ref[b] = total.astype(BF16)
+        leave(part).start()
         return carry
 
-    lax.fori_loop(0, out_ref.shape[0], body, 0, unroll=4)
+    parts = out_ref.shape[0] // count
+    lax.fori_loop(0, parts, body, 0)
+    for part in range(parts):
+        leave(part).wait()
 
 
 def finish_kernel(in_ref, own_ref, out_ref):
@@ -276,19 +298,24 @@
     hbm = pl.BlockSpec(memory_space=pltpu.HBM)
     smem = pl.BlockSpec(memory_space=pltpu.SMEM)
     tiles = owners * groups
-    pieces, dots = pl.pallas_call(
-        prepare_kernel,
-        out_shape=(
-            jax.ShapeDtypeStruct((tiles, 8, LANES), BF16),
-            jax.ShapeDtypeStruct((groups, per_group, rows), F32),
-        ),
-        in_specs=[hbm] * 3,
-        out_specs=(hbm, vmem()),
-        scratch_shapes=[pltpu.VMEM(queries.shape, BF16)] * 3
-        + [pltpu.VMEM((tiles, 8, LANES), BF16), pltpu.SemaphoreType.DMA((3,)), pltpu.SemaphoreType.DMA((2,))],
+    pieces = pl.pallas_call(
+        functools.partial(prepare_kernel, per_group=per_group),
+        out_shape=jax.ShapeDtypeStruct((tiles, 8, LANES), BF16),
+        in_specs=[hbm] * 2,
+        out_specs=hbm,
+        scratch_shapes=[pltpu.VMEM(queries.shape, BF16)] * 2
+        + [pltpu.VMEM((tiles, 8, LANES), BF16), pltpu.SemaphoreType.DMA((2,)), pltpu.SemaphoreType.DMA((2,))],
         compiler_params=params(),
         name="prepare",
-    )(in_hbm(queries), in_hbm(out_grad), in_hbm(attn_out))
+    )(in_hbm(queries), in_hbm(out_grad))
+    dots = pl.pallas_call(
+        dots_kernel,
+        out_shape=jax.ShapeDtypeStruct((groups, per_group, rows), F32),
+        in_specs=[vmem()] * 2,
+        out_specs=vmem(),
+        compiler_params=params(),
+        name="out_dot",
+    )(*lax.optimization_barrier((out_grad, attn_out, pieces))[:2])
     held = lax.all_to_all(pieces, ("seq", "head"), split_axis=0, concat_axis=0, tiled=True)
     held = held.reshape(owners, 64, LANES)
 
@@ -323,52 +350,6 @@
     items = lax.all_to_all(outgoing, "seq", split_axis=0, concat_axis=0, tiled=True)
     window = swap(window)
 
-    slot_rows = SLOTS * block_rows
-    work = 2 * slot_rows * key_rows * LANES * per_group
-    ctx_keys, ctx_values = in_hbm(ctx_keys), in_hbm(ctx_values)
-    wide = pltpu.VMEM((slot_rows, 2 * LANES), BF16)
-    slot_stats = pltpu.VMEM((SLOTS, 32, LANES), F32)
-    parts = pl.pallas_call(
-        query_kernel,
-        out_shape=jax.ShapeDtypeStruct((owners, SLOTS * 32, LANES), BF16),
-        in_specs=[smem, vmem(), hbm, hbm],
-        out_specs=hbm,
-        scratch_shapes=[pltpu.VMEM((per_group, key_rows, LANES), BF16)] * 2
-        + [pltpu.VMEM((owners, SLOTS * 32, LANES), BF16), wide, wide, slot_stats]
-        + [pltpu.SemaphoreType.DMA((per_group, 2)), pltpu.SemaphoreType.DMA((per_group,))],
-        compiler_params=params(32),
-        cost_estimate=pl.CostEstimate(flops=8 * work, bytes_accessed=6 << 20, transcendentals=0),
-        name="query_parts",
-    )(mine, items, ctx_keys, ctx_values)
-
-    returned = lax.all_to_all(parts, "seq", split_axis=0, concat_axis=0, tiled=True)
-
-    items_later, _ = lax.optimization_barrier((items, parts))
-    context_spec = pl.BlockSpec((key_rows, LANES), lambda g: (0, g))
-    items_spec = pl.BlockSpec((owners, item_rows, LANES), lambda g: (0, 0, 0))
-    ctx_key_grad, ctx_value_grad = pl.pallas_call(
-        functools.partial(context_kernel, chunk=256),
-        grid=(per_group,),
-        out_shape=(jax.ShapeDtypeStruct((key_rows, features), BF16),) * 2,
-        in_specs=[smem, items_spec, context_spec, context_spec],
-        out_specs=(context_spec, context_spec),
-        scratch_shapes=[wide, wide, slot_stats],
-        compiler_params=params(24),
-        cost_estimate=pl.CostEstimate(flops=10 * work, bytes_accessed=10 << 20, transcendentals=0),
-        name="context_grads",
-    )(mine, items_later, ctx_keys, ctx_values)
-
-    returned, ctx_key_grad, ctx_value_grad = lax.optimization_barrier((returned, ctx_key_grad, ctx_value_grad))
-    summed = pl.pallas_call(
-        pair_kernel,
-        out_shape=jax.ShapeDtypeStruct((owners, 32, LANES), BF16),
-        in_specs=[smem, smem, vmem()],
-        out_specs=vmem(),
-        compiler_params=params(),
-        name="pair_sum",
-    )(flat, slot_of * 32, returned)
-    home = lax.all_to_all(summed, "seq", split_axis=0, concat_axis=0, tiled=True)
-    window, _ = lax.optimization_barrier((jnp.stack(window), summed))
     head_spec = pl.BlockSpec((block_rows, LANES), lambda g: (0, g))
     own_dq, new_key_grad, new_value_grad = pl.pallas_call(
         own_kernel,
@@ -378,18 +359,70 @@
             jax.ShapeDtypeStruct((block_rows, features), BF16),
             jax.ShapeDtypeStruct((block_rows, features), BF16),
         ),
-        in_specs=[
-            smem,
-            pl.BlockSpec(window.shape, lambda g: (0, 0, 0)),
-            pl.BlockSpec((1, groups, LANES), lambda g: (g, 0, 0)),
-        ],
+        in_specs=[smem, pl.BlockSpec((1, groups, LANES), lambda g: (g, 0, 0))]
+        + [pl.BlockSpec(piece.shape, lambda g: (0, 0)) for piece in window],
         out_specs=(head_spec, head_spec, head_spec),
         scratch_shapes=[pltpu.VMEM((block_rows, 2 * LANES), BF16)] * 4,
         compiler_params=params(),
         cost_estimate=pl.CostEstimate(flops=10 * block_rows * block_rows * features, bytes_accessed=2 << 20, transcendentals=0),
         name="own_set",
-    )(me.reshape(1), window, stats.reshape(per_group, groups, LANES))
-
+    )(me.reshape(1), stats.reshape(per_group, groups, LANES), *window)
+
+    items, own_dq, new_key_grad, new_value_grad = lax.optimization_barrier((items, own_dq, new_key_grad, new_value_grad))
+
+    slot_rows = SLOTS * block_rows
+    work = 2 * slot_rows * key_rows * LANES * per_group
+    wide = pltpu.VMEM((slot_rows, 2 * LANES), BF16)
+    slot_stats = pltpu.VMEM((SLOTS, 32, LANES), F32)
+    ctx_keys, ctx_values = in_hbm(ctx_keys), in_hbm(ctx_values)
+    parts = pl.pallas_call(
+        query_kernel,
+        out_shape=jax.ShapeDtypeStruct((owners, SLOTS * 32, LANES), BF16),
+        in_specs=[smem, vmem(), hbm, hbm],
+        out_specs=hbm,
+        scratch_shapes=[pltpu.VMEM((per_group, key_rows, LANES), BF16)] * 2
+        + [pltpu.VMEM((owners, SLOTS * 32, LANES), BF16), wide, wide, slot_stats]
+        + [pltpu.SemaphoreType.DMA((per_group, 2)), pltpu.SemaphoreType.DMA((per_group,))],
+        compiler_params=params(28),
+        cost_estimate=pl.CostEstimate(flops=8 * work, bytes_accessed=6 << 20, transcendentals=0),
+        name="query_parts",
+    )(mine, items, ctx_keys, ctx_values)
+
+    returned = lax.all_to_all(parts, "seq", split_axis=0, concat_axis=0, tiled=True)
+
+    later = 3
+
+    def context_grads(first, count, rows_in, grads):
+        block = pl.BlockSpec((key_rows, LANES), lambda g: (0, first + g))
+        items_spec = pl.BlockSpec((owners, item_rows, LANES), lambda g: (0, 0, 0))
+        return pl.pallas_call(
+            functools.partial(context_kernel, chunk=256, first=first),
+            grid=(count,),
+            out_shape=(jax.ShapeDtypeStruct((key_rows, features), BF16),) * 2,
+            in_specs=[smem, items_spec, block, block] + [pl.BlockSpec(memory_space=pl.ANY)] * len(grads),
+            out_specs=(block, block),
+            scratch_shapes=[wide, wide, slot_stats],
+            input_output_aliases={4 + n: n for n in range(len(grads))},
+            compiler_params=params(24),
+            cost_estimate=pl.CostEstimate(flops=10 * work * count // per_group, bytes_accessed=10 << 20, transcendentals=0),
+            name="context_grads",
+        )(mine, rows_in, ctx_keys, ctx_values, *grads)
+
+    items, _ = lax.optimization_barrier((items, parts))
+    grads = context_grads(0, later, items, ())
+    returned, grads, items = lax.optimization_barrier((returned, grads, items))
+    summed = pl.pallas_call(
+        pair_kernel,
+        out_shape=jax.ShapeDtypeStruct((owners, 32, LANES), BF16),
+        in_specs=[smem, smem, vmem()],
+        out_specs=hbm,
+        scratch_shapes=[pltpu.VMEM((owners, 32, LANES), BF16), pltpu.SemaphoreType.DMA((4,))],
+        compiler_params=params(),
+        name="pair_sum",
+    )(flat, slot_of * 32, returned)
+    home = lax.all_to_all(summed, "seq", split_axis=0, concat_axis=0, tiled=True)
+    items, grads, _ = lax.optimization_barrier((items, grads, summed))
+    ctx_key_grad, ctx_value_grad = context_grads(later, per_group - later, items, grads)
     query_grad = pl.pallas_call(
         finish_kernel,
         out_shape=jax.ShapeDtypeStruct((block_rows, features), BF16),

time: 154 us -> 152 us (0.987)
  local copies, waits for them, and re-layouts: 13 us -> 4.52 us
  waiting for transfers between devices: 47.2 us -> 52.8 us
  Pallas kernels: 39.7 us -> 41.7 us
    unnamed x29 -> x21, local copies, waits for them, and re-layouts: 7.04 us -> 0.17 us
    all_to_all x1, waiting for transfers between devices: 3.02 us -> 8.71 us  [per_device(): lax.all_to_all(parts, 'seq', split_axis=0, concat_axis=0, tiled=True)]
    ppermute x14, waiting for transfers between devices: 20.5 us -> 16.5 us  [swap(): lax.ppermute(part, 'head', [(i, i ^ k) for i in range(groups)])]
    all_to_all x1, waiting for transfers between devices: 1.84 us -> 5.22 us  [per_device(): lax.all_to_all(summed, 'seq', split_axis=0, concat_axis=0, tiled=True)]
    pallas_call x2 -> x4, Pallas kernels: 18.4 us -> 20.8 us  [the longest x2 18.6 us: context_grads(): pl.pallas_call(functools.partial(context_kernel, chunk=256, first=first),...]
    ppermute x14, starting transfers between devices: 13.8 us -> 15.6 us  [swap(): lax.ppermute(part, 'head', [(i, i ^ k) for i in range(groups)])]
    another operation x1 -> x0, local copies, waits for them, and re-layouts: 1.57 us -> none  [per_device(): window, _ = lax.optimization_barrier((jnp.stack(window), summed))]
  transfers between devices with their start and end apart: 18 -> 18, of which waited for: 8 -> 12; matrix products, arithmetic and copies ran while one was open for 9% -> 4% of each run, Pallas kernels for 23% -> 15%
where the time goes in v4:
time: 152 us; the launch traced here: 151 us
  waiting for transfers between devices  52.8 us (35%)
  starting transfers between devices  49.7 us (33%)
  Pallas kernels  41.7 us (27%)
  local copies, waits for them, and re-layouts  4.52 us (3%)
    all_to_all x1, waiting for transfers between devices, per_device(): lax.all_to_all(outgoing, 'seq', split_axis=0, concat_axis=0, tiled=True)  19.3 us
    pallas_call x2, Pallas kernels, context_grads(): pl.pallas_call(functools.partial(context_kernel, chunk=256, first=first),...  18.6 us
    ppermute x14, waiting for transfers between devices, swap(): lax.ppermute(part, 'head', [(i, i ^ k) for i in range(groups)])  16.5 us
    ppermute x14, starting transfers between devices, swap(): lax.ppermute(part, 'head', [(i, i ^ k) for i in range(groups)])  15.6 us
    all_to_all x1, starting transfers between devices, per_device(): lax.all_to_all(pieces, ('seq', 'head'), split_axis=0, concat_axis=0, tile...  14.4 us
    pallas_call x1, Pallas kernels, per_device(): pl.pallas_call(query_kernel, out_shape=jax.ShapeDtypeStruct((owners, SLOT...  13.8 us
    all_to_all x1, waiting for transfers between devices, per_device(): lax.all_to_all(parts, 'seq', split_axis=0, concat_axis=0, tiled=True)  8.71 us
    all_to_all x1, starting transfers between devices, per_device(): lax.all_to_all(outgoing, 'seq', split_axis=0, concat_axis=0, tiled=True)  7.61 us
  transfers between devices with their start and end apart: 18, of which 12 were waited for; matrix products, arithmetic and copies ran while one was open for 4% of the time, Pallas kernels for 15%

profile of v4, /device:TPU:32, one launch (start us, length us, event | category | flops | bytes accessed | tf_op | source)
XLA Modules:
  0.0 151.2 jit_solution(7249891574711196352)
XLA Ops:
  0.7 1.9 %prepare.1 = bf16[256,8,128]{2,1,0:T(8,128)(2,1)} custom-call(bf16[32,4096]{1,0:T(8,128)(2,1)} %q_hbm.1, bf16[32,4096]{1,0:T(8,128)(2,1)} %do_ref), custom_call_target="tpu_custom_call" | custom-call | tf_op jit(solution)/shard_map/prepare/pallas_call | solution.py:301
  2.6 14.4 %all-to-all-start = ((bf16[256,8,128]{2,1,0:T(8,128)(2,1)}), bf16[256,8,128]{2,1,0:T(8,128)(2,1)S(1)}, u32[]{:S(2)}, u32[]{:S(2)}) async-start(bf16[256,8,128]{2,1,0:T(8,128)(2,1)} %prepare.1), calls=%async_computation | async-start | bytes 1048576 | tf_op jit(solution)/shard_map/all_to_all | solution.py:319
  19.3 3.0 %collective-permute-start.3 = (f32[4,32]{1,0:T(4,128)S(1)}, f32[4,32]{1,0:T(4,128)S(1)}, u32[]{:S(2)}, u32[]{:S(2)}) collective-permute-start(f32[4,32]{1,0:T(4,128)S(1)} %get-tuple-element.62), channel_id=1, source_target_pairs={{0,4},{1,5},{2,6},{3,7},{4,0},{5,1},{6,2},{7,3},{8,12},{9,13},{10,... | collective-permute-start | bytes 1544 | tf_op jit(solution)/shard_map/ppermute | solution.py:295
  25.7 2.8 %collective-permute-start.5 = (f32[4,32]{1,0:T(4,128)S(1)}, f32[4,32]{1,0:T(4,128)S(1)}, u32[]{:S(2)}, u32[]{:S(2)}) collective-permute-start(f32[4,32]{1,0:T(4,128)S(1)} %get-tuple-element.60), channel_id=1, source_target_pairs={{0,6},{1,7},{2,4},{3,5},{4,2},{5,3},{6,0},{7,1},{8,14},{9,15},{10,... | collective-permute-start | bytes 1544 | tf_op jit(solution)/shard_map/ppermute | solution.py:295
  28.7 1.9 %collective-permute-done.5 = f32[4,32]{1,0:T(4,128)S(1)} collective-permute-done((f32[4,32]{1,0:T(4,128)S(1)}, f32[4,32]{1,0:T(4,128)S(1)}, u32[]{:S(2)}, u32[]{:S(2)}) %collective-permute-start.5) | collective-permute-done | bytes 544 | tf_op jit(solution)/shard_map/ppermute | solution.py:295
  30.6 2.1 %collective-permute-done.6 = f32[4,32]{1,0:T(4,128)S(1)} collective-permute-done((f32[4,32]{1,0:T(4,128)S(1)}, f32[4,32]{1,0:T(4,128)S(1)}, u32[]{:S(2)}, u32[]{:S(2)}) %collective-permute-start.6) | collective-permute-done | bytes 544 | tf_op jit(solution)/shard_map/ppermute | solution.py:295
  33.7 3.1 %all-to-all-done = bf16[256,8,128]{2,1,0:T(8,128)(2,1)S(1)} async-done(((bf16[256,8,128]{2,1,0:T(8,128)(2,1)}), bf16[256,8,128]{2,1,0:T(8,128)(2,1)S(1)}, u32[]{:S(2)}, u32[]{:S(2)}) %all-to-all-start) | async-done | bytes 524320 | tf_op jit(solution)/shard_map/all_to_all | solution.py:319
  38.7 7.6 %all-to-all-start.1 = ((bf16[32,224,128]{2,1,0:T(8,128)(2,1)}), bf16[32,224,128]{2,1,0:T(8,128)(2,1)S(1)}, u32[]{:S(2)}, u32[]{:S(2)}) async-start(bf16[32,224,128]{2,1,0:T(8,128)(2,1)} %gather.11), calls=%async_computation.1 | async-start | bytes 3670016 | tf_op jit(solution)/shard_map/all_to_all | solution.py:350
  46.3 2.0 %dynamic-slice_bitcast_fusion = (bf16[512,128]{1,0:T(8,128)(2,1)S(1)}, bf16[512,128]{1,0:T(8,128)(2,1)S(1)}, bf16[512,128]{1,0:T(8,128)(2,1)S(1)}, bf16[512,128]...) fusion(bf16[8,512,128]{2,1,0:T(8,128)(2,1)} %pad_maximum_fusion, ...), kind=kLoop, calls=%fused_computation.2 | loop fusion | bytes 2097184 | tf_op jit(solution)/shard_map/jit(dynamic_index_in_dim)/squeeze | solution.py:294
  48.4 1.9 %collective-permute-start.9 = (bf16[512,128]{1,0:T(8,128)(2,1)}, bf16[512,128]{1,0:T(8,128)(2,1)S(1)}, u32[]{:S(2)}, u32[]{:S(2)}) collective-permute-start(bf16[512,128]{1,0:T(8,128)(2,1)} %get-tuple-element.55), channel_id=1, source_target_pairs={{0,3},{1,2},{2,1},{3,0},{4,7},{5,6},{6,5},{7,4},{8,11},{9,10},{10,... | collective-permute-start | bytes 393224 | tf_op jit(solution)/shard_map/ppermute | solution.py:295
  50.5 2.8 %collective-permute-start.11 = (bf16[512,128]{1,0:T(8,128)(2,1)S(1)}, bf16[512,128]{1,0:T(8,128)(2,1)S(1)}, u32[]{:S(2)}, u32[]{:S(2)}) collective-permute-start(bf16[512,128]{1,0:T(8,128)(2,1)S(1)} %get-tuple-element.53), channel_id=1, source_target_pairs={{0,5},{1,4},{2,7},{3,6},{4,1},{5,0},{6,3},{7,2},{8,13},{9,12},{10,... | collective-permute-start | bytes 393224 | tf_op jit(solution)/shard_map/ppermute | solution.py:295
  56.7 3.7 %collective-permute-done.10.refs_4_ = bf16[512,128]{1,0:T(8,128)(2,1)S(1)} collective-permute-done((bf16[512,128]{1,0:T(8,128)(2,1)S(1)}, bf16[512,128]{1,0:T(8,128)(2,1)S(1)}, u32[]{:S(2)}, u32[]{:S(2)}) %collective-permute-start.10) | collective-permute-done | bytes 131104 | tf_op jit(solution)/shard_map/ppermute | solution.py:295
  60.4 2.1 %collective-permute-done.11.refs_5_ = bf16[512,128]{1,0:T(8,128)(2,1)S(1)} collective-permute-done((bf16[512,128]{1,0:T(8,128)(2,1)S(1)}, bf16[512,128]{1,0:T(8,128)(2,1)S(1)}, u32[]{:S(2)}, u32[]{:S(2)}) %collective-permute-start.11) | collective-permute-done | bytes 131104 | tf_op jit(solution)/shard_map/ppermute | solution.py:295
  62.4 3.1 %collective-permute-done.12.refs_6_ = bf16[512,128]{1,0:T(8,128)(2,1)S(1)} collective-permute-done((bf16[512,128]{1,0:T(8,128)(2,1)S(1)}, bf16[512,128]{1,0:T(8,128)(2,1)S(1)}, u32[]{:S(2)}, u32[]{:S(2)}) %collective-permute-start.12) | collective-permute-done | bytes 131104 | tf_op jit(solution)/shard_map/ppermute | solution.py:295
  65.6 2.7 %collective-permute-done.13.refs_7_ = bf16[512,128]{1,0:T(8,128)(2,1)S(1)} collective-permute-done((bf16[512,128]{1,0:T(8,128)(2,1)S(1)}, bf16[512,128]{1,0:T(8,128)(2,1)S(1)}, u32[]{:S(2)}, u32[]{:S(2)}) %collective-permute-start.13) | collective-permute-done | bytes 131104 | tf_op jit(solution)/shard_map/ppermute | solution.py:295
  68.3 3.1 %own_set.1 = (f32[256,512]{1,0:T(8,128)S(1)}, bf16[256,512]{1,0:T(8,128)(2,1)}, bf16[256,512]{1,0:T(8,128)(2,1)}) custom-call(s32[1]{0:T(128)} %bitcast.26.me_ref, bf16[4,8,128]{2,1,0:T(8,128)(2,1)S(1)} %bitcast.63, bf16[512,128]{1,0:T(8,128)(2,1)S(1)} %get-tuple-element.58.refs_0_, bf16[512,128]{1,0:T(8,128)(2,1)S(1)} %collective-permute-done.7.refs_1_, ...), custom_call_target="tpu_custom_call" | custom-call | flops 335544320 | bytes 2097152 | tf_op jit(solution)/shard_map/own_set/pallas_call | solution.py:354
  71.3 19.3 %all-to-all-done.1.x_ref = bf16[32,224,128]{2,1,0:T(8,128)(2,1)S(1)} async-done(((bf16[32,224,128]{2,1,0:T(8,128)(2,1)}), bf16[32,224,128]{2,1,0:T(8,128)(2,1)S(1)}, u32[]{:S(2)}, u32[]{:S(2)}) %all-to-all-start.1) | async-done | bytes 1835040 | tf_op jit(solution)/shard_map/all_to_all | solution.py:350
  90.6 13.8 %query_parts.1 = bf16[32,96,128]{2,1,0:T(8,128)(2,1)} custom-call(s32[3]{0:T(128)S(1)} %dynamic_slice.53.src_ref, bf16[32,224,128]{2,1,0:T(8,128)(2,1)S(1)} %all-to-all-done.1.x_ref, bf16[2048,512]{1,0:T(8,128)(2,1)} %k_ref.3, bf16[2048,512]{1,0:T(8,128)(2,1)} %v_ref.3), custom_call_target="tpu_custom_call" | custom-call | flops 12884901888 | bytes 6291456 | tf_op jit(solution)/shard_map/query_parts/pallas_call | solution.py:378
  104.4 6.5 %all-to-all-start.2 = ((bf16[32,96,128]{2,1,0:T(8,128)(2,1)}), bf16[32,96,128]{2,1,0:T(8,128)(2,1)S(1)}, u32[]{:S(2)}, u32[]{:S(2)}) async-start(bf16[32,96,128]{2,1,0:T(8,128)(2,1)} %query_parts.1), calls=%async_computation.2 | async-start | bytes 1572864 | tf_op jit(solution)/shard_map/all_to_all | solution.py:391
  110.9 12.9 %context_grads.2 = (bf16[2048,512]{1,0:T(8,128)(2,1)}, bf16[2048,512]{1,0:T(8,128)(2,1)}) custom-call(s32[3]{0:T(128)S(1)} %dynamic_slice.53.src_ref, bf16[32,224,128]{2,1,0:T(8,128)(2,1)S(1)} %all-to-all-done.1.x_ref, bf16[2048,512]{1,0:T(8,128)(2,1)} %k_ref.3, bf16[2048,512]{1,0:T(8,128)(2,1)} %v_ref.3), custom_call_target="tpu_custom_call" | custom-call | flops 12079595520 | bytes 10485760 | tf_op jit(solution)/shard_map/context_grads/pallas_call | solution.py:398
  123.7 8.7 %all-to-all-done.2.in_ref = bf16[32,96,128]{2,1,0:T(8,128)(2,1)S(1)} async-done(((bf16[32,96,128]{2,1,0:T(8,128)(2,1)}), bf16[32,96,128]{2,1,0:T(8,128)(2,1)S(1)}, u32[]{:S(2)}, u32[]{:S(2)}) %all-to-all-start.2) | async-done | bytes 786464 | tf_op jit(solution)/shard_map/all_to_all | solution.py:391
  133.8 5.7 %all-to-all-start.3 = ((bf16[32,32,128]{2,1,0:T(8,128)(2,1)}), bf16[32,32,128]{2,1,0:T(8,128)(2,1)S(1)}, u32[]{:S(2)}, u32[]{:S(2)}) async-start(bf16[32,32,128]{2,1,0:T(8,128)(2,1)} %pair_sum.1), calls=%async_computation.3 | async-start | bytes 524288 | tf_op jit(solution)/shard_map/all_to_all | solution.py:423
  139.5 5.7 %context_grads.3 = (bf16[2048,512]{1,0:T(8,128)(2,1)}, bf16[2048,512]{1,0:T(8,128)(2,1)}) custom-call(s32[3]{0:T(128)S(1)} %dynamic_slice.53.src_ref, bf16[32,224,128]{2,1,0:T(8,128)(2,1)S(1)} %all-to-all-done.1.x_ref, bf16[2048,512]{1,0:T(8,128)(2,1)} %k_ref.3, bf16[2048,512]{1,0:T(8,128)(2,1)} %v_ref.3, ...), custom_call_target="tpu_custom_call", output_to_operand_aliasing={{0}: (4, {}), {1}: (5, {})} | custom-call | flops 4026531840 | bytes 10485760 | tf_op jit(solution)/shard_map/context_grads/pallas_call | solution.py:398
  145.2 5.2 %all-to-all-done.3.in_ref = bf16[32,32,128]{2,1,0:T(8,128)(2,1)S(1)} async-done(((bf16[32,32,128]{2,1,0:T(8,128)(2,1)}), bf16[32,32,128]{2,1,0:T(8,128)(2,1)S(1)}, u32[]{:S(2)}, u32[]{:S(2)}) %all-to-all-start.3) | async-done | bytes 262176 | tf_op jit(solution)/shard_map/all_to_all | solution.py:423
  (71 shorter events, 14.4 us)
Async XLA Ops:
  0.6 22.2 %copy-start.2 = (bf16[32,4096]{1,0:T(8,128)(2,1)S(1)}, bf16[32,4096]{1,0:T(8,128)(2,1)}, u32[]{:S(2)}) copy-start(bf16[32,4096]{1,0:T(8,128)(2,1)} %q_hbm.1) | copy-start | bytes 786436
  0.6 16.4 %copy-start = (bf16[32,4096]{1,0:T(8,128)(2,1)S(1)}, bf16[32,4096]{1,0:T(8,128)(2,1)}, u32[]{:S(2)}) copy-start(bf16[32,4096]{1,0:T(8,128)(2,1)} %do_ref) | copy-start | bytes 786436
  0.7 16.4 %copy-start.1 = (bf16[32,4096]{1,0:T(8,128)(2,1)S(1)}, bf16[32,4096]{1,0:T(8,128)(2,1)}, u32[]{:S(2)}) copy-start(bf16[32,4096]{1,0:T(8,128)(2,1)} %o_ref) | copy-start | bytes 786436
  0.7 22.3 %copy-start.6 = (s32[32,2]{0,1:T(2,128)S(1)}, s32[32,2]{0,1:T(2,128)}, u32[]{:S(2)}) copy-start(s32[32,2]{0,1:T(2,128)} %param.17) | copy-start | bytes 772
  0.7 22.7 %copy-start.3 = (bf16[32,4096]{1,0:T(8,128)(2,1)S(1)}, bf16[32,4096]{1,0:T(8,128)(2,1)}, u32[]{:S(2)}) copy-start(bf16[32,4096]{1,0:T(8,128)(2,1)} %param.11) | copy-start | bytes 786436
  2.6 21.1 %copy-start.4 = (bf16[32,4096]{1,0:T(8,128)(2,1)S(1)}, bf16[32,4096]{1,0:T(8,128)(2,1)}, u32[]{:S(2)}) copy-start(bf16[32,4096]{1,0:T(8,128)(2,1)} %param.10) | copy-start | bytes 786436
  2.6 34.2 %all-to-all-start = ((bf16[256,8,128]{2,1,0:T(8,128)(2,1)}), bf16[256,8,128]{2,1,0:T(8,128)(2,1)S(1)}, u32[]{:S(2)}, u32[]{:S(2)}) async-start(bf16[256,8,128]{2,1,0:T(8,128)(2,1)} %prepare.1), calls=%async_computation | async-start | bytes 1048576 | tf_op jit(solution)/shard_map/all_to_all | solution.py:319
  17.4 8.3 %collective-permute-start = (f32[4,32]{1,0:T(4,128)S(1)}, f32[4,32]{1,0:T(4,128)S(1)}, u32[]{:S(2)}, u32[]{:S(2)}) collective-permute-start(f32[4,32]{1,0:T(4,128)S(1)} %get-tuple-element.65), channel_id=1, source_target_pairs={{0,1},{1,0},{2,3},{3,2},{4,5},{5,4},{6,7},{7,6},{8,9},{9,8},{10,11... | collective-permute-start | bytes 1544 | tf_op jit(solution)/shard_map/ppermute | solution.py:295
  17.6 10.9 %collective-permute-start.1 = (f32[4,32]{1,0:T(4,128)S(1)}, f32[4,32]{1,0:T(4,128)S(1)}, u32[]{:S(2)}, u32[]{:S(2)}) collective-permute-start(f32[4,32]{1,0:T(4,128)S(1)} %get-tuple-element.64), channel_id=1, source_target_pairs={{0,2},{1,3},{2,0},{3,1},{4,6},{5,7},{6,4},{7,5},{8,10},{9,11},{10,... | collective-permute-start | bytes 1544 | tf_op jit(solution)/shard_map/ppermute | solution.py:295
  19.1 9.6 %collective-permute-start.2 = (f32[4,32]{1,0:T(4,128)S(1)}, f32[4,32]{1,0:T(4,128)S(1)}, u32[]{:S(2)}, u32[]{:S(2)}) collective-permute-start(f32[4,32]{1,0:T(4,128)S(1)} %get-tuple-element.63), channel_id=1, source_target_pairs={{0,3},{1,2},{2,1},{3,0},{4,7},{5,6},{6,5},{7,4},{8,11},{9,10},{10,... | collective-permute-start | bytes 1544 | tf_op jit(solution)/shard_map/ppermute | solution.py:295
  19.3 9.4 %collective-permute-start.3 = (f32[4,32]{1,0:T(4,128)S(1)}, f32[4,32]{1,0:T(4,128)S(1)}, u32[]{:S(2)}, u32[]{:S(2)}) collective-permute-start(f32[4,32]{1,0:T(4,128)S(1)} %get-tuple-element.62), channel_id=1, source_target_pairs={{0,4},{1,5},{2,6},{3,7},{4,0},{5,1},{6,2},{7,3},{8,12},{9,13},{10,... | collective-permute-start | bytes 1544 | tf_op jit(solution)/shard_map/ppermute | solution.py:295
  22.3 6.4 %collective-permute-start.4 = (f32[4,32]{1,0:T(4,128)S(1)}, f32[4,32]{1,0:T(4,128)S(1)}, u32[]{:S(2)}, u32[]{:S(2)}) collective-permute-start(f32[4,32]{1,0:T(4,128)S(1)} %get-tuple-element.61), channel_id=1, source_target_pairs={{0,5},{1,4},{2,7},{3,6},{4,1},{5,0},{6,3},{7,2},{8,13},{9,12},{10,... | collective-permute-start | bytes 1544 | tf_op jit(solution)/shard_map/ppermute | solution.py:295
  25.7 4.9 %collective-permute-start.5 = (f32[4,32]{1,0:T(4,128)S(1)}, f32[4,32]{1,0:T(4,128)S(1)}, u32[]{:S(2)}, u32[]{:S(2)}) collective-permute-start(f32[4,32]{1,0:T(4,128)S(1)} %get-tuple-element.60), channel_id=1, source_target_pairs={{0,6},{1,7},{2,4},{3,5},{4,2},{5,3},{6,0},{7,1},{8,14},{9,15},{10,... | collective-permute-start | bytes 1544 | tf_op jit(solution)/shard_map/ppermute | solution.py:295
  28.5 4.2 %collective-permute-start.6 = (f32[4,32]{1,0:T(4,128)S(1)}, f32[4,32]{1,0:T(4,128)S(1)}, u32[]{:S(2)}, u32[]{:S(2)}) collective-permute-start(f32[4,32]{1,0:T(4,128)S(1)} %get-tuple-element.59), channel_id=1, source_target_pairs={{0,7},{1,6},{2,5},{3,4},{4,3},{5,2},{6,1},{7,0},{8,15},{9,14},{10,... | collective-permute-start | bytes 1544 | tf_op jit(solution)/shard_map/ppermute | solution.py:295
  38.7 51.9 %all-to-all-start.1 = ((bf16[32,224,128]{2,1,0:T(8,128)(2,1)}), bf16[32,224,128]{2,1,0:T(8,128)(2,1)S(1)}, u32[]{:S(2)}, u32[]{:S(2)}) async-start(bf16[32,224,128]{2,1,0:T(8,128)(2,1)} %gather.11), calls=%async_computation.1 | async-start | bytes 3670016 | tf_op jit(solution)/shard_map/all_to_all | solution.py:350
  48.3 5.0 %collective-permute-start.7 = (bf16[512,128]{1,0:T(8,128)(2,1)S(1)}, bf16[512,128]{1,0:T(8,128)(2,1)S(1)}, u32[]{:S(2)}, u32[]{:S(2)}) collective-permute-start(bf16[512,128]{1,0:T(8,128)(2,1)S(1)} %get-tuple-element.57), channel_id=1, source_target_pairs={{0,1},{1,0},{2,3},{3,2},{4,5},{5,4},{6,7},{7,6},{8,9},{9,8},{10,11... | collective-permute-start | bytes 393224 | tf_op jit(solution)/shard_map/ppermute | solution.py:295
  48.4 6.3 %collective-permute-start.8 = (bf16[512,128]{1,0:T(8,128)(2,1)S(1)}, bf16[512,128]{1,0:T(8,128)(2,1)S(1)}, u32[]{:S(2)}, u32[]{:S(2)}) collective-permute-start(bf16[512,128]{1,0:T(8,128)(2,1)S(1)} %get-tuple-element.56), channel_id=1, source_target_pairs={{0,2},{1,3},{2,0},{3,1},{4,6},{5,7},{6,4},{7,5},{8,10},{9,11},{10,... | collective-permute-start | bytes 393224 | tf_op jit(solution)/shard_map/ppermute | solution.py:295
  48.4 8.4 %collective-permute-start.9 = (bf16[512,128]{1,0:T(8,128)(2,1)}, bf16[512,128]{1,0:T(8,128)(2,1)S(1)}, u32[]{:S(2)}, u32[]{:S(2)}) collective-permute-start(bf16[512,128]{1,0:T(8,128)(2,1)} %get-tuple-element.55), channel_id=1, source_target_pairs={{0,3},{1,2},{2,1},{3,0},{4,7},{5,6},{6,5},{7,4},{8,11},{9,10},{10,... | collective-permute-start | bytes 393224 | tf_op jit(solution)/shard_map/ppermute | solution.py:295
  50.2 10.1 %collective-permute-start.10 = (bf16[512,128]{1,0:T(8,128)(2,1)S(1)}, bf16[512,128]{1,0:T(8,128)(2,1)S(1)}, u32[]{:S(2)}, u32[]{:S(2)}) collective-permute-start(bf16[512,128]{1,0:T(8,128)(2,1)S(1)} %get-tuple-element.54), channel_id=1, source_target_pairs={{0,4},{1,5},{2,6},{3,7},{4,0},{5,1},{6,2},{7,3},{8,12},{9,13},{10,... | collective-permute-start | bytes 393224 | tf_op jit(solution)/shard_map/ppermute | solution.py:295
  50.5 11.9 %collective-permute-start.11 = (bf16[512,128]{1,0:T(8,128)(2,1)S(1)}, bf16[512,128]{1,0:T(8,128)(2,1)S(1)}, u32[]{:S(2)}, u32[]{:S(2)}) collective-permute-start(bf16[512,128]{1,0:T(8,128)(2,1)S(1)} %get-tuple-element.53), channel_id=1, source_target_pairs={{0,5},{1,4},{2,7},{3,6},{4,1},{5,0},{6,3},{7,2},{8,13},{9,12},{10,... | collective-permute-start | bytes 393224 | tf_op jit(solution)/shard_map/ppermute | solution.py:295
  53.4 12.2 %collective-permute-start.12 = (bf16[512,128]{1,0:T(8,128)(2,1)S(1)}, bf16[512,128]{1,0:T(8,128)(2,1)S(1)}, u32[]{:S(2)}, u32[]{:S(2)}) collective-permute-start(bf16[512,128]{1,0:T(8,128)(2,1)S(1)} %get-tuple-element.52), channel_id=1, source_target_pairs={{0,6},{1,7},{2,4},{3,5},{4,2},{5,3},{6,0},{7,1},{8,14},{9,15},{10,... | collective-permute-start | bytes 393224 | tf_op jit(solution)/shard_map/ppermute | solution.py:295
  54.6 13.6 %collective-permute-start.13 = (bf16[512,128]{1,0:T(8,128)(2,1)S(1)}, bf16[512,128]{1,0:T(8,128)(2,1)S(1)}, u32[]{:S(2)}, u32[]{:S(2)}) collective-permute-start(bf16[512,128]{1,0:T(8,128)(2,1)S(1)} %get-tuple-element.51), channel_id=1, source_target_pairs={{0,7},{1,6},{2,5},{3,4},{4,3},{5,2},{6,1},{7,0},{8,15},{9,14},{10,... | collective-permute-start | bytes 393224 | tf_op jit(solution)/shard_map/ppermute | solution.py:295
  104.4 28.1 %all-to-all-start.2 = ((bf16[32,96,128]{2,1,0:T(8,128)(2,1)}), bf16[32,96,128]{2,1,0:T(8,128)(2,1)S(1)}, u32[]{:S(2)}, u32[]{:S(2)}) async-start(bf16[32,96,128]{2,1,0:T(8,128)(2,1)} %query_parts.1), calls=%async_computation.2 | async-start | bytes 1572864 | tf_op jit(solution)/shard_map/all_to_all | solution.py:391
  133.8 16.6 %all-to-all-start.3 = ((bf16[32,32,128]{2,1,0:T(8,128)(2,1)}), bf16[32,32,128]{2,1,0:T(8,128)(2,1)S(1)}, u32[]{:S(2)}, u32[]{:S(2)}) async-start(bf16[32,32,128]{2,1,0:T(8,128)(2,1)} %pair_sum.1), calls=%async_computation.3 | async-start | bytes 524288 | tf_op jit(solution)/shard_map/all_to_all | solution.py:423
  (1 other events, 1.7 us)

commit v5 on v4

--- a/solution.py
+++ b/solution.py
@@ -145,7 +145,18 @@
 EXP_SCALE = SCALE * math.log2(math.e)
 
 
-def query_kernel(src_ref, x_ref, k_hbm, v_hbm, out_hbm, k_ref, v_ref, out_ref, qx, dx, stats, sems, out_sems):
+def preload_kernel(k_hbm, v_hbm, k_ref, v_ref, sems):
+    at = slice(0, LANES)
+    copies = [
+        pltpu.make_async_copy(src.at[:, at], dst, sems.at[n]) for n, (src, dst) in enumerate(((k_hbm, k_ref), (v_hbm, v_ref)))
+    ]
+    for copy in copies:
+        copy.start()
+    for copy in copies:
+        copy.wait()
+
+
+def query_kernel(src_ref, x_ref, k_near, v_near, k_hbm, v_hbm, out_hbm, k_ref, v_ref, out_ref, qx, dx, stats, sems, out_sems):
     per_group = k_ref.shape[0]
 
     def fetch(head, which):
@@ -157,12 +168,26 @@
         at = pl.ds(head * 8, 8)
         return pltpu.make_async_copy(out_ref.at[at], out_hbm.at[at], out_sems.at[head])
 
-    fetch(0, 0).start()
-    fetch(0, 1).start()
+    fetch(1, 0).start()
+    fetch(1, 1).start()
     load_statistics(src_ref, x_ref, stats)
 
+    def work(head, keys, values):
+        assemble(x_ref, stats, head, qx, dx)
+        keys_ext = extend(keys[...])
+        values_ext = extend(values[...])
+        for slot in range(SLOTS):
+            at = slice(slot * 256, slot * 256 + 256)
+            weights = jnp.exp2(dot(qx[at], keys_ext, NT) * EXP_SCALE)
+            dscores = (weights * dot(dx[at], values_ext, NT)).astype(BF16)
+            part = (dot(dscores, keys[...]) * SCALE).astype(BF16)
+            for e in range(8):
+                out_ref[head * 8 + e, slot * 32 : (slot + 1) * 32, :] = part[e * 32 : (e + 1) * 32]
+        leave(head).start()
+
+    work(0, k_near, v_near)
+
     def body(head, carry):
-        assemble(x_ref, stats, head, qx, dx)
         fetch(head, 0).wait()
         fetch(head, 1).wait()
 
@@ -171,20 +196,10 @@
             fetch(head + 1, 0).start()
             fetch(head + 1, 1).start()
 
-        keys = k_ref[head]
-        keys_ext = extend(keys)
-        values_ext = extend(v_ref[head])
-        for slot in range(SLOTS):
-            at = slice(slot * 256, slot * 256 + 256)
-            weights = jnp.exp2(dot(qx[at], keys_ext, NT) * EXP_SCALE)
-            dscores = (weights * dot(dx[at], values_ext, NT)).astype(BF16)
-            part = (dot(dscores, keys) * SCALE).astype(BF16)
-            for e in range(8):
-                out_ref[head * 8 + e, slot * 32 : (slot + 1) * 32, :] = part[e * 32 : (e + 1) * 32]
-        leave(head).start()
+        work(head, k_ref.at[head], v_ref.at[head])
         return carry
 
-    lax.fori_loop(0, per_group, body, 0)
+    lax.fori_loop(1, per_group, body, 0)
     for head in range(per_group):
         leave(head).wait()
 
@@ -368,17 +383,29 @@
         name="own_set",
     )(me.reshape(1), stats.reshape(per_group, groups, LANES), *window)
 
-    items, own_dq, new_key_grad, new_value_grad = lax.optimization_barrier((items, own_dq, new_key_grad, new_value_grad))
+    ctx_keys, ctx_values = in_hbm(ctx_keys), in_hbm(ctx_values)
+    *near, own_dq, new_key_grad = lax.optimization_barrier((ctx_keys, ctx_values, own_dq, new_key_grad))
+    near = pl.pallas_call(
+        preload_kernel,
+        out_shape=(jax.ShapeDtypeStruct((key_rows, LANES), BF16),) * 2,
+        in_specs=[hbm] * 2,
+        out_specs=(vmem(), vmem()),
+        scratch_shapes=[pltpu.SemaphoreType.DMA((2,))],
+        compiler_params=params(),
+        name="first_head",
+    )(in_hbm(near[0]), in_hbm(near[1]))
+    items, near, own_dq, new_key_grad, new_value_grad = lax.optimization_barrier(
+        (items, near, own_dq, new_key_grad, new_value_grad)
+    )
 
     slot_rows = SLOTS * block_rows
     work = 2 * slot_rows * key_rows * LANES * per_group
     wide = pltpu.VMEM((slot_rows, 2 * LANES), BF16)
     slot_stats = pltpu.VMEM((SLOTS, 32, LANES), F32)
-    ctx_keys, ctx_values = in_hbm(ctx_keys), in_hbm(ctx_values)
     parts = pl.pallas_call(
         query_kernel,
         out_shape=jax.ShapeDtypeStruct((owners, SLOTS * 32, LANES), BF16),
-        in_specs=[smem, vmem(), hbm, hbm],
+        in_specs=[smem, vmem(), vmem(), vmem(), hbm, hbm],
         out_specs=hbm,
         scratch_shapes=[pltpu.VMEM((per_group, key_rows, LANES), BF16)] * 2
         + [pltpu.VMEM((owners, SLOTS * 32, LANES), BF16), wide, wide, slot_stats]
@@ -386,7 +413,7 @@
         compiler_params=params(28),
         cost_estimate=pl.CostEstimate(flops=8 * work, bytes_accessed=6 << 20, transcendentals=0),
         name="query_parts",
-    )(mine, items, ctx_keys, ctx_values)
+    )(mine, items, *near, ctx_keys, ctx_values)
 
     returned = lax.all_to_all(parts, "seq", split_axis=0, concat_axis=0, tiled=True)
 

time: 152 us -> 151 us (level)
  waiting for transfers between devices: 52.8 us -> 50.8 us
  local copies, waits for them, and re-layouts: 4.52 us -> 6.35 us
    all_to_all x1, waiting for transfers between devices: 19.3 us -> 17.2 us  [per_device(): lax.all_to_all(outgoing, 'seq', split_axis=0, concat_axis=0, tiled=True)]
    unnamed x21 -> x25, local copies, waits for them, and re-layouts: 0.17 us -> 2 us
    pallas_call x1, Pallas kernels: 13.8 us -> 12.2 us  [per_device(): pl.pallas_call(query_kernel, out_shape=jax.ShapeDtypeStruct((owners, SLOT...]
where the time goes in v5:
time: 151 us
  waiting for transfers between devices  50.8 us (34%)
  starting transfers between devices  49.7 us (33%)
  Pallas kernels  41.4 us (27%)
  local copies, waits for them, and re-layouts  6.35 us (4%)
    pallas_call x2, Pallas kernels, context_grads(): pl.pallas_call(functools.partial(context_kernel, chunk=256, first=first),...  18.6 us
    all_to_all x1, waiting for transfers between devices, per_device(): lax.all_to_all(outgoing, 'seq', split_axis=0, concat_axis=0, tiled=True)  17.2 us
    ppermute x14, waiting for transfers between devices, swap(): lax.ppermute(part, 'head', [(i, i ^ k) for i in range(groups)])  16.5 us
    ppermute x14, starting transfers between devices, swap(): lax.ppermute(part, 'head', [(i, i ^ k) for i in range(groups)])  15.6 us
    all_to_all x1, starting transfers between devices, per_device(): lax.all_to_all(pieces, ('seq', 'head'), split_axis=0, concat_axis=0, tile...  14.4 us
    pallas_call x1, Pallas kernels, per_device(): pl.pallas_call(query_kernel, out_shape=jax.ShapeDtypeStruct((owners, SLOT...  12.2 us
    all_to_all x1, waiting for transfers between devices, per_device(): lax.all_to_all(parts, 'seq', split_axis=0, concat_axis=0, tiled=True)  8.71 us
    all_to_all x1, starting transfers between devices, per_device(): lax.all_to_all(outgoing, 'seq', split_axis=0, concat_axis=0, tiled=True)  7.61 us
  transfers between devices with their start and end apart: 18, of which 12 were waited for; matrix products, arithmetic and copies ran while one was open for 4% of the time, Pallas kernels for 15%

profile of v5, /device:TPU:32, one launch (start us, length us, event | category | flops | bytes accessed | tf_op | source)
XLA Modules:
  0.0 150.7 jit_solution(17959449895014060180)
XLA Ops:
  0.7 1.9 %prepare.1 = bf16[256,8,128]{2,1,0:T(8,128)(2,1)} custom-call(bf16[32,4096]{1,0:T(8,128)(2,1)} %q_hbm.1, bf16[32,4096]{1,0:T(8,128)(2,1)} %do_ref), custom_call_target="tpu_custom_call" | custom-call | tf_op jit(solution)/shard_map/prepare/pallas_call | solution.py:316
  2.6 14.4 %all-to-all-start = ((bf16[256,8,128]{2,1,0:T(8,128)(2,1)}), bf16[256,8,128]{2,1,0:T(8,128)(2,1)S(1)}, u32[]{:S(2)}, u32[]{:S(2)}) async-start(bf16[256,8,128]{2,1,0:T(8,128)(2,1)} %prepare.1), calls=%async_computation | async-start | bytes 1048576 | tf_op jit(solution)/shard_map/all_to_all | solution.py:334
  19.3 3.0 %collective-permute-start.3 = (f32[4,32]{1,0:T(4,128)S(1)}, f32[4,32]{1,0:T(4,128)S(1)}, u32[]{:S(2)}, u32[]{:S(2)}) collective-permute-start(f32[4,32]{1,0:T(4,128)S(1)} %get-tuple-element.78), channel_id=1, source_target_pairs={{0,4},{1,5},{2,6},{3,7},{4,0},{5,1},{6,2},{7,3},{8,12},{9,13},{10,... | collective-permute-start | bytes 1544 | tf_op jit(solution)/shard_map/ppermute | solution.py:310
  25.7 2.8 %collective-permute-start.5 = (f32[4,32]{1,0:T(4,128)S(1)}, f32[4,32]{1,0:T(4,128)S(1)}, u32[]{:S(2)}, u32[]{:S(2)}) collective-permute-start(f32[4,32]{1,0:T(4,128)S(1)} %get-tuple-element.76), channel_id=1, source_target_pairs={{0,6},{1,7},{2,4},{3,5},{4,2},{5,3},{6,0},{7,1},{8,14},{9,15},{10,... | collective-permute-start | bytes 1544 | tf_op jit(solution)/shard_map/ppermute | solution.py:310
  28.7 1.9 %collective-permute-done.5 = f32[4,32]{1,0:T(4,128)S(1)} collective-permute-done((f32[4,32]{1,0:T(4,128)S(1)}, f32[4,32]{1,0:T(4,128)S(1)}, u32[]{:S(2)}, u32[]{:S(2)}) %collective-permute-start.5) | collective-permute-done | bytes 544 | tf_op jit(solution)/shard_map/ppermute | solution.py:310
  30.6 2.1 %collective-permute-done.6 = f32[4,32]{1,0:T(4,128)S(1)} collective-permute-done((f32[4,32]{1,0:T(4,128)S(1)}, f32[4,32]{1,0:T(4,128)S(1)}, u32[]{:S(2)}, u32[]{:S(2)}) %collective-permute-start.6) | collective-permute-done | bytes 544 | tf_op jit(solution)/shard_map/ppermute | solution.py:310
  33.7 3.1 %all-to-all-done = bf16[256,8,128]{2,1,0:T(8,128)(2,1)S(1)} async-done(((bf16[256,8,128]{2,1,0:T(8,128)(2,1)}), bf16[256,8,128]{2,1,0:T(8,128)(2,1)S(1)}, u32[]{:S(2)}, u32[]{:S(2)}) %all-to-all-start) | async-done | bytes 524320 | tf_op jit(solution)/shard_map/all_to_all | solution.py:334
  38.7 7.6 %all-to-all-start.1 = ((bf16[32,224,128]{2,1,0:T(8,128)(2,1)}), bf16[32,224,128]{2,1,0:T(8,128)(2,1)S(1)}, u32[]{:S(2)}, u32[]{:S(2)}) async-start(bf16[32,224,128]{2,1,0:T(8,128)(2,1)} %gather.11), calls=%async_computation.1 | async-start | bytes 3670016 | tf_op jit(solution)/shard_map/all_to_all | solution.py:365
  46.3 2.0 %dynamic-slice_bitcast_fusion = (bf16[512,128]{1,0:T(8,128)(2,1)S(1)}, bf16[512,128]{1,0:T(8,128)(2,1)S(1)}, bf16[512,128]{1,0:T(8,128)(2,1)S(1)}, bf16[512,128]...) fusion(bf16[8,512,128]{2,1,0:T(8,128)(2,1)} %pad_maximum_fusion, ...), kind=kLoop, calls=%fused_computation.2 | loop fusion | bytes 2097184 | tf_op jit(solution)/shard_map/jit(dynamic_index_in_dim)/squeeze | solution.py:309
  48.4 1.9 %collective-permute-start.9 = (bf16[512,128]{1,0:T(8,128)(2,1)}, bf16[512,128]{1,0:T(8,128)(2,1)S(1)}, u32[]{:S(2)}, u32[]{:S(2)}) collective-permute-start(bf16[512,128]{1,0:T(8,128)(2,1)} %get-tuple-element.71), channel_id=1, source_target_pairs={{0,3},{1,2},{2,1},{3,0},{4,7},{5,6},{6,5},{7,4},{8,11},{9,10},{10,... | collective-permute-start | bytes 393224 | tf_op jit(solution)/shard_map/ppermute | solution.py:310
  50.5 2.8 %collective-permute-start.11 = (bf16[512,128]{1,0:T(8,128)(2,1)S(1)}, bf16[512,128]{1,0:T(8,128)(2,1)S(1)}, u32[]{:S(2)}, u32[]{:S(2)}) collective-permute-start(bf16[512,128]{1,0:T(8,128)(2,1)S(1)} %get-tuple-element.69), channel_id=1, source_target_pairs={{0,5},{1,4},{2,7},{3,6},{4,1},{5,0},{6,3},{7,2},{8,13},{9,12},{10,... | collective-permute-start | bytes 393224 | tf_op jit(solution)/shard_map/ppermute | solution.py:310
  56.7 3.7 %collective-permute-done.10.refs_4_ = bf16[512,128]{1,0:T(8,128)(2,1)S(1)} collective-permute-done((bf16[512,128]{1,0:T(8,128)(2,1)S(1)}, bf16[512,128]{1,0:T(8,128)(2,1)S(1)}, u32[]{:S(2)}, u32[]{:S(2)}) %collective-permute-start.10) | collective-permute-done | bytes 131104 | tf_op jit(solution)/shard_map/ppermute | solution.py:310
  60.4 2.1 %collective-permute-done.11.refs_5_ = bf16[512,128]{1,0:T(8,128)(2,1)S(1)} collective-permute-done((bf16[512,128]{1,0:T(8,128)(2,1)S(1)}, bf16[512,128]{1,0:T(8,128)(2,1)S(1)}, u32[]{:S(2)}, u32[]{:S(2)}) %collective-permute-start.11) | collective-permute-done | bytes 131104 | tf_op jit(solution)/shard_map/ppermute | solution.py:310
  62.4 3.1 %collective-permute-done.12.refs_6_ = bf16[512,128]{1,0:T(8,128)(2,1)S(1)} collective-permute-done((bf16[512,128]{1,0:T(8,128)(2,1)S(1)}, bf16[512,128]{1,0:T(8,128)(2,1)S(1)}, u32[]{:S(2)}, u32[]{:S(2)}) %collective-permute-start.12) | collective-permute-done | bytes 131104 | tf_op jit(solution)/shard_map/ppermute | solution.py:310
  65.6 2.7 %collective-permute-done.13.refs_7_ = bf16[512,128]{1,0:T(8,128)(2,1)S(1)} collective-permute-done((bf16[512,128]{1,0:T(8,128)(2,1)S(1)}, bf16[512,128]{1,0:T(8,128)(2,1)S(1)}, u32[]{:S(2)}, u32[]{:S(2)}) %collective-permute-start.13) | collective-permute-done | bytes 131104 | tf_op jit(solution)/shard_map/ppermute | solution.py:310
  68.3 3.1 %own_set.1 = (f32[256,512]{1,0:T(8,128)S(1)}, bf16[256,512]{1,0:T(8,128)(2,1)}, bf16[256,512]{1,0:T(8,128)(2,1)}) custom-call(s32[1]{0:T(128)} %bitcast.26.me_ref, bf16[4,8,128]{2,1,0:T(8,128)(2,1)S(1)} %bitcast.63, bf16[512,128]{1,0:T(8,128)(2,1)S(1)} %get-tuple-element.74.refs_0_, bf16[512,128]{1,0:T(8,128)(2,1)S(1)} %collective-permute-done.7.refs_1_, ...), custom_call_target="tpu_custom_call" | custom-call | flops 335544320 | bytes 2097152 | tf_op jit(solution)/shard_map/own_set/pallas_call | solution.py:369
  73.4 17.2 %all-to-all-done.1.x_ref = bf16[32,224,128]{2,1,0:T(8,128)(2,1)S(1)} async-done(((bf16[32,224,128]{2,1,0:T(8,128)(2,1)}), bf16[32,224,128]{2,1,0:T(8,128)(2,1)S(1)}, u32[]{:S(2)}, u32[]{:S(2)}) %all-to-all-start.1) | async-done | bytes 1835040 | tf_op jit(solution)/shard_map/all_to_all | solution.py:365
  91.7 12.2 %query_parts.1 = bf16[32,96,128]{2,1,0:T(8,128)(2,1)} custom-call(s32[3]{0:T(128)S(1)} %dynamic_slice.53.src_ref, bf16[32,224,128]{2,1,0:T(8,128)(2,1)S(1)} %all-to-all-done.1.x_ref, bf16[2048,128]{1,0:T(8,128)(2,1)S(1)} %get-tuple-element.50.k_near, bf16[2048,128]{1,0:T(8,128)(2,1)S(1)} %copy-done.3, bf16[2048,512]{1,0:T(8,128)(2,1)} %k_ref.3, ...), custom_call_target="tpu_custom_call" | custom-call | flops 12884901888 | bytes 6291456 | tf_op jit(solution)/shard_map/query_parts/pallas_call | solution.py:405
  103.9 6.5 %all-to-all-start.2 = ((bf16[32,96,128]{2,1,0:T(8,128)(2,1)}), bf16[32,96,128]{2,1,0:T(8,128)(2,1)S(1)}, u32[]{:S(2)}, u32[]{:S(2)}) async-start(bf16[32,96,128]{2,1,0:T(8,128)(2,1)} %query_parts.1), calls=%async_computation.2 | async-start | bytes 1572864 | tf_op jit(solution)/shard_map/all_to_all | solution.py:418
  110.3 12.9 %context_grads.2 = (bf16[2048,512]{1,0:T(8,128)(2,1)}, bf16[2048,512]{1,0:T(8,128)(2,1)}) custom-call(s32[3]{0:T(128)S(1)} %dynamic_slice.53.src_ref, bf16[32,224,128]{2,1,0:T(8,128)(2,1)S(1)} %all-to-all-done.1.x_ref, bf16[2048,512]{1,0:T(8,128)(2,1)} %k_ref.3, bf16[2048,512]{1,0:T(8,128)(2,1)} %v_ref.3), custom_call_target="tpu_custom_call" | custom-call | flops 12079595520 | bytes 10485760 | tf_op jit(solution)/shard_map/context_grads/pallas_call | solution.py:425
  123.2 8.7 %all-to-all-done.2.in_ref = bf16[32,96,128]{2,1,0:T(8,128)(2,1)S(1)} async-done(((bf16[32,96,128]{2,1,0:T(8,128)(2,1)}), bf16[32,96,128]{2,1,0:T(8,128)(2,1)S(1)}, u32[]{:S(2)}, u32[]{:S(2)}) %all-to-all-start.2) | async-done | bytes 786464 | tf_op jit(solution)/shard_map/all_to_all | solution.py:418
  133.3 5.7 %all-to-all-start.3 = ((bf16[32,32,128]{2,1,0:T(8,128)(2,1)}), bf16[32,32,128]{2,1,0:T(8,128)(2,1)S(1)}, u32[]{:S(2)}, u32[]{:S(2)}) async-start(bf16[32,32,128]{2,1,0:T(8,128)(2,1)} %pair_sum.1), calls=%async_computation.3 | async-start | bytes 524288 | tf_op jit(solution)/shard_map/all_to_all | solution.py:450
  139.0 5.7 %context_grads.3 = (bf16[2048,512]{1,0:T(8,128)(2,1)}, bf16[2048,512]{1,0:T(8,128)(2,1)}) custom-call(s32[3]{0:T(128)S(1)} %dynamic_slice.53.src_ref, bf16[32,224,128]{2,1,0:T(8,128)(2,1)S(1)} %all-to-all-done.1.x_ref, bf16[2048,512]{1,0:T(8,128)(2,1)} %k_ref.3, bf16[2048,512]{1,0:T(8,128)(2,1)} %v_ref.3, ...), custom_call_target="tpu_custom_call", output_to_operand_aliasing={{0}: (4, {}), {1}: (5, {})} | custom-call | flops 4026531840 | bytes 10485760 | tf_op jit(solution)/shard_map/context_grads/pallas_call | solution.py:425
  144.7 5.2 %all-to-all-done.3.in_ref = bf16[32,32,128]{2,1,0:T(8,128)(2,1)S(1)} async-done(((bf16[32,32,128]{2,1,0:T(8,128)(2,1)}), bf16[32,32,128]{2,1,0:T(8,128)(2,1)S(1)}, u32[]{:S(2)}, u32[]{:S(2)}) %all-to-all-start.3) | async-done | bytes 262176 | tf_op jit(solution)/shard_map/all_to_all | solution.py:450
  (76 shorter events, 17.4 us)
Async XLA Ops:
  0.6 22.2 %copy-start.4 = (bf16[32,4096]{1,0:T(8,128)(2,1)S(1)}, bf16[32,4096]{1,0:T(8,128)(2,1)}, u32[]{:S(2)}) copy-start(bf16[32,4096]{1,0:T(8,128)(2,1)} %q_hbm.1) | copy-start | bytes 786436
  0.6 16.4 %copy-start = (bf16[32,4096]{1,0:T(8,128)(2,1)S(1)}, bf16[32,4096]{1,0:T(8,128)(2,1)}, u32[]{:S(2)}) copy-start(bf16[32,4096]{1,0:T(8,128)(2,1)} %do_ref) | copy-start | bytes 786436
  0.7 16.4 %copy-start.1 = (bf16[32,4096]{1,0:T(8,128)(2,1)S(1)}, bf16[32,4096]{1,0:T(8,128)(2,1)}, u32[]{:S(2)}) copy-start(bf16[32,4096]{1,0:T(8,128)(2,1)} %o_ref) | copy-start | bytes 786436
  0.7 22.3 %copy-start.8 = (s32[32,2]{0,1:T(2,128)S(1)}, s32[32,2]{0,1:T(2,128)}, u32[]{:S(2)}) copy-start(s32[32,2]{0,1:T(2,128)} %param.17) | copy-start | bytes 772
  0.7 22.7 %copy-start.5 = (bf16[32,4096]{1,0:T(8,128)(2,1)S(1)}, bf16[32,4096]{1,0:T(8,128)(2,1)}, u32[]{:S(2)}) copy-start(bf16[32,4096]{1,0:T(8,128)(2,1)} %param.11) | copy-start | bytes 786436
  2.6 21.1 %copy-start.6 = (bf16[32,4096]{1,0:T(8,128)(2,1)S(1)}, bf16[32,4096]{1,0:T(8,128)(2,1)}, u32[]{:S(2)}) copy-start(bf16[32,4096]{1,0:T(8,128)(2,1)} %param.10) | copy-start | bytes 786436
  2.6 34.2 %all-to-all-start = ((bf16[256,8,128]{2,1,0:T(8,128)(2,1)}), bf16[256,8,128]{2,1,0:T(8,128)(2,1)S(1)}, u32[]{:S(2)}, u32[]{:S(2)}) async-start(bf16[256,8,128]{2,1,0:T(8,128)(2,1)} %prepare.1), calls=%async_computation | async-start | bytes 1048576 | tf_op jit(solution)/shard_map/all_to_all | solution.py:334
  17.4 8.3 %collective-permute-start = (f32[4,32]{1,0:T(4,128)S(1)}, f32[4,32]{1,0:T(4,128)S(1)}, u32[]{:S(2)}, u32[]{:S(2)}) collective-permute-start(f32[4,32]{1,0:T(4,128)S(1)} %get-tuple-element.81), channel_id=1, source_target_pairs={{0,1},{1,0},{2,3},{3,2},{4,5},{5,4},{6,7},{7,6},{8,9},{9,8},{10,11... | collective-permute-start | bytes 1544 | tf_op jit(solution)/shard_map/ppermute | solution.py:310
  17.6 10.9 %collective-permute-start.1 = (f32[4,32]{1,0:T(4,128)S(1)}, f32[4,32]{1,0:T(4,128)S(1)}, u32[]{:S(2)}, u32[]{:S(2)}) collective-permute-start(f32[4,32]{1,0:T(4,128)S(1)} %get-tuple-element.80), channel_id=1, source_target_pairs={{0,2},{1,3},{2,0},{3,1},{4,6},{5,7},{6,4},{7,5},{8,10},{9,11},{10,... | collective-permute-start | bytes 1544 | tf_op jit(solution)/shard_map/ppermute | solution.py:310
  19.1 9.6 %collective-permute-start.2 = (f32[4,32]{1,0:T(4,128)S(1)}, f32[4,32]{1,0:T(4,128)S(1)}, u32[]{:S(2)}, u32[]{:S(2)}) collective-permute-start(f32[4,32]{1,0:T(4,128)S(1)} %get-tuple-element.79), channel_id=1, source_target_pairs={{0,3},{1,2},{2,1},{3,0},{4,7},{5,6},{6,5},{7,4},{8,11},{9,10},{10,... | collective-permute-start | bytes 1544 | tf_op jit(solution)/shard_map/ppermute | solution.py:310
  19.3 9.4 %collective-permute-start.3 = (f32[4,32]{1,0:T(4,128)S(1)}, f32[4,32]{1,0:T(4,128)S(1)}, u32[]{:S(2)}, u32[]{:S(2)}) collective-permute-start(f32[4,32]{1,0:T(4,128)S(1)} %get-tuple-element.78), channel_id=1, source_target_pairs={{0,4},{1,5},{2,6},{3,7},{4,0},{5,1},{6,2},{7,3},{8,12},{9,13},{10,... | collective-permute-start | bytes 1544 | tf_op jit(solution)/shard_map/ppermute | solution.py:310
  22.3 6.4 %collective-permute-start.4 = (f32[4,32]{1,0:T(4,128)S(1)}, f32[4,32]{1,0:T(4,128)S(1)}, u32[]{:S(2)}, u32[]{:S(2)}) collective-permute-start(f32[4,32]{1,0:T(4,128)S(1)} %get-tuple-element.77), channel_id=1, source_target_pairs={{0,5},{1,4},{2,7},{3,6},{4,1},{5,0},{6,3},{7,2},{8,13},{9,12},{10,... | collective-permute-start | bytes 1544 | tf_op jit(solution)/shard_map/ppermute | solution.py:310
  25.7 4.9 %collective-permute-start.5 = (f32[4,32]{1,0:T(4,128)S(1)}, f32[4,32]{1,0:T(4,128)S(1)}, u32[]{:S(2)}, u32[]{:S(2)}) collective-permute-start(f32[4,32]{1,0:T(4,128)S(1)} %get-tuple-element.76), channel_id=1, source_target_pairs={{0,6},{1,7},{2,4},{3,5},{4,2},{5,3},{6,0},{7,1},{8,14},{9,15},{10,... | collective-permute-start | bytes 1544 | tf_op jit(solution)/shard_map/ppermute | solution.py:310
  28.5 4.2 %collective-permute-start.6 = (f32[4,32]{1,0:T(4,128)S(1)}, f32[4,32]{1,0:T(4,128)S(1)}, u32[]{:S(2)}, u32[]{:S(2)}) collective-permute-start(f32[4,32]{1,0:T(4,128)S(1)} %get-tuple-element.75), channel_id=1, source_target_pairs={{0,7},{1,6},{2,5},{3,4},{4,3},{5,2},{6,1},{7,0},{8,15},{9,14},{10,... | collective-permute-start | bytes 1544 | tf_op jit(solution)/shard_map/ppermute | solution.py:310
  38.7 51.9 %all-to-all-start.1 = ((bf16[32,224,128]{2,1,0:T(8,128)(2,1)}), bf16[32,224,128]{2,1,0:T(8,128)(2,1)S(1)}, u32[]{:S(2)}, u32[]{:S(2)}) async-start(bf16[32,224,128]{2,1,0:T(8,128)(2,1)} %gather.11), calls=%async_computation.1 | async-start | bytes 3670016 | tf_op jit(solution)/shard_map/all_to_all | solution.py:365
  48.3 5.0 %collective-permute-start.7 = (bf16[512,128]{1,0:T(8,128)(2,1)S(1)}, bf16[512,128]{1,0:T(8,128)(2,1)S(1)}, u32[]{:S(2)}, u32[]{:S(2)}) collective-permute-start(bf16[512,128]{1,0:T(8,128)(2,1)S(1)} %get-tuple-element.73), channel_id=1, source_target_pairs={{0,1},{1,0},{2,3},{3,2},{4,5},{5,4},{6,7},{7,6},{8,9},{9,8},{10,11... | collective-permute-start | bytes 393224 | tf_op jit(solution)/shard_map/ppermute | solution.py:310
  48.4 6.3 %collective-permute-start.8 = (bf16[512,128]{1,0:T(8,128)(2,1)S(1)}, bf16[512,128]{1,0:T(8,128)(2,1)S(1)}, u32[]{:S(2)}, u32[]{:S(2)}) collective-permute-start(bf16[512,128]{1,0:T(8,128)(2,1)S(1)} %get-tuple-element.72), channel_id=1, source_target_pairs={{0,2},{1,3},{2,0},{3,1},{4,6},{5,7},{6,4},{7,5},{8,10},{9,11},{10,... | collective-permute-start | bytes 393224 | tf_op jit(solution)/shard_map/ppermute | solution.py:310
  48.4 8.4 %collective-permute-start.9 = (bf16[512,128]{1,0:T(8,128)(2,1)}, bf16[512,128]{1,0:T(8,128)(2,1)S(1)}, u32[]{:S(2)}, u32[]{:S(2)}) collective-permute-start(bf16[512,128]{1,0:T(8,128)(2,1)} %get-tuple-element.71), channel_id=1, source_target_pairs={{0,3},{1,2},{2,1},{3,0},{4,7},{5,6},{6,5},{7,4},{8,11},{9,10},{10,... | collective-permute-start | bytes 393224 | tf_op jit(solution)/shard_map/ppermute | solution.py:310
  50.2 10.1 %collective-permute-start.10 = (bf16[512,128]{1,0:T(8,128)(2,1)S(1)}, bf16[512,128]{1,0:T(8,128)(2,1)S(1)}, u32[]{:S(2)}, u32[]{:S(2)}) collective-permute-start(bf16[512,128]{1,0:T(8,128)(2,1)S(1)} %get-tuple-element.70), channel_id=1, source_target_pairs={{0,4},{1,5},{2,6},{3,7},{4,0},{5,1},{6,2},{7,3},{8,12},{9,13},{10,... | collective-permute-start | bytes 393224 | tf_op jit(solution)/shard_map/ppermute | solution.py:310
  50.5 11.9 %collective-permute-start.11 = (bf16[512,128]{1,0:T(8,128)(2,1)S(1)}, bf16[512,128]{1,0:T(8,128)(2,1)S(1)}, u32[]{:S(2)}, u32[]{:S(2)}) collective-permute-start(bf16[512,128]{1,0:T(8,128)(2,1)S(1)} %get-tuple-element.69), channel_id=1, source_target_pairs={{0,5},{1,4},{2,7},{3,6},{4,1},{5,0},{6,3},{7,2},{8,13},{9,12},{10,... | collective-permute-start | bytes 393224 | tf_op jit(solution)/shard_map/ppermute | solution.py:310
  53.4 12.2 %collective-permute-start.12 = (bf16[512,128]{1,0:T(8,128)(2,1)S(1)}, bf16[512,128]{1,0:T(8,128)(2,1)S(1)}, u32[]{:S(2)}, u32[]{:S(2)}) collective-permute-start(bf16[512,128]{1,0:T(8,128)(2,1)S(1)} %get-tuple-element.68), channel_id=1, source_target_pairs={{0,6},{1,7},{2,4},{3,5},{4,2},{5,3},{6,0},{7,1},{8,14},{9,15},{10,... | collective-permute-start | bytes 393224 | tf_op jit(solution)/shard_map/ppermute | solution.py:310
  54.6 13.6 %collective-permute-start.13 = (bf16[512,128]{1,0:T(8,128)(2,1)S(1)}, bf16[512,128]{1,0:T(8,128)(2,1)S(1)}, u32[]{:S(2)}, u32[]{:S(2)}) collective-permute-start(bf16[512,128]{1,0:T(8,128)(2,1)S(1)} %get-tuple-element.67), channel_id=1, source_target_pairs={{0,7},{1,6},{2,5},{3,4},{4,3},{5,2},{6,1},{7,0},{8,15},{9,14},{10,... | collective-permute-start | bytes 393224 | tf_op jit(solution)/shard_map/ppermute | solution.py:310
  103.9 28.1 %all-to-all-start.2 = ((bf16[32,96,128]{2,1,0:T(8,128)(2,1)}), bf16[32,96,128]{2,1,0:T(8,128)(2,1)S(1)}, u32[]{:S(2)}, u32[]{:S(2)}) async-start(bf16[32,96,128]{2,1,0:T(8,128)(2,1)} %query_parts.1), calls=%async_computation.2 | async-start | bytes 1572864 | tf_op jit(solution)/shard_map/all_to_all | solution.py:418
  133.3 16.6 %all-to-all-start.3 = ((bf16[32,32,128]{2,1,0:T(8,128)(2,1)}), bf16[32,32,128]{2,1,0:T(8,128)(2,1)S(1)}, u32[]{:S(2)}, u32[]{:S(2)}) async-start(bf16[32,32,128]{2,1,0:T(8,128)(2,1)} %pair_sum.1), calls=%async_computation.3 | async-start | bytes 524288 | tf_op jit(solution)/shard_map/all_to_all | solution.py:450
  (3 other events, 3.5 us)
